TPU v7x, 32 devices: a whole 2x2x4 slice. The times are simulated.
32 devices in a mesh: seq: 8 (over y, x, core), tp: 4 (over z).
Axes of the slice: x: 2, y: 2, z: 4, core: 2. Of those that a mesh axis runs over, the one named last changes fastest.
Arguments:
- inputs: bfloat16 [4096, 2048], P(('seq', 'tp')), may hold values from -6 to 6
- segment_ids: int32 [4096], P('seq'), may hold values from 0 to 15, as said below
- cotangent: bfloat16 [4096, 2048], P(('seq', 'tp')), may hold values from -6 to 6
- qkv_weight: bfloat16 [3, 2048, 2048], P(None, None, 'tp'), may hold values from -0.125 to 0.125
- qkv_bias: bfloat16 [3, 2048], P(None, 'tp'), may hold values from -3 to 3
- out_weight: bfloat16 [2048, 2048], P('tp'), may hold values from -0.125 to 0.125
- out_bias: bfloat16 [2048], replicated, may hold values from -3 to 3
- up_weight: bfloat16 [2048, 8192], P(None, 'tp'), may hold values from -0.125 to 0.125
- up_bias: bfloat16 [8192], P('tp'), may hold values from -3 to 3
- down_weight: bfloat16 [8192, 2048], P('tp'), may hold values from -0.0625 to 0.0625
- down_bias: bfloat16 [2048], replicated, may hold values from -3 to 3
- input_gain: bfloat16 [2048], replicated, may hold values from 0.25 to 1.75
- input_bias: bfloat16 [2048], replicated, may hold values from -2 to 2
- mixed_gain: bfloat16 [2048], P('tp'), may hold values from 0.25 to 1.75
- mixed_bias: bfloat16 [2048], P('tp'), may hold values from -2 to 2
- middle_gain: bfloat16 [2048], replicated, may hold values from 0.25 to 1.75
- middle_bias: bfloat16 [2048], replicated, may hold values from -2 to 2
- hidden_gain: bfloat16 [8192], P('tp'), may hold values from 0.25 to 1.75
- hidden_bias: bfloat16 [8192], P('tp'), may hold values from -2 to 2
- qkv_average: float32 [3, 2048, 2048], P(None, 'seq', 'tp'), may hold values from -0.125 to 0.125
- out_average: float32 [2048, 2048], P('tp', 'seq'), may hold values from -0.125 to 0.125
- up_average: float32 [2048, 8192], P('seq', 'tp'), may hold values from -0.125 to 0.125
- down_average: float32 [8192, 2048], P('tp', 'seq'), may hold values from -0.0625 to 0.0625
- decay_rate: float32 [1], replicated, may hold values from 0.5 to 0.8
Outputs:
- layer_out: bfloat16 [4096, 2048], P(('seq', 'tp'))
- input_grad: bfloat16 [4096, 2048], P(('seq', 'tp'))
- qkv_grad: float32 [3, 2048, 2048], P(None, 'seq', 'tp')
- qkvbias_grad: float32 [3, 2048], P(None, ('tp', 'seq'))
- out_grad: float32 [2048, 2048], P('tp', 'seq')
- outbias_grad: float32 [2048], P(('seq', 'tp'))
- up_grad: float32 [2048, 8192], P('seq', 'tp')
- upbias_grad: float32 [8192], P(('tp', 'seq'))
- down_grad: float32 [8192, 2048], P('tp', 'seq')
- downbias_grad: float32 [2048], P(('seq', 'tp'))
- inputgain_grad: float32 [2048], P(('seq', 'tp'))
- inputbias_grad: float32 [2048], P(('seq', 'tp'))
- mixedgain_grad: float32 [2048], P(('tp', 'seq'))
- mixedbias_grad: float32 [2048], P(('tp', 'seq'))
- middlegain_grad: float32 [2048], P(('seq', 'tp'))
- middlebias_grad: float32 [2048], P(('seq', 'tp'))
- hiddengain_grad: float32 [8192], P(('tp', 'seq'))
- hiddenbias_grad: float32 [8192], P(('tp', 'seq'))
- qkv_new: float32 [3, 2048, 2048], P(None, 'seq', 'tp')
- out_new: float32 [2048, 2048], P('tp', 'seq')
- up_new: float32 [2048, 8192], P('seq', 'tp')
- down_new: float32 [8192, 2048], P('tp', 'seq')
Inputs may be any that keep to these rules, and one draw needn't show every extreme that they name: `segment_ids`: the tokens form one packed row of 4096 tokens holding exactly 16 documents; segment ids start at 0 and rise by one at each new document; one document begins within the first 512 tokens and ends within the last 512 tokens.
All inputs are finite; a program needn't handle non-finite values.
Results may differ from a plain program's by a relative error of at most 0.014.
Values may be sent and summed in bfloat16 or wider, within the bound.
No kernel may reach another device: no remote copies, remote signals or barrier semaphores. Data moves between devices by JAX's collectives and lax.ppermute only.
A program may use at most 256 MiB of HBM per device.

v0:
```python
import math

import jax
import jax.numpy as jnp
from jax import lax
from jax.sharding import PartitionSpec as P

FF = 8192
COUNT = 16
HD = 64


SCALE = 0.125
EPSILON = 1e-05
NEGATIVE = -1e30
LARGEST = 1 << 30


def xpos_tables(positions, head_size):
    half = head_size // 2
    index = jnp.arange(half, dtype=jnp.float32)
    frequency = jnp.exp(index * (-2.0 * math.log(10000.0) / head_size))
    zeta = (index * (2.0 / head_size) + 0.4) / 1.4
    places = positions.astype(jnp.float32)[:, None]
    angle = places * frequency[None, :]
    growth = jnp.exp(places * (jnp.log(zeta)[None, :] / 512.0))
    return (jnp.cos(angle), jnp.sin(angle), growth)


def turn(values, cosine, sine, scale, head_size):
    rows = values.shape[0]
    shaped = values.reshape(rows, -1, head_size)
    half = head_size // 2
    first = shaped[:, :, :half]
    second = shaped[:, :, half:]
    cosine = cosine[:, None, :]
    sine = sine[:, None, :]
    scale = scale[:, None, :]
    turned = jnp.concatenate(
        [(first * cosine - second * sine) * scale, (second * cosine + first * sine) * scale], axis=2
    )
    return turned.reshape(values.shape)


def norm_rows(values, gain, shift):
    center = jnp.mean(values, axis=-1, keepdims=True)
    spread = jnp.mean(values * values, axis=-1, keepdims=True) - center * center
    return (values - center) * lax.rsqrt(spread + EPSILON) * gain + shift


def exact_gelu(values):
    return jax.nn.gelu(values, approximate=False)


def gather_rows(values):
    return lax.all_gather(values, "tp", axis=0, tiled=True)


def tp_totals(first, second):
    return lax.psum((first, second), "tp")


def reduce_rows(term, rows):
    return lax.psum_scatter(
        term(jnp.int32(0), rows * lax.axis_size("tp")), "tp", scatter_dimension=0, tiled=True
    )


def split_norm(values, gain, shift, width):
    total, squares = tp_totals(jnp.sum(values, axis=1), jnp.sum(values * values, axis=1))
    center = (total / width)[:, None]
    spread = (squares / width)[:, None] - center * center
    factor = lax.rsqrt(spread + EPSILON)
    unit = (values - center) * factor
    return (unit * gain + shift, unit, factor)


def split_norm_back(grad, unit, factor, gain, width):
    scaled = grad * gain
    total, cross = tp_totals(jnp.sum(scaled, axis=1), jnp.sum(scaled * unit, axis=1))
    result = (scaled - (total / width)[:, None] - unit * (cross / width)[:, None]) * factor
    return (result, jnp.sum(grad * unit, axis=0), jnp.sum(grad, axis=0))


def shards(
    inputs,
    segment_ids,
    cotangent,
    qkv_weight,
    qkv_bias,
    out_weight,
    out_bias,
    up_weight,
    up_bias,
    down_weight,
    down_bias,
    input_gain,
    input_bias,
    mixed_gain,
    mixed_bias,
    middle_gain,
    middle_bias,
    hidden_gain,
    hidden_bias,
    qkv_average,
    out_average,
    up_average,
    down_average,
    decay_rate,
):
    wide = jnp.float32
    narrow = jnp.bfloat16
    seq_count = lax.axis_size("seq")
    seq_rank = lax.axis_index("seq")
    local_rows = segment_ids.shape[0]
    share_rows = inputs.shape[0]
    model_width = inputs.shape[1]
    local_width = qkv_weight.shape[2]
    heads_here = local_width // HD
    row_index = seq_rank * local_rows + jnp.arange(local_rows, dtype=jnp.int32)
    documents = jnp.arange(COUNT, dtype=jnp.int32)
    member = segment_ids[:, None] == documents[None, :]
    first_here = jnp.min(jnp.where(member, row_index[:, None], LARGEST), axis=0)
    first_all = lax.pmin(first_here, "seq")
    earlier = first_all[None, :] <= row_index[:, None]
    row_start = jnp.max(jnp.where(earlier, first_all[None, :], 0), axis=1)
    cosine, sine, growth = xpos_tables(row_index - row_start, HD)
    shrink = 1.0 / growth
    inputs_wide = inputs.astype(wide)
    input_normed, input_back = jax.vjp(
        norm_rows, inputs_wide, input_gain.astype(wide), input_bias.astype(wide)
    )
    attn_in = gather_rows(input_normed.astype(narrow))
    projected = jnp.einsum(
        "rd,cdf->crf", attn_in, qkv_weight, preferred_element_type=wide
    ) + qkv_bias[:, None, :].astype(wide)
    query_turned = turn(projected[0], cosine, sine, growth, HD).astype(narrow)
    key_turned = turn(projected[1], cosine, sine, shrink, HD).astype(narrow)
    value_low = projected[2].astype(narrow)
    all_keys, all_values = (
        lax.all_gather(key_turned, "seq", axis=0, tiled=True),
        lax.all_gather(value_low, "seq", axis=0, tiled=True),
    )
    key_count = all_keys.shape[0]
    block = min(512, key_count)
    block_count = key_count // block
    key_blocks = all_keys.reshape(block_count, block, heads_here, HD)
    value_blocks = all_values.reshape(block_count, block, heads_here, HD)
    block_starts = jnp.arange(block_count, dtype=jnp.int32) * block
    query_heads = query_turned.reshape(local_rows, heads_here, HD)
    lowest = row_start[0]
    highest = row_index[local_rows - 1]
    offsets = jnp.arange(block, dtype=jnp.int32)

    def needed(begin):
        return (begin + block > lowest) & (begin <= highest)

    def block_scores(queries, keys_block, query_rows, query_starts, key_rows):
        raw = jnp.einsum("qhd,khd->hqk", queries, keys_block, preferred_element_type=wide) * SCALE
        allowed = (key_rows[None, :] <= query_rows[:, None]) & (
            key_rows[None, :] >= query_starts[:, None]
        )
        return (raw, allowed[None])

    def probs_of(raw, allowed, logs):
        return jnp.where(allowed, jnp.exp(raw - logs[:, :, None]), 0.0)

    def measure(carry, item):
        keys_block, begin = item

        def measure_work(state):
            top, total = state
            raw, allowed = block_scores(
                query_heads, keys_block, row_index, row_start, begin + offsets
            )
            masked = jnp.where(allowed, raw, NEGATIVE)
            fresh_top = jnp.maximum(top, jnp.max(masked, axis=2))
            kept = jnp.where(allowed, jnp.exp(masked - fresh_top[:, :, None]), 0.0)
            return (fresh_top, total * jnp.exp(top - fresh_top) + jnp.sum(kept, axis=2))

        return (lax.cond(needed(begin), measure_work, lambda state: state, carry), None)

    start_state = (
        jnp.full((heads_here, local_rows), NEGATIVE, wide),
        jnp.zeros((heads_here, local_rows), wide),
    )
    (top, total), _ = lax.scan(measure, start_state, (key_blocks, block_starts))
    log_total = top + jnp.log(total)

    def attend(carry, item):
        keys_block, values_block, begin = item

        def attend_work(accum):
            raw, allowed = block_scores(
                query_heads, keys_block, row_index, row_start, begin + offsets
            )
            probs = probs_of(raw, allowed, log_total).astype(narrow)
            return accum + jnp.einsum(
                "hqk,khd->qhd", probs, values_block, preferred_element_type=wide
            )

        return (lax.cond(needed(begin), attend_work, lambda accum: accum, carry), None)

    mixed, _ = lax.scan(
        attend,
        jnp.zeros((local_rows, heads_here, HD), wide),
        (key_blocks, value_blocks, block_starts),
    )
    mixed = mixed.reshape(local_rows, local_width)
    mixed_norm, mixed_unit, mixed_factor = split_norm(mixed, mixed_gain, mixed_bias, model_width)
    mixed_low = mixed_norm.astype(narrow)

    def out_term(begin, count):
        return jnp.dot(mixed_low, out_weight, preferred_element_type=wide)

    middle = inputs_wide + reduce_rows(out_term, share_rows) + out_bias.astype(wide)
    middle_normed, middle_back = jax.vjp(
        norm_rows, middle, middle_gain.astype(wide), middle_bias.astype(wide)
    )
    ffn_in = gather_rows(middle_normed.astype(narrow))
    up_value = jnp.dot(ffn_in, up_weight, preferred_element_type=wide) + up_bias.astype(wide)
    activated, gelu_back = jax.vjp(exact_gelu, up_value)
    hidden_norm, hidden_unit, hidden_factor = split_norm(activated, hidden_gain, hidden_bias, FF)
    hidden_low = hidden_norm.astype(narrow)

    def down_term(begin, count):
        return jnp.dot(hidden_low, down_weight, preferred_element_type=wide)

    layer_out = (middle + reduce_rows(down_term, share_rows) + down_bias.astype(wide)).astype(
        narrow
    )
    grad_rows = gather_rows(cotangent)
    down_grad = jnp.einsum("rf,rd->fd", hidden_low, grad_rows, preferred_element_type=wide)
    downbias_part = jnp.sum(cotangent, axis=0, dtype=wide)
    grad_hidden = jnp.einsum("rd,fd->rf", grad_rows, down_weight, preferred_element_type=wide)
    grad_active, hiddengain_part, hiddenbias_part = split_norm_back(
        grad_hidden, hidden_unit, hidden_factor, hidden_gain, FF
    )
    grad_up = gelu_back(grad_active)[0].astype(narrow)
    up_grad = jnp.einsum("rd,rf->df", ffn_in, grad_up, preferred_element_type=wide)
    upbias_part = jnp.sum(grad_up, axis=0, dtype=wide)
    ffn_sums = (
        lax.psum_scatter(
            up_grad.astype(jnp.bfloat16), "seq", scatter_dimension=0, tiled=True
        ).astype(jnp.float32),
        lax.psum_scatter(
            upbias_part.astype(jnp.bfloat16), "seq", scatter_dimension=0, tiled=True
        ).astype(jnp.float32),
        lax.psum_scatter(
            down_grad.astype(jnp.bfloat16), "seq", scatter_dimension=1, tiled=True
        ).astype(jnp.float32),
        lax.psum_scatter(
            hiddengain_part.astype(jnp.bfloat16), "seq", scatter_dimension=0, tiled=True
        ).astype(jnp.float32),
        lax.psum_scatter(
            hiddenbias_part.astype(jnp.bfloat16), "seq", scatter_dimension=0, tiled=True
        ).astype(jnp.float32),
    )

    def ffn_back_term(begin, count):
        return jnp.einsum("rf,df->rd", grad_up, up_weight, preferred_element_type=wide)

    grad_ffn_in = reduce_rows(ffn_back_term, share_rows)
    grad_middle_norm, middlegain_part, middlebias_part = middle_back(grad_ffn_in)
    grad_middle = cotangent.astype(wide) + grad_middle_norm
    grad_middle_low = grad_middle.astype(narrow)
    grad_mixed_rows = gather_rows(grad_middle_low)
    out_grad = jnp.einsum("rf,rd->fd", mixed_low, grad_mixed_rows, preferred_element_type=wide)
    outbias_part = jnp.sum(grad_middle_low, axis=0, dtype=wide)
    grad_mixed_norm = jnp.einsum(
        "rd,fd->rf", grad_mixed_rows, out_weight, preferred_element_type=wide
    )
    grad_mixed_wide, mixedgain_part, mixedbias_part = split_norm_back(
        grad_mixed_norm, mixed_unit, mixed_factor, mixed_gain, model_width
    )
    grad_mixed = grad_mixed_wide.astype(narrow).reshape(local_rows, heads_here, HD)

    def weigh(carry, item):
        keys_block, values_block, begin = item

        def weigh_work(accum):
            raw, allowed = block_scores(
                query_heads, keys_block, row_index, row_start, begin + offsets
            )
            probs = probs_of(raw, allowed, log_total)
            grad_probs = jnp.einsum(
                "qhd,khd->hqk", grad_mixed, values_block, preferred_element_type=wide
            )
            return accum + jnp.sum(probs * grad_probs, axis=2)

        return (lax.cond(needed(begin), weigh_work, lambda accum: accum, carry), None)

    delta, _ = lax.scan(
        weigh, jnp.zeros((heads_here, local_rows), wide), (key_blocks, value_blocks, block_starts)
    )

    def spread(carry, item):
        keys_block, values_block, begin = item

        def spread_work(accum):
            raw, allowed = block_scores(
                query_heads, keys_block, row_index, row_start, begin + offsets
            )
            probs = probs_of(raw, allowed, log_total)
            grad_probs = jnp.einsum(
                "qhd,khd->hqk", grad_mixed, values_block, preferred_element_type=wide
            )
            grad_scores = (probs * (grad_probs - delta[:, :, None])).astype(narrow)
            accum = (
                accum
                + jnp.einsum("hqk,khd->qhd", grad_scores, keys_block, preferred_element_type=wide)
                * SCALE
            )
            key_part = (
                jnp.einsum("hqk,qhd->khd", grad_scores, query_heads, preferred_element_type=wide)
                * SCALE
            )
            value_part = jnp.einsum(
                "hqk,qhd->khd", probs.astype(narrow), grad_mixed, preferred_element_type=wide
            )
            return (
                accum,
                jnp.concatenate(
                    [key_part.reshape(block, local_width), value_part.reshape(block, local_width)],
                    axis=1,
                ),
            )

        def skip(accum):
            return (accum, jnp.zeros((block, 2 * local_width), wide))

        return lax.cond(needed(begin), spread_work, skip, carry)

    grad_query_turned, pieces = lax.scan(
        spread,
        jnp.zeros((local_rows, heads_here, HD), wide),
        (key_blocks, value_blocks, block_starts),
    )
    pieces = pieces.reshape(key_count, 2 * local_width)
    key_value_grads = lax.psum_scatter(
        pieces.astype(jnp.bfloat16), "seq", scatter_dimension=0, tiled=True
    ).astype(jnp.float32)
    grad_key_turned = key_value_grads[:, :local_width]
    grad_value = key_value_grads[:, local_width:]
    grad_query = turn(
        grad_query_turned.reshape(local_rows, local_width), cosine, -sine, growth, HD
    ).astype(narrow)
    grad_key = turn(grad_key_turned, cosine, -sine, shrink, HD).astype(narrow)
    grad_value_low = grad_value.astype(narrow)
    stacked = jnp.stack([grad_query, grad_key, grad_value_low])
    qkv_grad = jnp.einsum("rd,crf->cdf", attn_in, stacked, preferred_element_type=wide)
    qkvbias_part = jnp.sum(stacked, axis=1, dtype=wide)

    def attn_back_term(begin, count):
        return jnp.einsum("crf,cdf->rd", stacked, qkv_weight, preferred_element_type=wide)

    grad_attn_in = reduce_rows(attn_back_term, share_rows)
    grad_input_norm, inputgain_part, inputbias_part = input_back(grad_attn_in)
    input_grad = (grad_middle + grad_input_norm).astype(narrow)
    norm_parts = jnp.stack(
        [
            inputgain_part,
            inputbias_part,
            middlegain_part,
            middlebias_part,
            outbias_part,
            downbias_part,
        ]
    )
    norm_sums = lax.psum_scatter(norm_parts, ("seq", "tp"), scatter_dimension=1, tiled=True)
    attn_sums = (
        lax.psum_scatter(qkv_grad, "seq", scatter_dimension=1, tiled=True),
        lax.psum_scatter(qkvbias_part, "seq", scatter_dimension=1, tiled=True),
        lax.psum_scatter(out_grad, "seq", scatter_dimension=1, tiled=True),
        lax.psum_scatter(mixedgain_part, "seq", scatter_dimension=0, tiled=True),
        lax.psum_scatter(mixedbias_part, "seq", scatter_dimension=0, tiled=True),
    )
    rate = decay_rate[0]
    seq_part = model_width // seq_count
    offset = seq_rank * seq_part

    def average(old, weight, axis):
        piece = lax.dynamic_slice_in_dim(weight, offset, seq_part, axis).astype(wide)
        return rate * old + (1.0 - rate) * piece

    qkv_new = average(qkv_average, qkv_weight, 1)
    out_new = average(out_average, out_weight, 1)
    up_new = average(up_average, up_weight, 0)
    down_new = average(down_average, down_weight, 1)
    return (
        layer_out,
        input_grad,
        attn_sums[0],
        attn_sums[1],
        attn_sums[2],
        norm_sums[4],
        ffn_sums[0],
        ffn_sums[1],
        ffn_sums[2],
        norm_sums[5],
        norm_sums[0],
        norm_sums[1],
        attn_sums[3],
        attn_sums[4],
        norm_sums[2],
        norm_sums[3],
        ffn_sums[3],
        ffn_sums[4],
        qkv_new,
        out_new,
        up_new,
        down_new,
    )


def solution(mesh):
    in_specs = (
        P(("seq", "tp"), None),
        P("seq"),
        P(("seq", "tp"), None),
        P(None, None, "tp"),
        P(None, "tp"),
        P("tp", None),
        P(),
        P(None, "tp"),
        P("tp"),
        P("tp", None),
        P(),
        P(),
        P(),
        P("tp"),
        P("tp"),
        P(),
        P(),
        P("tp"),
        P("tp"),
        P(None, "seq", "tp"),
        P("tp", "seq"),
        P("seq", "tp"),
        P("tp", "seq"),
        P(),
    )
    out_specs = (
        P(("seq", "tp"), None),
        P(("seq", "tp"), None),
        P(None, "seq", "tp"),
        P(None, ("tp", "seq")),
        P("tp", "seq"),
        P(("seq", "tp")),
        P("seq", "tp"),
        P(("tp", "seq")),
        P("tp", "seq"),
        P(("seq", "tp")),
        P(("seq", "tp")),
        P(("seq", "tp")),
        P(("tp", "seq")),
        P(("tp", "seq")),
        P(("seq", "tp")),
        P(("seq", "tp")),
        P(("tp", "seq")),
        P(("tp", "seq")),
        P(None, "seq", "tp"),
        P("tp", "seq"),
        P("seq", "tp"),
        P("tp", "seq"),
    )
    return jax.shard_map(shards, mesh=mesh, in_specs=in_specs, out_specs=out_specs, check_vma=False)
```

profile of v0, /device:TPU:0, one launch (start us, length us, event | category | flops | bytes accessed | tf_op | source)
XLA Modules:
  0.0 1573.0 jit_solution(267580059441248647)
XLA Ops:
  24.8 36.7 %all-gather.8.cloned.1.call-done = bf16[512,2048]{1,0:T(8,128)(2,1)} async-done(((bf16[128,2048]{1,0:T(8,128)(2,1)}), bf16[512,2048]{1,0:T(8,128)(2,1)}) %all-gather.8.cloned.1.call-update) | async-done | bytes 2097168 | tf_op jit(solution)/shard_map/all_gather | solution.py:56
  73.0 32.9 %all-gather.10.cloned.1.call-done = bf16[4096,512]{0,1:T(8,128)(2,1)} async-done(((bf16[512,512]{0,1:T(8,128)(2,1)}), bf16[4096,512]{0,1:T(8,128)(2,1)}) %all-gather.10.cloned.1.call-update) | async-done | bytes 4194320 | tf_op jit(solution)/shard_map/all_gather | solution.py:141
  113.8 31.5 %while.57 = (s32[]{:T(128)}, f32[8,512]{1,0:T(8,128)S(1)}, f32[8,512]{1,0:T(8,128)S(1)}, s32[8]{0:T(128)S(1)}, s32[]{:T(128)}, /*index=5*/s32[]{:T(128)}, s32[51...) while((s32[]{:T(128)}, f32[8,512]{1,0:T(8,128)S(1)}, ...), condition=%wide.region_10.11_spmd.clone, body=%wide.region_5.10_spmd.clone.sunk | while | flops 286008320 | bytes 18842408 | solution.py:187
  153.8 30.5 %while.58 = (s32[]{:T(128)}, f32[512,8,64]{0,2,1:T(8,128)S(1)}, s32[8]{0:T(128)S(1)}, s32[]{:T(128)}, s32[]{:T(128)}, /*index=5*/s32[512]{0:T(512)S(1)}, bf16[8,...) while((s32[]{:T(128)}, f32[512,8,64]{0,2,1:T(8,128)S(1)}, ...), condition=%wide.region_14.15_spmd.clone, body=%wide.region_11.14_spmd.clone.sunk | while | flops 546309120 | bytes 4228375 | solution.py:204
  184.5 11.7 all-reduce.9
  201.6 143.4 %reduce-scatter.16.cloned.1.call-done = f32[128,2048]{1,0:T(8,128)} async-done(((f32[512,2048]{1,0:T(8,128)}), f32[128,2048]{1,0:T(8,128)}) %reduce-scatter.16.cloned.1.call-update) | async-done | bytes 1048592 | tf_op jit(solution)/shard_map/reduce_scatter | solution.py:64
  348.2 45.9 %all-gather.12.cloned.1.call-done = bf16[512,2048]{1,0:T(8,128)(2,1)} async-done(((bf16[128,2048]{1,0:T(8,128)(2,1)}), bf16[512,2048]{1,0:T(8,128)(2,1)}) %all-gather.12.cloned.1.call-update) | async-done | bytes 2097168 | tf_op jit(solution)/shard_map/all_gather | solution.py:56
  394.2 19.4 %fusion.100 = (f32[512]{0:T(512)S(1)}, f32[512]{0:T(512)S(1)}, f32[512,2048]{1,0:T(8,128)}, f32[512,2048]{1,0:T(8,128)}, f32[512,2048]{1,0:T(8,128)}) fusion(f32[2048]{0:T(1024)S(1)} %convert_element_type.209, bf16[512,2048]{1,0:T(8,128)(2,1)} %all-gather.12.cloned.1.call-done, bf16[2048,2048]{1,0:T(8,128)(2,1)} %param.47), kind=kOutput, calls=%fused_computation.205 | convolution fusion | flops 4366269440 | bytes 23080960 | tf_op jit(solution)/shard_map/dot_general | solution.py:221
  413.6 9.9 all-reduce.8
  423.5 17.1 %all-gather.14.cloned.1.call-done = bf16[512,2048]{1,0:T(8,128)(2,1)} async-done(((bf16[128,2048]{1,0:T(8,128)(2,1)}), bf16[512,2048]{1,0:T(8,128)(2,1)}) %all-gather.14.cloned.1.call-update) | async-done | bytes 2097168 | tf_op jit(solution)/shard_map/all_gather | solution.py:56
  440.6 12.7 multiply_reduce_fusion
  453.3 9.8 all-reduce.7
  483.6 11.8 fusion.99
  496.1 62.3 %reduce-scatter.20.cloned.1.call-done = f32[128,2048]{1,0:T(8,128)} async-done(((f32[512,2048]{1,0:T(8,128)}), f32[128,2048]{1,0:T(8,128)}) %reduce-scatter.20.cloned.1.call-update) | async-done | bytes 1048592 | tf_op jit(solution)/shard_map/reduce_scatter | solution.py:64
  560.7 77.2 %reduce-scatter.18.cloned.1.call-done = f32[128,2048]{1,0:T(8,128)} async-done(((f32[512,2048]{1,0:T(8,128)}), f32[128,2048]{1,0:T(8,128)}) %reduce-scatter.18.cloned.1.call-update) | async-done | bytes 1048592 | tf_op jit(solution)/shard_map/reduce_scatter | solution.py:64
  642.2 46.5 %all-gather.16.cloned.1.call-done = bf16[512,2048]{1,0:T(8,128)(2,1)} async-done(((bf16[128,2048]{1,0:T(8,128)(2,1)}), bf16[512,2048]{1,0:T(8,128)(2,1)}) %all-gather.16.cloned.1.call-update) | async-done | bytes 2097168 | tf_op jit(solution)/shard_map/all_gather | solution.py:56
  693.1 9.6 all-reduce.6
  703.8 33.0 %while.59 = (s32[]{:T(128)}, f32[8,512]{1,0:T(8,128)S(1)}, s32[8]{0:T(128)S(1)}, s32[]{:T(128)}, s32[]{:T(128)}, /*index=5*/s32[512]{0:T(512)S(1)}, bf16[8,512,8...) while((s32[]{:T(128)}, f32[8,512]{1,0:T(8,128)S(1)}, ...), condition=%wide.region_42.43_spmd.clone, body=%wide.region_38.42_spmd.clone.sunk | while | flops 548144128 | bytes 21595460 | solution.py:293
  736.9 47.3 %while.60 = (s32[]{:T(128)}, f32[512,8,64]{0,2,1:T(8,128)S(1)}, bf16[8,512,1024]{1,2,0:T(8,128)(2,1)}, s32[8]{0:T(128)S(1)}, s32[]{:T(128)}, /*index=5*/s32[]{:T...) while((s32[]{:T(128)}, f32[512,8,64]{0,2,1:T(8,128)S(1)}, ...), condition=%wide.region_46.47_spmd.clone, body=%wide.region_43.46_spmd.clone.sunk | while | flops 1367081984 | bytes 51710304 | solution.py:334
  740.1 12.5 conditional.15
  784.2 11.4 copy.110
  795.7 204.8 %reduce-scatter.22.cloned.1.call-done = bf16[512,1024]{1,0:T(8,128)(2,1)} async-done(((bf16[4096,1024]{1,0:T(8,128)(2,1)}), bf16[512,1024]{1,0:T(8,128)(2,1)}) %reduce-scatter.22.cloned.1.call-update) | async-done | bytes 1048592 | tf_op jit(solution)/shard_map/reduce_scatter | solution.py:340
  1015.0 10.8 convolution_convert_fusion
  1025.9 10.1 convolution_convert_fusion.1
  1037.2 54.6 %reduce-scatter.24.cloned.1.call-done = f32[128,2048]{1,0:T(8,128)} async-done(((f32[512,2048]{1,0:T(8,128)}), f32[128,2048]{1,0:T(8,128)}) %reduce-scatter.24.cloned.1.call-update) | async-done | bytes 1048592 | tf_op jit(solution)/shard_map/reduce_scatter | solution.py:64
  1124.0 24.3 %all-reduce.10 = (bf16[2048]{0:T(1024)(128)(2,1)S(1)}, bf16[2048]{0:T(1024)(128)(2,1)S(1)}, bf16[2048]{0:T(1024)(128)(2,1)S(1)}) all-reduce(bf16[2048]{0:T(1024)(128)(2,1)S(1)} %copy-done.28, bf16[2048]{0:T(1024)(128)(2,1)S(1)} %copy-done.42, bf16[2048]{0:T(1024)(128)(2,1)S(1)} %copy-done.43), channel_id=13, replica_groups=mesh['seq'=8,'tp'=4] {'seq'}, use_global_device_ids=true, to_apply=%region_64.65.clone | all-reduce | flops 6144 | bytes 24576
  1150.3 12.1 all-reduce.5
  1170.7 72.0 %reduce-scatter.30.cloned.1.call-done = bf16[256,2048]{1,0:T(8,128)(2,1)} async-done(((bf16[2048,2048]{1,0:T(8,128)(2,1)}), bf16[256,2048]{1,0:T(8,128)(2,1)}) %reduce-scatter.30.cloned.1.call-update) | async-done | bytes 1048592 | tf_op jit(solution)/shard_map/reduce_scatter | solution.py:243
  1245.5 34.6 %reduce-scatter.34.cloned.1.call-done = f32[64,3]{1,0:T(8,128)} async-done(((f32[512,3]{1,0:T(8,128)}), f32[64,3]{1,0:T(8,128)}) %reduce-scatter.34.cloned.1.call-update) | async-done | bytes 784
  1282.7 134.8 %reduce-scatter.36.cloned.1.call-done = f32[64,6]{1,0:T(8,128)} async-done(((f32[2048,6]{1,0:T(8,128)}), f32[64,6]{1,0:T(8,128)}) %reduce-scatter.36.cloned.1.call-update) | async-done | bytes 1552
  1422.1 88.4 %reduce-scatter.26.cloned.1.call-done = f32[3,256,512]{1,2,0:T(8,128)} async-done(((f32[3,2048,512]{1,2,0:T(8,128)}), f32[3,256,512]{1,2,0:T(8,128)}) %reduce-scatter.26.cloned.1.call-update) | async-done | bytes 1572880 | tf_op jit(solution)/shard_map/reduce_scatter | solution.py:372
  1513.5 52.5 %reduce-scatter.28.cloned.1.call-done = f32[512,256]{1,0:T(8,128)} async-done(((f32[512,2048]{1,0:T(8,128)}), f32[512,256]{1,0:T(8,128)}) %reduce-scatter.28.cloned.1.call-update) | async-done | bytes 524304 | tf_op jit(solution)/shard_map/reduce_scatter | solution.py:374
  (370 shorter events, 231.9 us)
Async XLA Ops:
  7.2 54.3 %all-gather.8.cloned.1.call-start = ((), (), s32[]{:S(2)}) async-start(), calls=%async_computation.11 | async-start | bytes 2621440 | tf_op jit(solution)/shard_map/all_gather | solution.py:56
  9.2 58.5 %copy-start.22 = (f32[2048]{0:T(1024)}, f32[2048]{0:T(1024)S(1)}, u32[]{:S(2)}) copy-start(f32[2048]{0:T(1024)S(1)} %convert_element_type.195) | copy-start | bytes 24580
  12.7 93.2 %all-gather.10.cloned.1.call-start = ((), (), s32[]{:S(2)}) async-start(), calls=%async_computation.12 | async-start | bytes 4718592 | tf_op jit(solution)/shard_map/all_gather | solution.py:141
  69.6 76.2 %all-gather.18.cloned.1.call-start = ((), (), s32[]{:S(2)}) async-start(), calls=%async_computation.25 | async-start | bytes 4718592 | tf_op jit(solution)/shard_map/all_gather | solution.py:142
  71.8 273.2 %reduce-scatter.16.cloned.1.call-start = ((), (), s32[]{:S(2)}) async-start(), calls=%async_computation.13 | async-start | bytes 5242880 | tf_op jit(solution)/shard_map/reduce_scatter | solution.py:64
  196.4 148.5 %copy-start = (bf16[128,2048]{1,0:T(8,128)(2,1)S(1)}, bf16[128,2048]{1,0:T(8,128)(2,1)}, u32[]{:S(2)}) copy-start(bf16[128,2048]{1,0:T(8,128)(2,1)} %param.40) | copy-start | bytes 1572868
  201.5 146.7 %copy-start.38 = (bf16[2048]{0:T(1024)(128)(2,1)S(1)}, bf16[2048]{0:T(1024)(128)(2,1)}, u32[]{:S(2)}) copy-start(bf16[2048]{0:T(1024)(128)(2,1)} %param.48) | copy-start | bytes 12292
  201.5 146.8 %copy-start.39 = (bf16[2048]{0:T(1024)(128)(2,1)S(1)}, bf16[2048]{0:T(1024)(128)(2,1)}, u32[]{:S(2)}) copy-start(bf16[2048]{0:T(1024)(128)(2,1)} %param.57) | copy-start | bytes 12292
  201.5 192.7 %all-gather.12.cloned.1.call-start = ((), (), s32[]{:S(2)}) async-start(), calls=%async_computation.14 | async-start | bytes 2621440 | tf_op jit(solution)/shard_map/all_gather | solution.py:56
  347.6 93.0 %all-gather.14.cloned.1.call-start = ((), (), s32[]{:S(2)}) async-start(), calls=%async_computation.16 | async-start | bytes 2621440 | tf_op jit(solution)/shard_map/all_gather | solution.py:56
  348.2 210.2 %reduce-scatter.20.cloned.1.call-start = ((), (), s32[]{:S(2)}) async-start(), calls=%async_computation.17 | async-start | bytes 5242880 | tf_op jit(solution)/shard_map/reduce_scatter | solution.py:64
  482.9 155.0 %reduce-scatter.18.cloned.1.call-start = ((), (), s32[]{:S(2)}) async-start(), calls=%async_computation.15 | async-start | bytes 5242880 | tf_op jit(solution)/shard_map/reduce_scatter | solution.py:64
  495.4 142.6 %copy-start.7 = (bf16[128,2048]{1,0:T(8,128)(2,1)S(1)}, bf16[128,2048]{1,0:T(8,128)(2,1)}, u32[]{:S(2)}) copy-start(bf16[128,2048]{1,0:T(8,128)(2,1)} %param.42) | copy-start | bytes 1572868
  495.4 193.3 %all-gather.16.cloned.1.call-start = ((), (), s32[]{:S(2)}) async-start(), calls=%async_computation.18 | async-start | bytes 2621440 | tf_op jit(solution)/shard_map/all_gather | solution.py:56
  642.1 358.4 %reduce-scatter.22.cloned.1.call-start = ((), (), s32[]{:S(2)}) async-start(), calls=%async_computation.19 | async-start | bytes 9437184 | tf_op jit(solution)/shard_map/reduce_scatter | solution.py:340
  795.6 208.8 %copy-start.13 = (f32[512,32]{0,1:T(8,128)S(1)}, f32[512,32]{0,1:T(8,128)}, u32[]{:S(2)}) copy-start(f32[512,32]{0,1:T(8,128)} %copy-done.12) | copy-start | bytes 196612
  795.6 208.8 %copy-start.15 = (f32[512,32]{0,1:T(8,128)S(1)}, f32[512,32]{0,1:T(8,128)}, u32[]{:S(2)}) copy-start(f32[512,32]{0,1:T(8,128)} %copy-done.14) | copy-start | bytes 196612
  795.6 208.8 %copy-start.17 = (f32[512,32]{0,1:T(8,128)S(1)}, f32[512,32]{0,1:T(8,128)}, u32[]{:S(2)}) copy-start(f32[512,32]{0,1:T(8,128)} %copy-done.16) | copy-start | bytes 196612
  795.6 208.8 %copy-start.21 = (f32[512,32]{0,1:T(8,128)S(1)}, f32[512,32]{0,1:T(8,128)}, u32[]{:S(2)}) copy-start(f32[512,32]{0,1:T(8,128)} %get-tuple-element.1196) | copy-start | bytes 196612
  795.7 296.2 %reduce-scatter.24.cloned.1.call-start = ((), (), s32[]{:S(2)}) async-start(), calls=%async_computation.20 | async-start | bytes 5242880 | tf_op jit(solution)/shard_map/reduce_scatter | solution.py:64
  1014.9 153.1 %reduce-scatter.32.cloned.1.call-start = ((), (), s32[]{:S(2)}) async-start(), calls=%async_computation.24 | async-start | bytes 9437184 | tf_op jit(solution)/shard_map/reduce_scatter | solution.py:249
  1025.8 216.9 %reduce-scatter.30.cloned.1.call-start = ((), (), s32[]{:S(2)}) async-start(), calls=%async_computation.23 | async-start | bytes 9437184 | tf_op jit(solution)/shard_map/reduce_scatter | solution.py:243
  1035.9 57.7 %copy-start.24 = (f32[2048]{0:T(1024)S(1)}, f32[2048]{0:T(1024)}, u32[]{:S(2)}) copy-start(f32[2048]{0:T(1024)} %get-tuple-element.1023) | copy-start | bytes 24580
  1036.0 57.7 %copy-start.25 = (f32[2048]{0:T(1024)S(1)}, f32[2048]{0:T(1024)}, u32[]{:S(2)}) copy-start(f32[2048]{0:T(1024)} %get-tuple-element.1031) | copy-start | bytes 24580
  1036.0 244.1 %reduce-scatter.34.cloned.1.call-start = ((), (), s32[]{:S(2)}) async-start(), calls=%async_computation.26 | async-start | bytes 294912
  1037.2 380.3 %reduce-scatter.36.cloned.1.call-start = ((), (), s32[]{:S(2)}) async-start(), calls=%async_computation.27 | async-start | bytes 1081344
  1095.1 415.4 %reduce-scatter.26.cloned.1.call-start = ((), (), s32[]{:S(2)}) async-start(), calls=%async_computation.21 | async-start | bytes 14155776 | tf_op jit(solution)/shard_map/reduce_scatter | solution.py:372
  1104.1 461.9 %reduce-scatter.28.cloned.1.call-start = ((), (), s32[]{:S(2)}) async-start(), calls=%async_computation.22 | async-start | bytes 4718592 | tf_op jit(solution)/shard_map/reduce_scatter | solution.py:374
  1124.0 157.5 %copy-start.46 = (f32[128]{0:T(128)S(1)}, f32[128]{0:T(128)}, u32[]{:S(2)}) copy-start(f32[128]{0:T(128)} %get-tuple-element.1161) | copy-start | bytes 1540
  1124.0 157.5 %copy-start.34 = (f32[128]{0:T(128)S(1)}, f32[128]{0:T(128)}, u32[]{:S(2)}) copy-start(f32[128]{0:T(128)} %copy-done.33) | copy-start | bytes 1540
  1124.0 157.6 %copy-start.4 = (f32[128,2048]{1,0:T(8,128)S(1)}, f32[128,2048]{1,0:T(8,128)}, u32[]{:S(2)}) copy-start(f32[128,2048]{1,0:T(8,128)} %get-tuple-element.1150) | copy-start | bytes 3145732
  1124.0 157.6 %copy-start.5 = (f32[128,2048]{1,0:T(8,128)S(1)}, f32[128,2048]{1,0:T(8,128)}, u32[]{:S(2)}) copy-start(f32[128,2048]{1,0:T(8,128)} %reduce-scatter.24.cloned.1.call-done) | copy-start | bytes 3145732
  (35 other events, 683.5 us)
Sparse Core Ops, SparseCore 0:
  12.8 48.6 all-gather.7
  69.7 36.1 all-gather.9
  108.4 37.4 all-gather.17
  201.6 143.3 reduce-scatter.15
  347.7 46.4 all-gather.11
  395.7 44.8 all-gather.13
  483.1 75.2 reduce-scatter.19
  560.7 77.2 reduce-scatter.17
  642.2 46.4 all-gather.15
  795.7 204.6 reduce-scatter.21
  1015.0 76.7 reduce-scatter.23
  1095.5 72.4 reduce-scatter.31
  1171.5 71.2 reduce-scatter.29
  1246.5 33.5 reduce-scatter.33
  1282.2 135.2 reduce-scatter.35
  1421.3 89.1 reduce-scatter.25
  1514.7 51.2 reduce-scatter.27
where the time goes:
time: 1580 us; the launch traced here: 1570 us
  waiting for transfers between devices  1110 us (70%)
  matrix products  134 us (8%)
  blocking collectives  86.9 us (6%)
  loops' own time  84.6 us (5%)
  local copies, waits for them, and re-layouts  78.6 us (5%)
  other arithmetic  60.9 us (4%)
  between operations  17.7 us (1%)
    reduce_scatter x4, waiting for transfers between devices, reduce_rows(): lax.psum_scatter(term(jnp.int32(0), rows * lax.axis_size('tp')), 'tp', sc...  337 us
    reduce_scatter x1, waiting for transfers between devices, shards(): lax.psum_scatter(pieces.astype(jnp.bfloat16), 'seq', scatter_dimension=0,...  205 us
    unnamed x19, waiting for transfers between devices  170 us
    all_gather x4, waiting for transfers between devices, gather_rows(): return lax.all_gather(values, 'tp', axis=0, tiled=True)  146 us
    reduce_scatter x1, waiting for transfers between devices, shards(): lax.psum_scatter(qkv_grad, 'seq', scatter_dimension=1, tiled=True)  88.4 us
    reduce_scatter x1, waiting for transfers between devices, shards(): lax.psum_scatter(up_grad.astype(jnp.bfloat16), 'seq', scatter_dimension=0...  72 us
    reduce_scatter x1, waiting for transfers between devices, shards(): lax.psum_scatter(out_grad, 'seq', scatter_dimension=1, tiled=True)  52.5 us
    psum x4, blocking collectives, tp_totals(): return lax.psum((first, second), 'tp')  41 us
  transfers between devices with their start and end apart: 17, of which 17 were waited for; matrix products, arithmetic and copies ran while one was open for 8% of the time, Pallas kernels for 0%

commit v1 on v0

v1 whole, which is shorter than its diff:
```python
import functools
import math

import jax
import jax.numpy as jnp
from jax import lax
from jax.experimental import pallas as pl
from jax.experimental.pallas import tpu as pltpu
from jax.sharding import PartitionSpec as P

FF = 8192
COUNT = 16
HD = 64

SCALE = 0.125
LOG2E = 1.4426950408889634
EPSILON = 1e-05
OUTSIDE = -2e30
LOWEST = -1e30
LARGEST = 1 << 30
WIDE = jnp.float32
NARROW = jnp.bfloat16
MIB = 1 << 20


def xpos_tables(positions, head_size):
    half = head_size // 2
    index = jnp.arange(half, dtype=jnp.float32)
    frequency = jnp.exp(index * (-2.0 * math.log(10000.0) / head_size))
    zeta = (index * (2.0 / head_size) + 0.4) / 1.4
    places = positions.astype(jnp.float32)[:, None]
    angle = places * frequency[None, :]
    growth = jnp.exp(places * (jnp.log(zeta)[None, :] / 512.0))
    return (jnp.cos(angle), jnp.sin(angle), growth)


def norm_rows(values, gain, shift):
    center = jnp.mean(values, axis=-1, keepdims=True)
    spread = jnp.mean(values * values, axis=-1, keepdims=True) - center * center
    return (values - center) * lax.rsqrt(spread + EPSILON) * gain + shift


def exact_gelu(values):
    return jax.nn.gelu(values, approximate=False)


def gather_rows(values):
    return lax.all_gather(values, "tp", axis=0, tiled=True)


def scatter_rows(values):
    return lax.psum_scatter(values.astype(NARROW), "tp", scatter_dimension=0, tiled=True).astype(WIDE)


def hop(values, axis, mask, count):
    return lax.ppermute(values, axis, [(i, i ^ mask) for i in range(count)])


def tp_total(values):
    count = lax.axis_size("tp")
    if count & (count - 1):
        return lax.psum(values, "tp")
    total = values
    for mask in range(1, count):
        total = total + hop(values, "tp", mask, count)
    return total


def after(value, *others):
    return lax.optimization_barrier((value,) + others)[0]


def halving(values, bits, count):
    axes = sorted(bits, reverse=True)
    for bit in bits:
        axis = axes.index(bit)
        keep = lax.index_in_dim(values, 0, axis, keepdims=False)
        send = lax.index_in_dim(values, 1, axis, keepdims=False)
        got = hop(send, "seq", 1 << bit, count)
        values = keep.astype(WIDE) + got.astype(WIDE)
        axes.remove(bit)
        if axes:
            values = values.astype(NARROW)
    return values


def vector_scatter(values, rank, count):
    bit = count // 2
    while bit:
        pair = values.reshape(2, bit, -1)
        mine = (rank & bit) // bit
        send = lax.dynamic_index_in_dim(pair, 1 - mine, 0, keepdims=False)
        keep = lax.dynamic_index_in_dim(pair, mine, 0, keepdims=False)
        values = keep + hop(send, "seq", bit, count)
        bit //= 2
    return values.reshape(-1)


def tp_scatter(values):
    count = lax.axis_size("tp")
    rank = lax.axis_index("tp")
    if count & (count - 1):
        return lax.psum_scatter(values, "tp", scatter_dimension=0)
    total = lax.dynamic_index_in_dim(values, rank, 0, keepdims=False)
    for mask in range(1, count):
        part = lax.dynamic_index_in_dim(values, rank ^ mask, 0, keepdims=False)
        total = total + hop(part, "tp", mask, count)
    return total


def sent_kernel(place, left, right, out, *, tall):
    if tall:
        out[0] = lax.dot_general(
            left[...], right[...], (((0,), (0,)), ((), ())), preferred_element_type=WIDE
        ).astype(NARROW)
    else:
        turned = right[...].T
        for c in range(left.shape[0]):
            out[0, c] = jnp.dot(turned, left[c], preferred_element_type=WIDE).astype(NARROW)


def kept_kernel(place, left, right, got, first, second, *, tall):
    if tall:
        total = lax.dot_general(
            left[...], right[...], (((0,), (0,)), ((), ())), preferred_element_type=WIDE
        ) + got[0].astype(WIDE)
        cut = total.shape[0] // 2
        first[0] = total[:cut].astype(NARROW)
        second[0] = total[cut:].astype(NARROW)
    else:
        turned = right[...].T
        cut = turned.shape[0] // 2
        for c in range(left.shape[0]):
            total = jnp.dot(turned, left[c], preferred_element_type=WIDE) + got[0, c].astype(WIDE)
            first[0, c] = total[:cut].astype(NARROW)
            second[0, c] = total[cut:].astype(NARROW)


def gradient_blocks(seat, left, right, count, tall, got=None):
    rows = right.shape[0]
    part = right.shape[1] // count
    slots = count // 2
    if tall:
        block = (left.shape[1], part)
        half = (left.shape[1] // 2, part)
        left_spec = pl.BlockSpec(left.shape, lambda k, seat: (0, 0))
    else:
        block = (left.shape[0], part, left.shape[2])
        half = (left.shape[0], part // 2, left.shape[2])
        left_spec = pl.BlockSpec(left.shape, lambda k, seat: (0, 0, 0))
    zeros = (0,) * len(block)
    if part % 128:
        order = 2 * (jnp.arange(slots, dtype=jnp.int32) ^ seat[0]) + seat[1]
        right = right.reshape(rows, count, part)[:, order].transpose(1, 0, 2)
        right_spec = pl.BlockSpec((None, rows, part), lambda k, seat: (k, 0, 0))
    else:
        right_spec = pl.BlockSpec((rows, part), lambda k, seat: (0, 2 * (k ^ seat[0]) + seat[1]))
    block_spec = pl.BlockSpec((1,) + block, lambda k, seat: (k,) + zeros)
    half_spec = pl.BlockSpec((1,) + half, lambda k, seat: (k,) + zeros)
    whole = jax.ShapeDtypeStruct((slots,) + block, NARROW)
    piece = jax.ShapeDtypeStruct((slots,) + half, NARROW)
    flops = left.size * part * slots * 2
    moved = 2 * left.size + right.size + 2 * left.size // rows * part * slots
    return pl.pallas_call(
        functools.partial(sent_kernel if got is None else kept_kernel, tall=tall),
        grid_spec=pltpu.PrefetchScalarGridSpec(
            num_scalar_prefetch=1,
            grid=(slots,),
            in_specs=[left_spec, right_spec] + ([] if got is None else [block_spec]),
            out_specs=block_spec if got is None else (half_spec, half_spec),
        ),
        out_shape=whole if got is None else (piece, piece),
        compiler_params=params(32),
        cost_estimate=pl.CostEstimate(flops=flops, bytes_accessed=moved, transcendentals=0),
    )(seat, left, right, *([] if got is None else [got]))


def seq_gradient(left, right, rank, count, tall):
    own = rank >> 1
    side = rank & 1
    sent = gradient_blocks(jnp.stack([own, 1 - side]), left, right, count, tall)
    got = hop(sent, "seq", 1, count)
    pieces = gradient_blocks(jnp.stack([own, side]), left, right, count, tall, got)
    return pieces


def finish_gradient(pieces, count, axis):
    levels = count.bit_length() - 2
    bits = list(range(1, levels + 1))
    first, second = (p.reshape((2,) * levels + p.shape[1:]) for p in pieces)
    return jnp.concatenate(
        [halving(first, bits, count), halving(second, bits[::-1], count)], axis=axis
    )


def whole_spec():
    return pl.BlockSpec(memory_space=pltpu.VMEM)


def scalar_spec():
    return pl.BlockSpec(memory_space=pltpu.SMEM)


def params(mib):
    return pltpu.CompilerParams(vmem_limit_bytes=mib * MIB)


def turn_packed(values, straight, crossed):
    lane = lax.broadcasted_iota(jnp.int32, values.shape, 1)
    ahead = pltpu.roll(values, 2 * HD - HD // 2, 1)
    behind = pltpu.roll(values, HD // 2, 1)
    partner = jnp.where((lane & (HD // 2)) == 0, ahead, behind)
    return values * straight + partner * crossed


def pack_kernel(place, rows, weight, bias, straight, crossed, *rest):
    outs, held = rest[:-1], rest[-1]
    count = len(outs)
    half = rows.shape[0] // 2
    total = rows.shape[0]
    for pair in range(count // 2):
        cols = slice(pair * 2 * HD, (pair + 1) * 2 * HD)
        query, key, value = (
            jnp.dot(rows[...], weight[c, :, cols], preferred_element_type=WIDE)
            + bias[c : c + 1, cols]
            for c in range(3)
        )
        for side in range(2):
            part = slice(side * HD, (side + 1) * HD)
            both = jnp.concatenate([query[:, part], key[:, part]], axis=1)
            held[2 * pair + side, :total, :] = turn_packed(
                both, straight[...], crossed[...]
            ).astype(NARROW)
            one = value[:, part]
            held[2 * pair + side, total:, :] = jnp.concatenate(
                [one[:half], one[half:]], axis=1
            ).astype(NARROW)
    me = place[0]
    for slot in range(count):
        outs[slot][...] = held[me ^ slot]


def pack_heads(place, rows, weight, bias, straight, crossed, count):
    total = rows.shape[0]
    shape = jax.ShapeDtypeStruct((total + total // 2, 2 * HD), NARROW)
    return pl.pallas_call(
        pack_kernel,
        out_shape=(shape,) * count,
        in_specs=[scalar_spec()] + [whole_spec()] * 5,
        out_specs=(whole_spec(),) * count,
        scratch_shapes=[pltpu.VMEM((count,) + shape.shape, NARROW)],
        compiler_params=params(48),
        cost_estimate=pl.CostEstimate(
            flops=2 * total * weight.size, bytes_accessed=weight.size * 2 + 8 * MIB, transcendentals=0
        ),
    )(place, rows, weight, bias, straight, crossed)


def split_chunk(chunk):
    block = chunk.shape[0] * 2 // 3
    both = chunk[:block, :]
    packed = chunk[block:, :]
    value = jnp.concatenate([packed[:, :HD], packed[:, HD:]], axis=0)
    return both[:, :HD], both[:, HD:], value


def allowed_mask(begin, q_begin, starts, shape):
    keys = begin + lax.broadcasted_iota(jnp.int32, shape, 0)
    queries = q_begin + lax.broadcasted_iota(jnp.int32, shape, 1)
    return (keys >= starts) & (keys <= queries)


def key_ranges(info, index, first_block, block):
    here = first_block + index
    low = info[2 + 2 * index] // block
    clear = jnp.minimum((info[3 + 2 * index] + block - 1) // block, here)
    return low, clear, here


def forward_kernel(info, starts, *refs, groups, spread):
    count = groups
    chunks = refs[:count]
    at = count + (1 if spread else 0)
    outs = refs[at : at + count]
    mixed, logs, keys, values, queries = refs[at + count :]
    me = info[0]
    first_block = info[1]
    block = starts.shape[2]
    for slot in range(count):
        query, key, value = split_chunk(chunks[slot][...])
        queries[me ^ slot] = query.T
        if not spread:
            keys[me ^ slot] = key
            values[me ^ slot] = value.T
    if spread:

        @pl.loop(0, keys.shape[0])
        def _(kb):
            _, key, value = split_chunk(refs[count][kb])
            keys[kb] = key
            values[kb] = value.T

    @pl.loop(0, count)
    def _(index):
        low, clear, here = key_ranges(info, index, first_block, block)
        query = queries[index]
        begins = starts[index]

        def step(kb, carry, masked):
            top, total, accum = carry
            raw = jnp.dot(keys[kb], query, preferred_element_type=WIDE)
            if masked:
                raw = jnp.where(
                    allowed_mask(kb * block, here * block, begins, raw.shape), raw, OUTSIDE
                )
            fresh = jnp.maximum(top, jnp.max(raw, axis=0, keepdims=True) * (SCALE * LOG2E))
            kept = jnp.exp2(raw * (SCALE * LOG2E) - fresh)
            fade = jnp.exp2(top - fresh)
            total = total * fade + jnp.sum(kept, axis=0, keepdims=True)
            accum = accum * fade + jnp.dot(
                values[kb], kept.astype(NARROW), preferred_element_type=WIDE
            )
            return fresh, total, accum

        carry = (
            jnp.full((1, block), LOWEST, WIDE),
            jnp.zeros((1, block), WIDE),
            jnp.zeros((HD, block), WIDE),
        )
        carry = lax.fori_loop(low, clear, functools.partial(step, masked=True), carry)
        carry = lax.fori_loop(clear, here, functools.partial(step, masked=False), carry)
        top, total, accum = step(here, carry, True)
        mixed[index] = accum / total
        logs[index] = top + jnp.log2(total)

    for slot in range(count):
        outs[slot][...] = mixed[me ^ slot].astype(NARROW)


def attend_forward(info, starts, chunks, everyone):
    count = len(chunks)
    block = starts.shape[2]
    spread = everyone is not None
    blocks = everyone.shape[0] if spread else count
    pairs = count * block * blocks * block // 2
    extra = [everyone] if spread else []
    return pl.pallas_call(
        functools.partial(forward_kernel, groups=count, spread=spread),
        out_shape=(jax.ShapeDtypeStruct((HD, block), NARROW),) * count
        + (
            jax.ShapeDtypeStruct((count, HD, block), WIDE),
            jax.ShapeDtypeStruct((count, 1, block), WIDE),
        ),
        in_specs=[scalar_spec()] + [whole_spec()] * (1 + count + len(extra)),
        out_specs=(whole_spec(),) * (count + 2),
        scratch_shapes=[
            pltpu.VMEM((blocks, block, HD), NARROW),
            pltpu.VMEM((blocks, HD, block), NARROW),
            pltpu.VMEM((count, HD, block), NARROW),
        ],
        compiler_params=params(48),
        cost_estimate=pl.CostEstimate(
            flops=16 * HD * pairs, bytes_accessed=4 * MIB, transcendentals=pairs
        ),
    )(info, starts, *chunks, *extra)


def backward_kernel(info, starts, logs, mixed, *refs, groups, spread):
    count = groups
    chunks = refs[:count]
    grads = refs[count : 2 * count]
    at = 2 * count
    if spread:
        everyone = refs[at]
        at += 1
    outs = refs[at : at + (1 if spread else count)]
    at += len(outs)
    keys, keys_up, values, queries, queries_up, downs, downs_up, key_sum, value_sum, query_sum = refs[at:]
    me = info[0]
    first_block = info[1]
    block = starts.shape[2]
    blocks = keys.shape[0]
    for slot in range(count):
        query, key, value = split_chunk(chunks[slot][...])
        place = me ^ slot
        queries[place] = query
        queries_up[place] = query.T
        down = grads[slot][...]
        downs_up[place] = down
        downs[place] = down.T
        if not spread:
            keys[place] = key
            keys_up[place] = key.T
            values[place] = value
    if spread:

        @pl.loop(0, blocks)
        def _(kb):
            _, key, value = split_chunk(everyone[kb])
            keys[kb] = key
            keys_up[kb] = key.T
            values[kb] = value

    key_sum[...] = jnp.zeros_like(key_sum)
    value_sum[...] = jnp.zeros_like(value_sum)

    @pl.loop(0, count)
    def _(index):
        low, clear, here = key_ranges(info, index, first_block, block)
        query_up = queries_up[index]
        down_up = downs_up[index]
        begins = starts[index]
        log = logs[index]
        delta = jnp.sum(down_up.astype(WIDE) * mixed[index], axis=0, keepdims=True)

        def step(kb, accum, masked):
            raw = jnp.dot(keys[kb], query_up, preferred_element_type=WIDE)
            probs = jnp.exp2(raw * (SCALE * LOG2E) - log)
            if masked:
                probs = jnp.where(
                    allowed_mask(kb * block, here * block, begins, raw.shape), probs, 0.0
                )
            grad_probs = jnp.dot(values[kb], down_up, preferred_element_type=WIDE)
            grad_scores = (probs * (grad_probs - delta)).astype(NARROW)
            value_sum[kb] += jnp.dot(
                probs.astype(NARROW), downs[index], preferred_element_type=WIDE
            )
            key_sum[kb] += jnp.dot(grad_scores, queries[index], preferred_element_type=WIDE)
            return accum + jnp.dot(keys_up[kb], grad_scores, preferred_element_type=WIDE)

        accum = jnp.zeros((HD, block), WIDE)
        accum = lax.fori_loop(low, clear, functools.partial(step, masked=True), accum)
        accum = lax.fori_loop(clear, here, functools.partial(step, masked=False), accum)
        query_sum[index] = step(here, accum, True)

    half = block // 2

    def packed(kb, query):
        both = jnp.concatenate([query, key_sum[kb]], axis=1) * SCALE
        one = value_sum[kb]
        return both.astype(NARROW), jnp.concatenate([one[:half], one[half:]], axis=1).astype(NARROW)

    if spread:

        @pl.loop(0, blocks)
        def _(kb):
            inside = (kb >= first_block) & (kb < first_block + count)
            query = query_sum[jnp.clip(kb - first_block, 0, count - 1)]
            both, value = packed(kb, jnp.where(inside, query, 0.0).T)
            outs[0][kb, :block, :] = both
            outs[0][kb, block:, :] = value

    else:
        for slot in range(count):
            place = me ^ slot
            both, value = packed(place, query_sum[place].T)
            outs[slot][:block, :] = both
            outs[slot][block:, :] = value


def attend_backward(info, starts, logs, mixed, chunks, grads, everyone):
    count = len(chunks)
    block = starts.shape[2]
    spread = everyone is not None
    blocks = everyone.shape[0] if spread else count
    pairs = count * block * blocks * block // 2
    extra = [everyone] if spread else []
    rows = block + block // 2
    if spread:
        shapes = (jax.ShapeDtypeStruct((blocks, rows, 2 * HD), NARROW),)
    else:
        shapes = (jax.ShapeDtypeStruct((rows, 2 * HD), NARROW),) * count
    tall = (block, HD)
    flat = (HD, block)
    return pl.pallas_call(
        functools.partial(backward_kernel, groups=count, spread=spread),
        out_shape=shapes,
        in_specs=[scalar_spec()] + [whole_spec()] * (3 + 2 * count + len(extra)),
        out_specs=(whole_spec(),) * len(shapes),
        scratch_shapes=[
            pltpu.VMEM((blocks,) + tall, NARROW),
            pltpu.VMEM((blocks,) + flat, NARROW),
            pltpu.VMEM((blocks,) + tall, NARROW),
            pltpu.VMEM((count,) + tall, NARROW),
            pltpu.VMEM((count,) + flat, NARROW),
            pltpu.VMEM((count,) + tall, NARROW),
            pltpu.VMEM((count,) + flat, NARROW),
            pltpu.VMEM((blocks,) + tall, WIDE),
            pltpu.VMEM((blocks,) + tall, WIDE),
            pltpu.VMEM((count,) + flat, WIDE),
        ],
        compiler_params=params(56),
        cost_estimate=pl.CostEstimate(
            flops=40 * HD * pairs, bytes_accessed=6 * MIB, transcendentals=pairs
        ),
    )(info, starts, logs, mixed, *chunks, *grads, *extra)


def join_kernel(place, *refs):
    count = len(refs) - 3
    chunks, out, sums, held = refs[:count], refs[count], refs[count + 1], refs[count + 2]
    me = place[0]
    total = 0.0
    squares = 0.0
    for slot in range(count):
        held[me ^ slot] = chunks[slot][...]
        wide = chunks[slot][...].astype(WIDE)
        total = total + jnp.sum(wide, axis=0, keepdims=True)
        squares = squares + jnp.sum(wide * wide, axis=0, keepdims=True)
    sums[0:1, :] = total
    sums[1:2, :] = squares
    for pair in range(count // 2):
        both = jnp.concatenate([held[2 * pair], held[2 * pair + 1]], axis=0)
        out[:, pair * 2 * HD : (pair + 1) * 2 * HD] = both.T


def join_heads(place, chunks):
    count = len(chunks)
    block = chunks[0].shape[1]
    return pl.pallas_call(
        join_kernel,
        out_shape=(
            jax.ShapeDtypeStruct((block, count * HD), NARROW),
            jax.ShapeDtypeStruct((2, block), WIDE),
        ),
        in_specs=[scalar_spec()] + [whole_spec()] * count,
        out_specs=(whole_spec(),) * 2,
        scratch_shapes=[pltpu.VMEM((count, HD, block), NARROW)],
        compiler_params=params(16),
        cost_estimate=pl.CostEstimate(flops=MIB, bytes_accessed=MIB, transcendentals=0),
    )(place, *chunks)


def cut_kernel(place, rows, *refs):
    outs, held = refs[:-1], refs[-1]
    me = place[0]
    count = len(outs)
    for pair in range(count // 2):
        both = rows[:, pair * 2 * HD : (pair + 1) * 2 * HD].T
        held[2 * pair] = both[:HD]
        held[2 * pair + 1] = both[HD:]
    for slot in range(count):
        outs[slot][...] = held[me ^ slot]


def cut_heads(place, rows, count):
    block = rows.shape[0]
    return pl.pallas_call(
        cut_kernel,
        out_shape=(jax.ShapeDtypeStruct((HD, block), NARROW),) * count,
        in_specs=[scalar_spec(), whole_spec()],
        out_specs=(whole_spec(),) * count,
        scratch_shapes=[pltpu.VMEM((count, HD, block), NARROW)],
        compiler_params=params(16),
        cost_estimate=pl.CostEstimate(flops=MIB, bytes_accessed=MIB, transcendentals=0),
    )(place, rows)


def unpack_kernel(place, straight, crossed, *refs):
    count = len(refs) - 3
    chunks, out, sums, held = refs[:count], refs[count], refs[count + 1], refs[count + 2]
    me = place[0]
    block = straight.shape[0]
    for slot in range(count):
        both = turn_packed(chunks[slot][:block, :].astype(WIDE), straight[...], -crossed[...])
        held[me ^ slot, :block, :] = both.astype(NARROW)
        held[me ^ slot, block:, :] = chunks[slot][block:, :]
    for pair in range(count // 2):
        parts = [split_chunk(held[2 * pair + side]) for side in range(2)]
        cols = slice(pair * 2 * HD, (pair + 1) * 2 * HD)
        for c in range(3):
            joined = jnp.concatenate([parts[0][c], parts[1][c]], axis=1)
            out[c, :, cols] = joined
            sums[c : c + 1, cols] = jnp.sum(joined.astype(WIDE), axis=0, keepdims=True)


def unpack_heads(place, straight, crossed, chunks):
    count = len(chunks)
    block = straight.shape[0]
    return pl.pallas_call(
        unpack_kernel,
        out_shape=(
            jax.ShapeDtypeStruct((3, block, count * HD), NARROW),
            jax.ShapeDtypeStruct((3, count * HD), WIDE),
        ),
        in_specs=[scalar_spec()] + [whole_spec()] * (2 + count),
        out_specs=(whole_spec(),) * 2,
        scratch_shapes=[pltpu.VMEM((count,) + chunks[0].shape, NARROW)],
        compiler_params=params(24),
        cost_estimate=pl.CostEstimate(flops=MIB, bytes_accessed=3 * MIB, transcendentals=0),
    )(place, straight, crossed, *chunks)


def shards(
    inputs,
    segment_ids,
    cotangent,
    qkv_weight,
    qkv_bias,
    out_weight,
    out_bias,
    up_weight,
    up_bias,
    down_weight,
    down_bias,
    input_gain,
    input_bias,
    mixed_gain,
    mixed_bias,
    middle_gain,
    middle_bias,
    hidden_gain,
    hidden_bias,
    qkv_average,
    out_average,
    up_average,
    down_average,
    decay_rate,
):
    seq_count = lax.axis_size("seq")
    seq_rank = lax.axis_index("seq")
    local_rows = segment_ids.shape[0]
    model_width = inputs.shape[1]
    local_width = qkv_weight.shape[2]
    heads_here = local_width // HD
    team = heads_here
    teams = seq_count // team
    place = seq_rank % team
    home = seq_rank - place

    def trade(chunks):
        return [chunks[0]] + [hop(chunks[m], "seq", m, seq_count) for m in range(1, team)]

    row_index = seq_rank * local_rows + jnp.arange(local_rows, dtype=jnp.int32)
    documents = jnp.arange(COUNT, dtype=jnp.int32)
    member = segment_ids[:, None] == documents[None, :]
    first_all = jnp.min(jnp.where(member, row_index[:, None], LARGEST), axis=0)
    bit = 1
    while bit < seq_count:
        first_all = jnp.minimum(first_all, hop(first_all, "seq", bit, seq_count))
        bit *= 2

    def starts_of(rows):
        earlier = first_all[None, :] <= rows[:, None]
        return jnp.max(jnp.where(earlier, first_all[None, :], 0), axis=1)

    cosine, sine, growth = xpos_tables(row_index - starts_of(row_index), HD)
    shrink = 1.0 / growth
    straight = jnp.concatenate([cosine * growth] * 2 + [cosine * shrink] * 2, axis=1)
    crossed = jnp.concatenate(
        [-sine * growth, sine * growth, -sine * shrink, sine * shrink], axis=1
    )
    team_rows = home * local_rows + jnp.arange(team * local_rows, dtype=jnp.int32)
    team_starts = starts_of(team_rows).reshape(team, local_rows)
    spans = jnp.stack([jnp.min(team_starts, axis=1), jnp.max(team_starts, axis=1)], axis=1)
    info = jnp.concatenate([jnp.stack([place, home]).astype(jnp.int32), spans.reshape(-1)])
    team_starts = team_starts.reshape(team, 1, local_rows)
    seat = jnp.reshape(place, (1,)).astype(jnp.int32)

    inputs_wide = inputs.astype(WIDE)
    input_normed, input_back = jax.vjp(
        norm_rows, inputs_wide, input_gain.astype(WIDE), input_bias.astype(WIDE)
    )
    attn_in = gather_rows(input_normed.astype(NARROW))
    rate = decay_rate[0]
    seq_part = model_width // seq_count
    offset = seq_rank * seq_part

    def average(old, weight, axis):
        piece = lax.dynamic_slice_in_dim(weight, offset, seq_part, axis).astype(WIDE)
        return rate * old + (1.0 - rate) * piece

    qkv_new = average(qkv_average, qkv_weight, 1)
    out_new = average(out_average, out_weight, 1)
    up_new = average(up_average, up_weight, 0)
    down_new = average(down_average, down_weight, 1)
    attn_in = after(attn_in, qkv_new, out_new, up_new, down_new)
    grad_rows = gather_rows(after(cotangent, attn_in))

    packs = pack_heads(
        seat, attn_in, qkv_weight, qkv_bias.astype(WIDE), straight, crossed, team
    )
    chunks = trade(packs)
    everyone = None
    if teams > 1:
        rings = [[j + team * t for t in range(teams)] for j in range(team)]
        natural = jnp.stack(chunks)[jnp.arange(team) ^ place]
        everyone = lax.all_gather(
            natural, "seq", axis=0, tiled=True, axis_index_groups=rings
        )
    *mixed_out, mixed_wide, logs = attend_forward(info, team_starts, chunks, everyone)
    mixed_got = trade(mixed_out)
    mixed_got[0] = after(mixed_got[0], grad_rows)
    mixed, mixed_sums = join_heads(seat, mixed_got)
    mixed_sums = tp_total(mixed_sums) / model_width
    mixed_center = mixed_sums[0][:, None]
    mixed_factor = lax.rsqrt(mixed_sums[1][:, None] - mixed_center * mixed_center + EPSILON)
    mixed_unit = (mixed.astype(WIDE) - mixed_center) * mixed_factor
    mixed_low = (mixed_unit * mixed_gain + mixed_bias).astype(NARROW)
    grad_hidden = jnp.einsum("rd,fd->rf", grad_rows, down_weight, preferred_element_type=WIDE)
    out_rows = scatter_rows(jnp.dot(mixed_low, out_weight, preferred_element_type=WIDE))
    out_rows = after(out_rows, grad_hidden)
    middle = inputs_wide + out_rows + out_bias.astype(WIDE)
    middle_normed, middle_back = jax.vjp(
        norm_rows, middle, middle_gain.astype(WIDE), middle_bias.astype(WIDE)
    )
    ffn_in = gather_rows(middle_normed.astype(NARROW))
    up_value = jnp.dot(ffn_in, up_weight, preferred_element_type=WIDE) + up_bias.astype(WIDE)
    activated, gelu_back = jax.vjp(exact_gelu, up_value)
    scaled = grad_hidden * hidden_gain.astype(WIDE)
    sums = jnp.stack(
        [
            jnp.sum(activated, axis=1),
            jnp.sum(activated * activated, axis=1),
            jnp.sum(scaled, axis=1),
            jnp.sum(scaled * activated, axis=1),
        ]
    )
    sums = tp_total(sums) / FF
    center = sums[0][:, None]
    factor = lax.rsqrt(sums[1][:, None] - center * center + EPSILON)
    lean = sums[2][:, None]
    cross = (sums[3][:, None] - center * lean) * factor
    unit = (activated - center) * factor
    hidden_low = (unit * hidden_gain + hidden_bias).astype(NARROW)
    grad_active = (scaled - lean - unit * cross) * factor
    grad_up = gelu_back(grad_active)[0].astype(NARROW)
    hiddengain_part = jnp.sum(grad_hidden * unit, axis=0)
    hiddenbias_part = jnp.sum(grad_hidden, axis=0)
    upbias_part = jnp.sum(grad_up, axis=0, dtype=WIDE)

    grad_ffn_in = scatter_rows(
        jnp.einsum("rf,df->rd", grad_up, up_weight, preferred_element_type=WIDE)
    )
    down_pieces = seq_gradient(hidden_low, grad_rows, seq_rank, seq_count, True)
    grad_ffn_in = after(grad_ffn_in, *down_pieces)
    grad_middle_norm, middlegain_part, middlebias_part = middle_back(grad_ffn_in)
    grad_middle = cotangent.astype(WIDE) + grad_middle_norm
    grad_middle_low = grad_middle.astype(NARROW)
    grad_mixed_rows = gather_rows(grad_middle_low)
    up_pieces = seq_gradient(grad_up[None], ffn_in, seq_rank, seq_count, False)
    down_grad = finish_gradient(down_pieces, seq_count, 0)
    grad_mixed_rows = after(grad_mixed_rows, down_grad, *up_pieces)
    outbias_part = jnp.sum(grad_middle_low, axis=0, dtype=WIDE)
    downbias_part = jnp.sum(cotangent, axis=0, dtype=WIDE)
    grad_mixed_norm = jnp.einsum(
        "rd,fd->rf", grad_mixed_rows, out_weight, preferred_element_type=WIDE
    )
    mixed_scaled = grad_mixed_norm * mixed_gain.astype(WIDE)
    back_sums = tp_total(
        jnp.stack([jnp.sum(mixed_scaled, axis=1), jnp.sum(mixed_scaled * mixed_unit, axis=1)])
    )
    back_sums = back_sums / model_width
    grad_mixed = (
        (mixed_scaled - back_sums[0][:, None] - mixed_unit * back_sums[1][:, None]) * mixed_factor
    ).astype(NARROW)
    mixedgain_part = jnp.sum(grad_mixed_norm * mixed_unit, axis=0)
    mixedbias_part = jnp.sum(grad_mixed_norm, axis=0)
    up_grad = finish_gradient(up_pieces, seq_count, 1)[0]
    out_pieces = seq_gradient(mixed_low, grad_mixed_rows, seq_rank, seq_count, True)

    def spread_norms(parts):
        tp_count = lax.axis_size("tp")
        both = jnp.stack(parts).reshape(len(parts), seq_count, tp_count, -1)
        mine = tp_scatter(both.transpose(2, 1, 0, 3))
        return mine.reshape(seq_count, -1)

    early = jnp.concatenate(
        [
            item.reshape(seq_count, -1)
            for item in (
                upbias_part,
                hiddengain_part,
                hiddenbias_part,
                mixedgain_part,
                mixedbias_part,
            )
        ]
        + [spread_norms([middlegain_part, middlebias_part, outbias_part, downbias_part])],
        axis=1,
    )
    early_sums = vector_scatter(early, seq_rank, seq_count)
    layer_out = (
        middle
        + scatter_rows(jnp.dot(hidden_low, down_weight, preferred_element_type=WIDE))
        + down_bias.astype(WIDE)
    ).astype(NARROW)

    grad_chunks = trade(cut_heads(seat, grad_mixed, team))
    pieces = attend_backward(
        info,
        team_starts,
        logs,
        mixed_wide,
        chunks,
        grad_chunks,
        everyone,
    )
    pieces = list(pieces)
    pieces[0] = after(pieces[0], up_grad, layer_out, early_sums, *out_pieces)
    out_grad = finish_gradient(out_pieces, seq_count, 0)
    if teams > 1:
        natural = lax.psum_scatter(
            pieces[0], "seq", scatter_dimension=0, tiled=True, axis_index_groups=rings
        )
        pieces = [
            lax.dynamic_index_in_dim(natural, place ^ m, 0, keepdims=False) for m in range(team)
        ]
    parts_got = trade(pieces)
    parts_got[0] = after(parts_got[0], out_grad)
    stacked, qkvbias_part = unpack_heads(seat, straight, crossed, parts_got)
    grad_attn_in = scatter_rows(
        jnp.einsum("crf,cdf->rd", stacked, qkv_weight, preferred_element_type=WIDE)
    )
    grad_input_norm, inputgain_part, inputbias_part = input_back(grad_attn_in)
    input_grad = (grad_middle + grad_input_norm).astype(NARROW)

    qkv_pieces = seq_gradient(stacked, attn_in, seq_rank, seq_count, False)
    qkv_grad = finish_gradient(qkv_pieces, seq_count, 1)
    late = jnp.concatenate(
        [
            qkvbias_part.reshape(3, seq_count, -1).transpose(1, 0, 2).reshape(seq_count, -1),
            spread_norms([inputgain_part, inputbias_part]),
        ],
        axis=1,
    )
    late_sums = vector_scatter(late, seq_rank, seq_count)
    narrow_part = local_width // seq_count
    wide_part = up_bias.shape[0] // seq_count
    norm_part = model_width // (seq_count * lax.axis_size("tp"))

    def cuts(vector, widths):
        begin = 0
        pieces = []
        for width in widths:
            pieces.append(vector[begin : begin + width])
            begin += width
        return pieces

    q_bias, k_bias, v_bias, inputgain_grad, inputbias_grad = cuts(
        late_sums, (narrow_part,) * 3 + (norm_part,) * 2
    )
    (
        upbias_grad,
        hiddengain_grad,
        hiddenbias_grad,
        mixedgain_grad,
        mixedbias_grad,
        middlegain_grad,
        middlebias_grad,
        outbias_grad,
        downbias_grad,
    ) = cuts(early_sums, (wide_part,) * 3 + (narrow_part,) * 2 + (norm_part,) * 4)
    return (
        layer_out,
        input_grad,
        qkv_grad,
        jnp.stack([q_bias, k_bias, v_bias]),
        out_grad,
        outbias_grad,
        up_grad,
        upbias_grad,
        down_grad,
        downbias_grad,
        inputgain_grad,
        inputbias_grad,
        mixedgain_grad,
        mixedbias_grad,
        middlegain_grad,
        middlebias_grad,
        hiddengain_grad,
        hiddenbias_grad,
        qkv_new,
        out_new,
        up_new,
        down_new,
    )


def solution(mesh):
    in_specs = (
        P(("seq", "tp"), None),
        P("seq"),
        P(("seq", "tp"), None),
        P(None, None, "tp"),
        P(None, "tp"),
        P("tp", None),
        P(),
        P(None, "tp"),
        P("tp"),
        P("tp", None),
        P(),
        P(),
        P(),
        P("tp"),
        P("tp"),
        P(),
        P(),
        P("tp"),
        P("tp"),
        P(None, "seq", "tp"),
        P("tp", "seq"),
        P("seq", "tp"),
        P("tp", "seq"),
        P(),
    )
    out_specs = (
        P(("seq", "tp"), None),
        P(("seq", "tp"), None),
        P(None, "seq", "tp"),
        P(None, ("tp", "seq")),
        P("tp", "seq"),
        P(("seq", "tp")),
        P("seq", "tp"),
        P(("tp", "seq")),
        P("tp", "seq"),
        P(("seq", "tp")),
        P(("seq", "tp")),
        P(("seq", "tp")),
        P(("tp", "seq")),
        P(("tp", "seq")),
        P(("seq", "tp")),
        P(("seq", "tp")),
        P(("tp", "seq")),
        P(("tp", "seq")),
        P(None, "seq", "tp"),
        P("tp", "seq"),
        P("seq", "tp"),
        P("tp", "seq"),
    )
    return jax.shard_map(shards, mesh=mesh, in_specs=in_specs, out_specs=out_specs, check_vma=False)
```

time: 1580 us -> 671 us (0.42)
  waiting for transfers between devices: 1110 us -> 300 us
  Pallas kernels: 0 us -> 111 us
  blocking collectives: 86.9 us -> 0 us
  loops' own time: 84.6 us -> 0 us
  matrix products: 134 us -> 61.8 us
  starting transfers between devices: 0.96 us -> 72.7 us
  local copies, waits for them, and re-layouts: 78.6 us -> 38.7 us
    reduce_scatter x9 -> x4, waiting for transfers between devices: 760 us -> 78.3 us  [scatter_rows(): lax.psum_scatter(values.astype(NARROW), 'tp', scatter_dimension=0, tiled=...]
    unnamed x19 -> x8, waiting for transfers between devices: 170 us -> 0.13 us
    ppermute x0 -> x72, waiting for transfers between devices: none -> 139 us  [hop(): return lax.ppermute(values, axis, [(i, i ^ mask) for i in range(count)])]
    pallas_call x0 -> x14, Pallas kernels: none -> 111 us  [the longest x1 35.2 us: attend_backward(): pl.pallas_call(functools.partial(backward_kernel, groups=count, spread=sp...]
    another operation x36 -> x0, loops' own time: 84.6 us -> none  [the longest x1 21.1 us: shards(): (top, total), _ = lax.scan(measure, start_state, (key_blocks, block_starts))]
    ppermute x0 -> x72, starting transfers between devices: none -> 72.3 us  [hop(): return lax.ppermute(values, axis, [(i, i ^ mask) for i in range(count)])]
    dot_general x20 -> x6, matrix products: 129 us -> 57.3 us  [the longest x1 17.7 us: shards(): jnp.dot(ffn_in, up_weight, preferred_element_type=WIDE)]
    all_gather x4, waiting for transfers between devices: 146 us -> 82.5 us  [gather_rows(): return lax.all_gather(values, 'tp', axis=0, tiled=True)]
  transfers between devices with their start and end apart: 17 -> 80, of which waited for: 17 -> 38; matrix products, arithmetic and copies ran while one was open for 8% -> 14% of each run, Pallas kernels for 0% -> 16%
where the time goes in v1:
time: 671 us; the launch traced here: 662 us
  waiting for transfers between devices  300 us (45%)
  Pallas kernels  111 us (17%)
  starting transfers between devices  72.7 us (11%)
  matrix products  61.8 us (9%)
  other arithmetic  61 us (9%)
  local copies, waits for them, and re-layouts  38.7 us (6%)
  between operations  16.7 us (2%)
    ppermute x72, waiting for transfers between devices, hop(): return lax.ppermute(values, axis, [(i, i ^ mask) for i in range(count)])  139 us
    all_gather x4, waiting for transfers between devices, gather_rows(): return lax.all_gather(values, 'tp', axis=0, tiled=True)  82.5 us
    reduce_scatter x4, waiting for transfers between devices, scatter_rows(): lax.psum_scatter(values.astype(NARROW), 'tp', scatter_dimension=0, tiled=...  78.3 us
    ppermute x72, starting transfers between devices, hop(): return lax.ppermute(values, axis, [(i, i ^ mask) for i in range(count)])  72.3 us
    pallas_call x1, Pallas kernels, attend_backward(): pl.pallas_call(functools.partial(backward_kernel, groups=count, spread=sp...  35.2 us
    pallas_call x8, Pallas kernels, gradient_blocks(): pl.pallas_call(functools.partial(sent_kernel if got is None else kept_ker...  34.7 us
    pallas_call x1, Pallas kernels, attend_forward(): pl.pallas_call(functools.partial(forward_kernel, groups=count, spread=spr...  28.5 us
    unnamed x152, local copies, waits for them, and re-layouts  21.8 us
  transfers between devices with their start and end apart: 80, of which 38 were waited for; matrix products, arithmetic and copies ran while one was open for 14% of the time, Pallas kernels for 16%

profile of v1, /device:TPU:0, one launch (start us, length us, event | category | flops | bytes accessed | tf_op | source)
XLA Modules:
  0.0 661.6 jit_solution(12495086099859693408)
XLA Ops:
  25.0 37.1 %all-gather.5.cloned.1.call-done.rows.right = bf16[512,2048]{1,0:T(8,128)(2,1)} async-done(((bf16[128,2048]{1,0:T(8,128)(2,1)}), bf16[512,2048]{1,0:T(8,128)(2,1)}) %all-gather.5.cloned.1.call-update) | async-done | bytes 2097168 | tf_op jit(solution)/shard_map/all_gather | solution.py:48
  72.3 10.7 %shard_map.399 = (bf16[768,128]{1,0:T(8,128)(2,1)S(1)}, bf16[768,128]{1,0:T(8,128)(2,1)}, bf16[768,128]{1,0:T(8,128)(2,1)}, bf16[768,128]{1,0:T(8,128)(2,1)S(1)}...) custom-call(s32[1]{0:T(128)} %bitcast.place, ...), custom_call_target="tpu_custom_call" | custom-call | flops 3221225472 | bytes 14680064 | tf_op jit(solution)/shard_map/pallas_call | solution.py:246
  95.0 10.0 %collective-permute-done.7.refs_5_ = bf16[768,128]{1,0:T(8,128)(2,1)S(1)} collective-permute-done((bf16[768,128]{1,0:T(8,128)(2,1)S(1)}, bf16[768,128]{1,0:T(8,128)(2,1)S(1)}, u32[]{:S(2)}, u32[]{:S(2)}) %collective-permute-start.7) | collective-permute-done | bytes 196640 | tf_op jit(solution)/shard_map/ppermute | solution.py:56
  106.2 28.5 %shard_map.400 = (bf16[64,512]{1,0:T(8,128)(2,1)S(1)}, bf16[64,512]{1,0:T(8,128)(2,1)S(1)}, bf16[64,512]{1,0:T(8,128)(2,1)S(1)}, bf16[64,512]{1,0:T(8,128)(2,1)S...) custom-call(s32[18]{0:T(128)S(1)} %pad_add_fusion.1.info, ...), custom_call_target="tpu_custom_call" | custom-call | flops 8589934592 | bytes 4194304 | tf_op jit(solution)/shard_map/pallas_call | solution.py:347
  156.3 4.3 convolution_convert_fusion.2
  160.8 9.5 %fusion.56 = f32[512,2048]{1,0:T(8,128)} fusion(bf16[512,2048]{1,0:T(8,128)(2,1)S(1)} %copy-done.5, bf16[2048,2048]{1,0:T(8,128)(2,1)} %param.33), kind=kOutput, calls=%fused_computation.225 | convolution fusion | flops 4294967296 | bytes 14680064 | tf_op jit(solution)/shard_map/rd,fd->rf/dot_general | solution.py:700
  170.3 33.6 %reduce-scatter.5.cloned.1.call-done = bf16[128,2048]{1,0:T(8,128)(2,1)} async-done(((bf16[512,2048]{1,0:T(8,128)(2,1)}), bf16[128,2048]{1,0:T(8,128)(2,1)}) %reduce-scatter.5.cloned.1.call-update) | async-done | bytes 524304 | tf_op jit(solution)/shard_map/reduce_scatter | solution.py:52
  207.6 45.3 %all-gather.9.cloned.1.call-done.right = bf16[512,2048]{1,0:T(8,128)(2,1)} async-done(((bf16[128,2048]{1,0:T(8,128)(2,1)}), bf16[512,2048]{1,0:T(8,128)(2,1)}) %all-gather.9.cloned.1.call-update) | async-done | bytes 2097168 | tf_op jit(solution)/shard_map/all_gather | solution.py:48
  252.9 17.7 %multiply_reduce_fusion.3 = (f32[512]{0:T(512)S(1)}, f32[512]{0:T(512)S(1)}, f32[512]{0:T(512)S(1)}, f32[512]{0:T(512)S(1)}, f32[512,2048]{1,0:T(8,128)S(1)}, /*...) fusion(f32[512,2048]{1,0:T(8,128)} %fusion.56, f32[2048]{0:T(1024)S(1)} %convert_element_type.327, ...), kind=kOutput, calls=%fused_computation.24 | convolution fusion | flops 4370462720 | bytes 27287552 | tf_op jit(solution)/shard_map/dot_general | solution.py:708
  278.0 6.1 fusion.45
  284.1 9.1 %convolution_convert_fusion = bf16[512,2048]{1,0:T(8,128)(2,1)} fusion(bf16[512,2048]{1,0:T(8,128)(2,1)S(1)} %get-tuple-element.171, bf16[2048,2048]{1,0:T(8,128)(2,1)} %param.31), kind=kOutput, calls=%fused_computation.25 | convolution fusion | flops 4296015872 | bytes 12582912 | tf_op jit(solution)/shard_map/rf,df->rd/dot_general | solution.py:733
  296.5 5.1 shard_map.402
  301.6 9.1 %convolution_convert_fusion.1 = bf16[512,2048]{1,0:T(8,128)(2,1)} fusion(bf16[512,2048]{1,0:T(8,128)(2,1)S(1)} %copy-done, bf16[2048,2048]{1,0:T(8,128)(2,1)} %param.33), kind=kOutput, calls=%fused_computation.26 | convolution fusion | flops 4296015872 | bytes 12582912 | tf_op jit(solution)/shard_map/dot_general | solution.py:785
  312.3 4.9 shard_map.404
  321.0 5.6 shard_map.403
  330.3 7.1 %reduce-scatter.9.cloned.1.call-done = bf16[128,2048]{1,0:T(8,128)(2,1)} async-done(((bf16[512,2048]{1,0:T(8,128)(2,1)}), bf16[128,2048]{1,0:T(8,128)(2,1)}) %reduce-scatter.9.cloned.1.call-update) | async-done | bytes 524304 | tf_op jit(solution)/shard_map/reduce_scatter | solution.py:52
  345.2 37.6 %reduce-scatter.7.cloned.1.call-done = bf16[128,2048]{1,0:T(8,128)(2,1)} async-done(((bf16[512,2048]{1,0:T(8,128)(2,1)}), bf16[128,2048]{1,0:T(8,128)(2,1)}) %reduce-scatter.7.cloned.1.call-update) | async-done | bytes 524304 | tf_op jit(solution)/shard_map/reduce_scatter | solution.py:52
  389.9 5.7 shard_map.405
  401.1 12.0 %collective-permute-done.26 = bf16[2,1024,256]{2,1,0:T(8,128)(2,1)} collective-permute-done((bf16[2,1024,256]{2,1,0:T(8,128)(2,1)}, bf16[2,1024,256]{2,1,0:T(8,128)(2,1)}, u32[]{:S(2)}, u32[]{:S(2)}) %collective-permute-start.26) | collective-permute-done | bytes 1048608 | tf_op jit(solution)/shard_map/ppermute | solution.py:56
  416.2 5.7 collective-permute-done.39
  422.9 12.5 %collective-permute-done.41 = bf16[2,1,128,2048]{3,2,1,0:T(8,128)(2,1)S(1)} collective-permute-done((bf16[2,1,128,2048]{3,2,1,0:T(8,128)(2,1)S(1)}, bf16[2,1,128,2048]{3,2,1,0:T(8,128)(2,1)S(1)}, u32[]{:S(2)}, u32[]{:S(2)}) %collective-permute-start.41) | collective-permute-done | bytes 1048608 | tf_op jit(solution)/shard_map/ppermute | solution.py:56
  438.2 8.5 %collective-permute-done.25 = bf16[1024,256]{1,0:T(8,128)(2,1)S(1)} collective-permute-done((bf16[1024,256]{1,0:T(8,128)(2,1)S(1)}, bf16[1024,256]{1,0:T(8,128)(2,1)S(1)}, u32[]{:S(2)}, u32[]{:S(2)}) %collective-permute-start.25) | collective-permute-done | bytes 524320 | tf_op jit(solution)/shard_map/ppermute | solution.py:56
  448.5 8.1 %collective-permute-done.40 = bf16[1,128,2048]{2,1,0:T(8,128)(2,1)S(1)} collective-permute-done((bf16[1,128,2048]{2,1,0:T(8,128)(2,1)S(1)}, bf16[1,128,2048]{2,1,0:T(8,128)(2,1)S(1)}, u32[]{:S(2)}, u32[]{:S(2)}) %collective-permute-start.40) | collective-permute-done | bytes 524320 | tf_op jit(solution)/shard_map/ppermute | solution.py:56
  456.8 4.5 multiply_reduce_fusion.5
  486.5 35.2 %shard_map.407 = (bf16[768,128]{1,0:T(8,128)(2,1)}, bf16[768,128]{1,0:T(8,128)(2,1)}, bf16[768,128]{1,0:T(8,128)(2,1)}, bf16[768,128]{1,0:T(8,128)(2,1)}, bf16[7...) custom-call(s32[18]{0:T(128)} %copy-done.22, ...), custom_call_target="tpu_custom_call" | custom-call | flops 21474836480 | bytes 6291456 | tf_op jit(solution)/shard_map/pallas_call | solution.py:475
  525.9 10.8 %collective-permute-done.46 = bf16[2,256,256]{2,1,0:T(8,128)(2,1)S(1)} collective-permute-done((bf16[2,256,256]{2,1,0:T(8,128)(2,1)S(1)}, bf16[2,256,256]{2,1,0:T(8,128)(2,1)S(1)}, u32[]{:S(2)}, u32[]{:S(2)}) %collective-permute-start.46) | collective-permute-done | bytes 262176 | tf_op jit(solution)/shard_map/ppermute | solution.py:56
  537.3 4.3 collective-permute-done.45
  547.5 10.6 %collective-permute-done.52.refs_5_ = bf16[768,128]{1,0:T(8,128)(2,1)S(1)} collective-permute-done((bf16[768,128]{1,0:T(8,128)(2,1)}, bf16[768,128]{1,0:T(8,128)(2,1)S(1)}, u32[]{:S(2)}, u32[]{:S(2)}) %collective-permute-start.52) | collective-permute-done | bytes 196640 | tf_op jit(solution)/shard_map/ppermute | solution.py:56
  559.5 4.3 shard_map.411
  564.0 7.6 %bitcast_convert_fusion = bf16[512,2048]{1,0:T(8,128)(2,1)} fusion(bf16[3,512,512]{2,1,0:T(8,128)(2,1)S(1)} %get-tuple-element.126.left, bf16[3,2048,512]{2,1,0:T(8,128)(2,1)} %weight.1), kind=kOutput, calls=%fused_computation.2 | convolution fusion | flops 3222274048 | bytes 9961472 | tf_op jit(solution)/shard_map/crf,cdf->rd/dot_general | solution.py:813
  589.5 4.8 shard_map.412
  598.8 15.7 %collective-permute-done.56 = bf16[2,3,128,512]{3,2,1,0:T(8,128)(2,1)} collective-permute-done((bf16[2,3,128,512]{3,2,1,0:T(8,128)(2,1)S(1)}, bf16[2,3,128,512]{3,2,1,0:T(8,128)(2,1)}, u32[]{:S(2)}, u32[]{:S(2)}) %collective-permute-start.56) | collective-permute-done | bytes 786464 | tf_op jit(solution)/shard_map/ppermute | solution.py:56
  (454 shorter events, 213.3 us)
Async XLA Ops:
  7.2 54.9 %all-gather.5.cloned.1.call-start = ((), (), s32[]{:S(2)}) async-start(), calls=%async_computation.4 | async-start | bytes 2621440 | tf_op jit(solution)/shard_map/all_gather | solution.py:48
  13.3 129.2 %all-gather.7.cloned.1.call-start = ((), (), s32[]{:S(2)}) async-start(), calls=%async_computation.5 | async-start | bytes 2621440 | tf_op jit(solution)/shard_map/all_gather | solution.py:48
  62.2 141.7 %reduce-scatter.5.cloned.1.call-start = ((), (), s32[]{:S(2)}) async-start(), calls=%async_computation.6 | async-start | bytes 2621440 | tf_op jit(solution)/shard_map/reduce_scatter | solution.py:52
  87.4 17.6 %collective-permute-start.7 = (bf16[768,128]{1,0:T(8,128)(2,1)S(1)}, bf16[768,128]{1,0:T(8,128)(2,1)S(1)}, u32[]{:S(2)}, u32[]{:S(2)}) collective-permute-start(bf16[768,128]{1,0:T(8,128)(2,1)S(1)} %get-tuple-element.82), channel_id=1, source_target_pairs={{0,20},{4,16},{8,28},{12,24},{16,4},{20,0},{24,12},{28,8},{1,21},{... | collective-permute-start | bytes 589832 | tf_op jit(solution)/shard_map/ppermute | solution.py:56
  87.6 17.4 %collective-permute-start.8 = (bf16[768,128]{1,0:T(8,128)(2,1)S(1)}, bf16[768,128]{1,0:T(8,128)(2,1)S(1)}, u32[]{:S(2)}, u32[]{:S(2)}) collective-permute-start(bf16[768,128]{1,0:T(8,128)(2,1)S(1)} %get-tuple-element.83), channel_id=1, source_target_pairs={{0,24},{4,28},{8,16},{12,20},{16,8},{20,12},{24,0},{28,4},{1,25},{... | collective-permute-start | bytes 589832 | tf_op jit(solution)/shard_map/ppermute | solution.py:56
  160.7 92.2 %all-gather.9.cloned.1.call-start = ((), (), s32[]{:S(2)}) async-start(), calls=%async_computation.7 | async-start | bytes 2621440 | tf_op jit(solution)/shard_map/all_gather | solution.py:48
  207.5 130.0 %reduce-scatter.9.cloned.1.call-start = ((), (), s32[]{:S(2)}) async-start(), calls=%async_computation.9 | async-start | bytes 2621440 | tf_op jit(solution)/shard_map/reduce_scatter | solution.py:52
  293.2 89.6 %reduce-scatter.7.cloned.1.call-start = ((), (), s32[]{:S(2)}) async-start(), calls=%async_computation.8 | async-start | bytes 2621440 | tf_op jit(solution)/shard_map/reduce_scatter | solution.py:52
  301.6 16.3 %collective-permute-start.23 = (bf16[4,2048,256]{2,1,0:T(8,128)(2,1)}, bf16[4,2048,256]{2,1,0:T(8,128)(2,1)}, u32[]{:S(2)}, u32[]{:S(2)}) collective-permute-start(bf16[4,2048,256]{2,1,0:T(8,128)(2,1)} %shard_map.402), channel_id=1, source_target_pairs={{0,4},{4,0},{8,12},{12,8},{16,20},{20,16},{24,28},{28,24},{1,5},{5... | collective-permute-start | bytes 12582920 | tf_op jit(solution)/shard_map/ppermute | solution.py:56
  310.6 146.1 %all-gather.11.cloned.1.call-start = ((), (), s32[]{:S(2)}) async-start(), calls=%async_computation.10 | async-start | bytes 2621440 | tf_op jit(solution)/shard_map/all_gather | solution.py:48
  317.2 71.1 %collective-permute-start.28 = (bf16[4,1,256,2048]{3,2,1,0:T(8,128)(2,1)}, bf16[4,1,256,2048]{3,2,1,0:T(8,128)(2,1)}, u32[]{:S(2)}, u32[]{:S(2)}) collective-permute-start(bf16[4,1,256,2048]{3,2,1,0:T(8,128)(2,1)} %shard_map.404), channel_id=1, source_target_pairs={{0,4},{4,0},{8,12},{12,8},{16,20},{20,16},{24,28},{28,24},{1,5},{5... | collective-permute-start | bytes 12582920 | tf_op jit(solution)/shard_map/ppermute | solution.py:56
  343.7 54.2 %collective-permute-start.24 = (bf16[2,1024,256]{2,1,0:T(8,128)(2,1)}, bf16[2,1024,256]{2,1,0:T(8,128)(2,1)}, u32[]{:S(2)}, u32[]{:S(2)}) collective-permute-start(bf16[2,1024,256]{2,1,0:T(8,128)(2,1)} %slice_bitcast_fusion.2), channel_id=1, source_target_pairs={{0,8},{4,12},{8,0},{12,4},{16,24},{20,28},{24,16},{28,20},{1,9},{5... | collective-permute-start | bytes 3145736 | tf_op jit(solution)/shard_map/ppermute | solution.py:56
  386.7 26.4 %collective-permute-start.26 = (bf16[2,1024,256]{2,1,0:T(8,128)(2,1)}, bf16[2,1024,256]{2,1,0:T(8,128)(2,1)}, u32[]{:S(2)}, u32[]{:S(2)}) collective-permute-start(bf16[2,1024,256]{2,1,0:T(8,128)(2,1)} %slice.217), channel_id=1, source_target_pairs={{0,16},{4,20},{8,24},{12,28},{16,0},{20,4},{24,8},{28,12},{1,17},{... | collective-permute-start | bytes 3145736 | tf_op jit(solution)/shard_map/ppermute | solution.py:56
  388.2 230.4 %reduce-scatter.11.cloned.1.call-start = ((), (), s32[]{:S(2)}) async-start(), calls=%async_computation.11 | async-start | bytes 2621440 | tf_op jit(solution)/shard_map/reduce_scatter | solution.py:52
  395.7 26.2 %collective-permute-start.39 = (bf16[2,1,128,2048]{3,2,1,0:T(8,128)(2,1)S(1)}, bf16[2,1,128,2048]{3,2,1,0:T(8,128)(2,1)S(1)}, u32[]{:S(2)}, u32[]{:S(2)}) collective-permute-start(bf16[2,1,128,2048]{3,2,1,0:T(8,128)(2,1)S(1)} %slice_bitcast_fusion), channel_id=1, source_target_pairs={{0,8},{4,12},{8,0},{12,4},{16,24},{20,28},{24,16},{28,20},{1,9},{5... | collective-permute-start | bytes 3145736 | tf_op jit(solution)/shard_map/ppermute | solution.py:56
  397.3 38.2 %collective-permute-start.41 = (bf16[2,1,128,2048]{3,2,1,0:T(8,128)(2,1)S(1)}, bf16[2,1,128,2048]{3,2,1,0:T(8,128)(2,1)S(1)}, u32[]{:S(2)}, u32[]{:S(2)}) collective-permute-start(bf16[2,1,128,2048]{3,2,1,0:T(8,128)(2,1)S(1)} %slice.227), channel_id=1, source_target_pairs={{0,16},{4,20},{8,24},{12,28},{16,0},{20,4},{24,8},{28,12},{1,17},{... | collective-permute-start | bytes 3145736 | tf_op jit(solution)/shard_map/ppermute | solution.py:56
  399.5 47.2 %collective-permute-start.25 = (bf16[1024,256]{1,0:T(8,128)(2,1)S(1)}, bf16[1024,256]{1,0:T(8,128)(2,1)S(1)}, u32[]{:S(2)}, u32[]{:S(2)}) collective-permute-start(bf16[1024,256]{1,0:T(8,128)(2,1)S(1)} %slice_bitcast_fusion.12), channel_id=1, source_target_pairs={{0,16},{4,20},{8,24},{12,28},{16,0},{20,4},{24,8},{28,12},{1,17},{... | collective-permute-start | bytes 1572872 | tf_op jit(solution)/shard_map/ppermute | solution.py:56
  414.7 32.2 %collective-permute-start.27 = (bf16[1024,256]{1,0:T(8,128)(2,1)S(1)}, bf16[1024,256]{1,0:T(8,128)(2,1)S(1)}, u32[]{:S(2)}, u32[]{:S(2)}) collective-permute-start(bf16[1024,256]{1,0:T(8,128)(2,1)S(1)} %slice_bitcast_fusion.10), channel_id=1, source_target_pairs={{0,8},{4,12},{8,0},{12,4},{16,24},{20,28},{24,16},{28,20},{1,9},{5... | collective-permute-start | bytes 1572872 | tf_op jit(solution)/shard_map/ppermute | solution.py:56
  422.3 34.3 %collective-permute-start.40 = (bf16[1,128,2048]{2,1,0:T(8,128)(2,1)S(1)}, bf16[1,128,2048]{2,1,0:T(8,128)(2,1)S(1)}, u32[]{:S(2)}, u32[]{:S(2)}) collective-permute-start(bf16[1,128,2048]{2,1,0:T(8,128)(2,1)S(1)} %slice_bitcast_fusion.8), channel_id=1, source_target_pairs={{0,16},{4,20},{8,24},{12,28},{16,0},{20,4},{24,8},{28,12},{1,17},{... | collective-permute-start | bytes 1572872 | tf_op jit(solution)/shard_map/ppermute | solution.py:56
  436.7 31.2 %collective-permute-start.42 = (bf16[1,128,2048]{2,1,0:T(8,128)(2,1)}, bf16[1,128,2048]{2,1,0:T(8,128)(2,1)}, u32[]{:S(2)}, u32[]{:S(2)}) collective-permute-start(bf16[1,128,2048]{2,1,0:T(8,128)(2,1)} %slice_bitcast_fusion.6), channel_id=1, source_target_pairs={{0,8},{4,12},{8,0},{12,4},{16,24},{20,28},{24,16},{28,20},{1,9},{5... | collective-permute-start | bytes 1572872 | tf_op jit(solution)/shard_map/ppermute | solution.py:56
  480.7 43.6 %collective-permute-start.44 = (bf16[2,256,256]{2,1,0:T(8,128)(2,1)S(1)}, bf16[2,256,256]{2,1,0:T(8,128)(2,1)S(1)}, u32[]{:S(2)}, u32[]{:S(2)}) collective-permute-start(bf16[2,256,256]{2,1,0:T(8,128)(2,1)S(1)} %slice_bitcast_fusion.18), channel_id=1, source_target_pairs={{0,8},{4,12},{8,0},{12,4},{16,24},{20,28},{24,16},{28,20},{1,9},{5... | collective-permute-start | bytes 786440 | tf_op jit(solution)/shard_map/ppermute | solution.py:56
  521.7 20.8 %collective-permute-start.48 = (bf16[768,128]{1,0:T(8,128)(2,1)}, bf16[768,128]{1,0:T(8,128)(2,1)S(1)}, u32[]{:S(2)}, u32[]{:S(2)}) collective-permute-start(bf16[768,128]{1,0:T(8,128)(2,1)} %get-tuple-element.119), channel_id=1, source_target_pairs={{0,4},{4,0},{8,12},{12,8},{16,20},{20,16},{24,28},{28,24},{1,5},{5... | collective-permute-start | bytes 589832 | tf_op jit(solution)/shard_map/ppermute | solution.py:56
  521.8 20.8 %collective-permute-start.49 = (bf16[768,128]{1,0:T(8,128)(2,1)}, bf16[768,128]{1,0:T(8,128)(2,1)S(1)}, u32[]{:S(2)}, u32[]{:S(2)}) collective-permute-start(bf16[768,128]{1,0:T(8,128)(2,1)} %get-tuple-element.120), channel_id=1, source_target_pairs={{0,8},{4,12},{8,0},{12,4},{16,24},{20,28},{24,16},{28,20},{1,9},{5... | collective-permute-start | bytes 589832 | tf_op jit(solution)/shard_map/ppermute | solution.py:56
  522.4 25.1 %collective-permute-start.50 = (bf16[768,128]{1,0:T(8,128)(2,1)}, bf16[768,128]{1,0:T(8,128)(2,1)S(1)}, u32[]{:S(2)}, u32[]{:S(2)}) collective-permute-start(bf16[768,128]{1,0:T(8,128)(2,1)} %get-tuple-element.121), channel_id=1, source_target_pairs={{0,12},{4,8},{8,4},{12,0},{16,28},{20,24},{24,20},{28,16},{1,13},{... | collective-permute-start | bytes 589832 | tf_op jit(solution)/shard_map/ppermute | solution.py:56
  523.7 23.9 %collective-permute-start.51 = (bf16[768,128]{1,0:T(8,128)(2,1)}, bf16[768,128]{1,0:T(8,128)(2,1)S(1)}, u32[]{:S(2)}, u32[]{:S(2)}) collective-permute-start(bf16[768,128]{1,0:T(8,128)(2,1)} %get-tuple-element.122), channel_id=1, source_target_pairs={{0,16},{4,20},{8,24},{12,28},{16,0},{20,4},{24,8},{28,12},{1,17},{... | collective-permute-start | bytes 589832 | tf_op jit(solution)/shard_map/ppermute | solution.py:56
  542.5 15.6 %collective-permute-start.52 = (bf16[768,128]{1,0:T(8,128)(2,1)}, bf16[768,128]{1,0:T(8,128)(2,1)S(1)}, u32[]{:S(2)}, u32[]{:S(2)}) collective-permute-start(bf16[768,128]{1,0:T(8,128)(2,1)} %get-tuple-element.123), channel_id=1, source_target_pairs={{0,20},{4,16},{8,28},{12,24},{16,4},{20,0},{24,12},{28,8},{1,21},{... | collective-permute-start | bytes 589832 | tf_op jit(solution)/shard_map/ppermute | solution.py:56
  542.6 15.5 %collective-permute-start.53 = (bf16[768,128]{1,0:T(8,128)(2,1)}, bf16[768,128]{1,0:T(8,128)(2,1)S(1)}, u32[]{:S(2)}, u32[]{:S(2)}) collective-permute-start(bf16[768,128]{1,0:T(8,128)(2,1)} %get-tuple-element.124), channel_id=1, source_target_pairs={{0,24},{4,28},{8,16},{12,20},{16,8},{20,12},{24,0},{28,4},{1,25},{... | collective-permute-start | bytes 589832 | tf_op jit(solution)/shard_map/ppermute | solution.py:56
  563.8 24.2 %collective-permute-start.55 = (bf16[4,3,256,512]{3,2,1,0:T(8,128)(2,1)}, bf16[4,3,256,512]{3,2,1,0:T(8,128)(2,1)}, u32[]{:S(2)}, u32[]{:S(2)}) collective-permute-start(bf16[4,3,256,512]{3,2,1,0:T(8,128)(2,1)} %shard_map.411), channel_id=1, source_target_pairs={{0,4},{4,0},{8,12},{12,8},{16,20},{20,16},{24,28},{28,24},{1,5},{5... | collective-permute-start | bytes 9437192 | tf_op jit(solution)/shard_map/ppermute | solution.py:56
  594.4 20.1 %collective-permute-start.56 = (bf16[2,3,128,512]{3,2,1,0:T(8,128)(2,1)S(1)}, bf16[2,3,128,512]{3,2,1,0:T(8,128)(2,1)}, u32[]{:S(2)}, u32[]{:S(2)}) collective-permute-start(bf16[2,3,128,512]{3,2,1,0:T(8,128)(2,1)S(1)} %slice_bitcast_fusion.4), channel_id=1, source_target_pairs={{0,8},{4,12},{8,0},{12,4},{16,24},{20,28},{24,16},{28,20},{1,9},{5... | collective-permute-start | bytes 2359304 | tf_op jit(solution)/shard_map/ppermute | solution.py:56
  596.5 20.6 %collective-permute-start.58 = (bf16[2,3,128,512]{3,2,1,0:T(8,128)(2,1)}, bf16[2,3,128,512]{3,2,1,0:T(8,128)(2,1)}, u32[]{:S(2)}, u32[]{:S(2)}) collective-permute-start(bf16[2,3,128,512]{3,2,1,0:T(8,128)(2,1)} %slice.243), channel_id=1, source_target_pairs={{0,16},{4,20},{8,24},{12,28},{16,0},{20,4},{24,8},{28,12},{1,17},{... | collective-permute-start | bytes 2359304 | tf_op jit(solution)/shard_map/ppermute | solution.py:56
  616.1 34.7 %collective-permute-start.57 = (bf16[3,128,512]{2,1,0:T(8,128)(2,1)S(1)}, bf16[3,128,512]{2,1,0:T(8,128)(2,1)}, u32[]{:S(2)}, u32[]{:S(2)}) collective-permute-start(bf16[3,128,512]{2,1,0:T(8,128)(2,1)S(1)} %slice_bitcast_fusion.16), channel_id=1, source_target_pairs={{0,16},{4,20},{8,24},{12,28},{16,0},{20,4},{24,8},{28,12},{1,17},{... | collective-permute-start | bytes 1179656 | tf_op jit(solution)/shard_map/ppermute | solution.py:56
  632.5 19.5 %collective-permute-start.59 = (bf16[3,128,512]{2,1,0:T(8,128)(2,1)}, bf16[3,128,512]{2,1,0:T(8,128)(2,1)}, u32[]{:S(2)}, u32[]{:S(2)}) collective-permute-start(bf16[3,128,512]{2,1,0:T(8,128)(2,1)} %slice_bitcast_fusion.14), channel_id=1, source_target_pairs={{0,8},{4,12},{8,0},{12,4},{16,24},{20,28},{24,16},{28,20},{1,9},{5... | collective-permute-start | bytes 1179656 | tf_op jit(solution)/shard_map/ppermute | solution.py:56
  (122 other events, 1504.0 us)
Sparse Core Ops, SparseCore 0:
  13.5 48.6 all-gather.4
  63.7 44.6 all-gather.6
  160.8 43.0 reduce-scatter.4
  207.6 45.2 all-gather.8
  293.3 44.1 reduce-scatter.8
  339.6 43.1 reduce-scatter.6
  388.3 44.3 all-gather.10
  571.7 42.4 reduce-scatter.10

commit v2 on v1

v2 whole, which is shorter than its diff:
```python
import functools
import math

import jax
import jax.numpy as jnp
from jax import lax
from jax.experimental import pallas as pl
from jax.experimental.pallas import tpu as pltpu
from jax.sharding import PartitionSpec as P

FF = 8192
COUNT = 16
HD = 64

SCALE = 0.125
LOG2E = 1.4426950408889634
EPSILON = 1e-05
OUTSIDE = -2e30
LOWEST = -1e30
LARGEST = 1 << 30
WIDE = jnp.float32
NARROW = jnp.bfloat16
MIB = 1 << 20
SMALL = pl.CostEstimate(flops=1 << 20, bytes_accessed=1 << 16, transcendentals=0)


def xpos_tables(positions, head_size):
    half = head_size // 2
    index = jnp.arange(half, dtype=jnp.float32)
    frequency = jnp.exp(index * (-2.0 * math.log(10000.0) / head_size))
    zeta = (index * (2.0 / head_size) + 0.4) / 1.4
    places = positions.astype(jnp.float32)[:, None]
    angle = places * frequency[None, :]
    growth = jnp.exp(places * (jnp.log(zeta)[None, :] / 512.0))
    return (jnp.cos(angle), jnp.sin(angle), growth)


def norm_rows(values, gain, shift):
    center = jnp.mean(values, axis=-1, keepdims=True)
    spread = jnp.mean(values * values, axis=-1, keepdims=True) - center * center
    return (values - center) * lax.rsqrt(spread + EPSILON) * gain + shift


def exact_gelu(values):
    return jax.nn.gelu(values, approximate=False)


def gather_rows(values):
    return lax.all_gather(values, "tp", axis=0, tiled=True)


def ring_order(count):
    return [0] + list(range(1, count, 2)) + list(range(2, count, 2))[::-1]


def gather_parts(values):
    order = ring_order(lax.axis_size("tp"))
    parts = [values]
    for _ in order[1:]:
        pairs = [(a, b) for a, b in zip(order, order[1:] + order[:1])]
        parts.append(lax.ppermute(parts[-1], "tp", pairs))
    return parts


def part_owners():
    order = ring_order(lax.axis_size("tp"))
    count = len(order)
    spot = jnp.array([order.index(rank) for rank in range(count)], jnp.int32)[lax.axis_index("tp")]
    ranks = jnp.array(order, jnp.int32)
    return [ranks[(spot + count - slot) % count] for slot in range(count)]


def scatter_rows(values):
    return lax.psum_scatter(values.astype(NARROW), "tp", scatter_dimension=0, tiled=True).astype(WIDE)


def hop(values, axis, mask, count):
    return lax.ppermute(values, axis, [(i, i ^ mask) for i in range(count)])


def tp_total(values):
    count = lax.axis_size("tp")
    if count & (count - 1):
        return lax.psum(values, "tp")
    total = values
    for mask in range(1, count):
        total = total + hop(values, "tp", mask, count)
    return total


def after(value, *others):
    return lax.optimization_barrier((value,) + others)[0]


def vector_scatter(values, rank, count):
    bit = count // 2
    while bit:
        pair = values.reshape(2, bit, -1)
        mine = (rank & bit) // bit
        send = lax.dynamic_index_in_dim(pair, 1 - mine, 0, keepdims=False)
        keep = lax.dynamic_index_in_dim(pair, mine, 0, keepdims=False)
        values = keep + hop(send, "seq", bit, count)
        bit //= 2
    return values.reshape(-1)


def tp_scatter(values):
    count = lax.axis_size("tp")
    rank = lax.axis_index("tp")
    if count & (count - 1):
        return lax.psum_scatter(values, "tp", scatter_dimension=0)
    total = lax.dynamic_index_in_dim(values, rank, 0, keepdims=False)
    for mask in range(1, count):
        part = lax.dynamic_index_in_dim(values, rank ^ mask, 0, keepdims=False)
        total = total + hop(part, "tp", mask, count)
    return total


def sent_kernel(place, left, right, out, *, tall):
    if tall:
        out[0] = lax.dot_general(
            left[...], right[...], (((0,), (0,)), ((), ())), preferred_element_type=WIDE
        ).astype(NARROW)
    else:
        turned = right[...].T
        for c in range(left.shape[0]):
            out[0, c] = jnp.dot(turned, left[c], preferred_element_type=WIDE).astype(NARROW)


def kept_kernel(seat, left, right, got, *outs, tall, crossing):
    slots = pl.num_programs(0)
    step = pl.program_id(0)
    if tall:
        total = lax.dot_general(
            left[...], right[...], (((0,), (0,)), ((), ())), preferred_element_type=WIDE
        ) + got[0].astype(WIDE)
        rows = total.shape[0]
    else:
        turned = right[...].T
        total = jnp.stack(
            [
                jnp.dot(turned, left[c], preferred_element_type=WIDE) + got[0, c].astype(WIDE)
                for c in range(left.shape[0])
            ]
        )
        rows = total.shape[1]

    def at(slot):
        return pl.when(step == (slot - 1) % slots)

    @at(0)
    def _():
        outs[0][...] = total

    if crossing:
        cut = rows // 2
        low = total.astype(NARROW)
        first, second = (low[:cut], low[cut:]) if tall else (low[:, :cut], low[:, cut:])
        across, along, keep_first, keep_second = outs[1:]

        @at(1)
        def _():
            across[0] = first
            keep_second[...] = second

        @at(2)
        def _():
            keep_first[...] = first
            along[0] = second

        @at(3)
        def _():
            across[1] = first
            along[1] = second

    else:
        for slot in range(1, len(outs)):

            @at(slot)
            def _():
                outs[slot][...] = total.astype(NARROW)


def gradient_blocks(seat, left, right, count, tall, got=None, crossing=False):
    rows = right.shape[0]
    part = right.shape[1] // count
    slots = count // 2
    if tall:
        block = (left.shape[1], part)
        half = (left.shape[1] // 2, part)
    else:
        block = (left.shape[0], part, left.shape[2])
        half = (left.shape[0], part // 2, left.shape[2])
    first = 0 if got is None else 1
    slot_of = lambda k: (k + first) & (slots - 1)
    left_spec = pl.BlockSpec(left.shape, lambda k, seat: (0,) * left.ndim)
    if part % 128:
        order = 2 * (jnp.arange(slots, dtype=jnp.int32) ^ seat[0]) + seat[1]
        right = right.reshape(rows, count, part)[:, order].transpose(1, 0, 2)
        right_spec = pl.BlockSpec((None, rows, part), lambda k, seat: (slot_of(k), 0, 0))
    else:
        right_spec = pl.BlockSpec(
            (rows, part), lambda k, seat: (0, 2 * (slot_of(k) ^ seat[0]) + seat[1])
        )

    def fixed(shape):
        return pl.BlockSpec(shape, lambda k, seat: (0,) * len(shape))

    block_spec = pl.BlockSpec((1,) + block, lambda k, seat: (slot_of(k),) + (0,) * len(block))
    if got is None:
        shapes = [jax.ShapeDtypeStruct((slots,) + block, NARROW)]
        specs = [block_spec]
    else:
        rest = [(2,) + half, (2,) + half, half, half] if crossing else [block] * (slots - 1)
        shapes = [jax.ShapeDtypeStruct(block, WIDE)]
        shapes += [jax.ShapeDtypeStruct(shape, NARROW) for shape in rest]
        specs = [fixed(shape.shape) for shape in shapes]
    kernel = (
        functools.partial(sent_kernel, tall=tall)
        if got is None
        else functools.partial(kept_kernel, tall=tall, crossing=crossing)
    )
    return pl.pallas_call(
        kernel,
        name="sent" if got is None else "kept",
        grid_spec=pltpu.PrefetchScalarGridSpec(
            num_scalar_prefetch=1,
            grid=(slots,),
            in_specs=[left_spec, right_spec] + ([] if got is None else [block_spec]),
            out_specs=tuple(specs),
        ),
        out_shape=tuple(shapes),
        compiler_params=params(40),
        cost_estimate=SMALL,
    )(seat, left, right, *([] if got is None else [got]))


def send_gradient(left, right, rank, count, tall):
    seat = jnp.stack([rank >> 1, 1 - (rank & 1)])
    return gradient_blocks(seat, left, right, count, tall)[0]


def keep_gradient(left, right, got, rank, count, tall, crossing=False):
    seat = jnp.stack([rank >> 1, rank & 1])
    return gradient_blocks(
        seat, left, right, count, tall, got, crossing=crossing and count == 8
    )


def finish_gradient(pieces, count, arrived=None):
    total = pieces[0]
    if count == 8 and pieces[1].ndim > total.ndim:
        _, across, along, keep_first, keep_second = pieces
        axis = total.ndim - 2
        across = hop(across, "seq", 2, count)
        along = hop(along, "seq", 4, count)
        if arrived is not None:
            arrived += [across, along]
        first = (keep_first.astype(WIDE) + across[1].astype(WIDE)).astype(NARROW)
        second = (keep_second.astype(WIDE) + along[1].astype(WIDE)).astype(NARROW)
        first = hop(first, "seq", 4, count).astype(WIDE) + across[0].astype(WIDE)
        second = hop(second, "seq", 2, count).astype(WIDE) + along[0].astype(WIDE)
        return total + jnp.concatenate([first, second], axis=axis)
    for slot in range(1, len(pieces)):
        total = total + hop(pieces[slot], "seq", 2 * slot, count).astype(WIDE)
    return total


def scalar_spec():
    return pl.BlockSpec(memory_space=pltpu.SMEM)


def full_spec(array):
    return pl.BlockSpec(array.shape, lambda i: (0,) * len(array.shape))


def local_call(kernel, name, scalars, inputs, heavy, outs, scratch, mib):
    return pl.pallas_call(
        kernel,
        name=name,
        grid=(1,),
        out_shape=tuple(outs),
        in_specs=[scalar_spec()] * len(scalars)
        + [full_spec(item) for item in inputs]
        + [pl.BlockSpec(memory_space=pl.ANY)] * len(heavy),
        out_specs=tuple(full_spec(item) for item in outs),
        scratch_shapes=list(scratch),
        compiler_params=params(mib),
        cost_estimate=SMALL,
    )(*scalars, *inputs, *heavy)


def shaped(shape, dtype):
    return jax.ShapeDtypeStruct(tuple(shape), dtype)


SPAN = 256


def span_of(step):
    return pl.ds(pl.multiple_of(step * SPAN, SPAN), SPAN)


def fetch(source, held, sems, step, axis):
    where = (slice(None),) * axis + (span_of(step),)
    return pltpu.make_async_copy(source.at[where], held.at[where], sems.at[step])


def fetch_all(source, held, sems, axis):
    for step in range(source.shape[axis] // SPAN):
        fetch(source, held, sems, step, axis).start()


def params(mib):
    return pltpu.CompilerParams(vmem_limit_bytes=mib * MIB)


def turn_packed(values, straight, crossed):
    lane = lax.broadcasted_iota(jnp.int32, values.shape, 1)
    ahead = pltpu.roll(values, 2 * HD - HD // 2, 1)
    behind = pltpu.roll(values, HD // 2, 1)
    partner = jnp.where((lane & (HD // 2)) == 0, ahead, behind)
    return values * straight + partner * crossed


def rows_at(owner, rows):
    return pl.ds(pl.multiple_of(owner * rows, rows), rows)


def pack_kernel(seat, *refs, parts, heads, merge):
    rows_in = refs[:parts]
    bias, straight, crossed = refs[parts : parts + 3]
    at = parts + 3
    if merge:
        earlier, earlier_rows = refs[at : at + 2]
        at += 2
    weight = refs[at]
    at += 1
    if merge:
        outs, rows_out = refs[at : at + heads], refs[at + heads]
    else:
        out, rows_out = refs[at], refs[at + 1]
    rows, held, kept, sems = refs[-4:]
    fetch_all(weight, kept, sems, 2)
    part = rows_in[0].shape[0]
    half = part // 2
    size = part + half
    for i in range(parts):
        rows[i * part : (i + 1) * part, :] = rows_in[i][...]
    straight, crossed = (
        jnp.concatenate([table[rows_at(seat[1 + i], part), :] for i in range(parts)], axis=0)
        for table in (straight, crossed)
    )
    for step in range(weight.shape[2] // SPAN):
        fetch(weight, kept, sems, step, 2).wait()
        cols = slice(step * SPAN, (step + 1) * SPAN)
        query, key, value = (
            jnp.dot(rows[...], kept[c, :, cols], preferred_element_type=WIDE)
            + bias[c : c + 1, cols]
            for c in range(3)
        )
        for side in range(SPAN // HD):
            lanes = slice(side * HD, (side + 1) * HD)
            head = step * (SPAN // HD) + side
            both = jnp.concatenate([query[:, lanes], key[:, lanes]], axis=1)
            both = turn_packed(both, straight, crossed).astype(NARROW)
            for i in range(parts):
                held[i, head, :part, :] = both[i * part : (i + 1) * part]
                one = value[i * part : (i + 1) * part, lanes]
                held[i, head, part:, :] = jnp.concatenate(
                    [one[:half], one[half:]], axis=1
                ).astype(NARROW)
    if merge:
        for i in range(parts):
            mine = rows_at(seat[1 + i], size)
            other = rows_at(seat[1 + parts + i], size)
            for slot in range(heads):
                outs[slot][mine, :] = held[i, seat[0] ^ slot]
                outs[slot][other, :] = earlier[i, seat[0] ^ slot]
            rows_out[rows_at(seat[1 + i], part), :] = rows[i * part : (i + 1) * part, :]
            rows_out[rows_at(seat[1 + parts + i], part), :] = earlier_rows[
                i * part : (i + 1) * part, :
            ]
    else:
        out[...] = held[...]
        rows_out[...] = rows[...]


def pack_heads(seat, parts, weight, bias, straight, crossed, heads, earlier=()):
    count = len(parts)
    part, depth = parts[0].shape
    size = part + part // 2
    if earlier:
        outs = [shaped((2 * count * size, 2 * HD), NARROW)] * heads
        outs += [shaped((2 * count * part, depth), NARROW)]
    else:
        outs = [shaped((count, heads, size, 2 * HD), NARROW), shaped((count * part, depth), NARROW)]
    return local_call(
        functools.partial(pack_kernel, parts=count, heads=heads, merge=bool(earlier)),
        "pack",
        [seat],
        [*parts, bias, straight, crossed, *earlier],
        [weight],
        outs,
        [
            pltpu.VMEM((count * part, depth), NARROW),
            pltpu.VMEM((count, heads, size, 2 * HD), NARROW),
            pltpu.VMEM(weight.shape, NARROW),
            pltpu.SemaphoreType.DMA((weight.shape[2] // SPAN,)),
        ],
        48,
    )


def split_chunk(chunk):
    block = chunk.shape[0] * 2 // 3
    both = chunk[:block, :]
    packed = chunk[block:, :]
    value = jnp.concatenate([packed[:, :HD], packed[:, HD:]], axis=0)
    return both[:, :HD], both[:, HD:], value


def allowed_mask(begin, q_begin, starts, shape):
    keys = begin + lax.broadcasted_iota(jnp.int32, shape, 0)
    queries = q_begin + lax.broadcasted_iota(jnp.int32, shape, 1)
    return (keys >= starts) & (keys <= queries)


def key_ranges(info, index, first_block, block):
    here = first_block + index
    low = info[2 + 2 * index] // block
    clear = jnp.minimum((info[3 + 2 * index] + block - 1) // block, here)
    return low, clear, here


def forward_kernel(info, starts, *refs, groups, spread, parts):
    count = groups
    chunks = refs[:count]
    at = count + (1 if spread else 0)
    outs = refs[at : at + count]
    mixed, logs, keys, values, queries = refs[at + count :]
    me = info[0]
    first_block = info[1]
    block = starts.shape[2]
    part = block // parts
    size = part + part // 2
    for slot in range(parts * count):
        side = slot // count
        query, key, value = split_chunk(chunks[slot % count][side * size : (side + 1) * size, :])
        place = me ^ (slot % count)
        rows = slice(side * part, (side + 1) * part)
        queries[place, :, rows] = query.T
        if not spread:
            keys[place, rows, :] = key
            values[place, :, rows] = value.T
    if spread:

        @pl.loop(0, keys.shape[0])
        def _(kb):
            for side in range(parts):
                _, key, value = split_chunk(refs[count][kb, side * size : (side + 1) * size, :])
                rows = slice(side * part, (side + 1) * part)
                keys[kb, rows, :] = key
                values[kb, :, rows] = value.T

    @pl.loop(0, count)
    def _(index):
        low, clear, here = key_ranges(info, index, first_block, block)
        query = queries[index]
        begins = starts[index]

        def step(kb, carry, masked):
            top, total, accum = carry
            raw = jnp.dot(keys[kb], query, preferred_element_type=WIDE)
            if masked:
                raw = jnp.where(
                    allowed_mask(kb * block, here * block, begins, raw.shape), raw, OUTSIDE
                )
            fresh = jnp.maximum(top, jnp.max(raw, axis=0, keepdims=True) * (SCALE * LOG2E))
            kept = jnp.exp2(raw * (SCALE * LOG2E) - fresh)
            fade = jnp.exp2(top - fresh)
            total = total * fade + jnp.sum(kept, axis=0, keepdims=True)
            accum = accum * fade + jnp.dot(
                values[kb], kept.astype(NARROW), preferred_element_type=WIDE
            )
            return fresh, total, accum

        carry = (
            jnp.full((1, block), LOWEST, WIDE),
            jnp.zeros((1, block), WIDE),
            jnp.zeros((HD, block), WIDE),
        )
        carry = lax.fori_loop(low, clear, functools.partial(step, masked=True), carry)
        carry = lax.fori_loop(clear, here, functools.partial(step, masked=False), carry)
        top, total, accum = step(here, carry, True)
        mixed[index] = accum / total
        logs[index] = top + jnp.log2(total)

    for slot in range(count):
        outs[slot][...] = mixed[me ^ slot].astype(NARROW)


def attend_forward(info, starts, chunks, everyone, parts):
    count = len(chunks)
    block = starts.shape[2]
    spread = everyone is not None
    blocks = everyone.shape[0] if spread else count
    return local_call(
        functools.partial(forward_kernel, groups=count, spread=spread, parts=parts),
        "forward",
        [info],
        [starts, *chunks] + ([everyone] if spread else []),
        [],
        [shaped((HD, block), NARROW)] * count
        + [shaped((count, HD, block), WIDE), shaped((count, 1, block), WIDE)],
        [
            pltpu.VMEM((blocks, block, HD), NARROW),
            pltpu.VMEM((blocks, HD, block), NARROW),
            pltpu.VMEM((count, HD, block), NARROW),
        ],
        48,
    )


def backward_kernel(info, starts, logs, mixed, *refs, groups, spread, parts):
    count = groups
    chunks = refs[:count]
    grads = refs[count : 2 * count]
    at = 2 * count
    if spread:
        everyone = refs[at]
        at += 1
    outs = refs[at : at + (1 if spread else count)]
    at += len(outs)
    keys, keys_up, values, queries, queries_up, downs, downs_up, key_sum, value_sum, query_sum = refs[at:]
    me = info[0]
    first_block = info[1]
    block = starts.shape[2]
    blocks = keys.shape[0]
    part = block // parts
    half = block // 2
    size = part + part // 2
    for slot in range(parts * count):
        side = slot // count
        query, key, value = split_chunk(chunks[slot % count][side * size : (side + 1) * size, :])
        place = me ^ (slot % count)
        rows = slice(side * part, (side + 1) * part)
        queries[place, rows, :] = query
        queries_up[place, :, rows] = query.T
        if not spread:
            keys[place, rows, :] = key
            keys_up[place, :, rows] = key.T
            values[place, rows, :] = value
    for slot in range(count):
        down = grads[slot][...]
        downs_up[me ^ slot] = down
        downs[me ^ slot] = down.T
    if spread:

        @pl.loop(0, blocks)
        def _(kb):
            for side in range(parts):
                _, key, value = split_chunk(everyone[kb, side * size : (side + 1) * size, :])
                rows = slice(side * part, (side + 1) * part)
                keys[kb, rows, :] = key
                keys_up[kb, :, rows] = key.T
                values[kb, rows, :] = value

    key_sum[...] = jnp.zeros_like(key_sum)
    value_sum[...] = jnp.zeros_like(value_sum)

    @pl.loop(0, count)
    def _(index):
        low, clear, here = key_ranges(info, index, first_block, block)
        query_up = queries_up[index]
        down_up = downs_up[index]
        begins = starts[index]
        log = logs[index]
        delta = jnp.sum(down_up.astype(WIDE) * mixed[index], axis=0, keepdims=True)

        def step(kb, accum, masked):
            raw = jnp.dot(keys[kb], query_up, preferred_element_type=WIDE)
            probs = jnp.exp2(raw * (SCALE * LOG2E) - log)
            if masked:
                probs = jnp.where(
                    allowed_mask(kb * block, here * block, begins, raw.shape), probs, 0.0
                )
            grad_probs = jnp.dot(values[kb], down_up, preferred_element_type=WIDE)
            grad_scores = (probs * (grad_probs - delta)).astype(NARROW)
            value_sum[kb] += jnp.dot(
                probs.astype(NARROW), downs[index], preferred_element_type=WIDE
            )
            key_sum[kb] += jnp.dot(grad_scores, queries[index], preferred_element_type=WIDE)
            return accum + jnp.dot(keys_up[kb], grad_scores, preferred_element_type=WIDE)

        accum = jnp.zeros((HD, block), WIDE)
        accum = lax.fori_loop(low, clear, functools.partial(step, masked=True), accum)
        accum = lax.fori_loop(clear, here, functools.partial(step, masked=False), accum)
        query_sum[index] = step(here, accum, True)

    def packed(kb, query):
        both = jnp.concatenate([query, key_sum[kb]], axis=1) * SCALE
        one = value_sum[kb]
        return both.astype(NARROW), jnp.concatenate([one[:half], one[half:]], axis=1).astype(NARROW)

    if spread:

        @pl.loop(0, blocks)
        def _(kb):
            inside = (kb >= first_block) & (kb < first_block + count)
            query = query_sum[jnp.clip(kb - first_block, 0, count - 1)]
            both, value = packed(kb, jnp.where(inside, query, 0.0).T)
            outs[0][kb, :block, :] = both
            outs[0][kb, block:, :] = value

    else:
        for slot in range(count):
            place = me ^ slot
            both, value = packed(place, query_sum[place].T)
            outs[slot][:block, :] = both
            outs[slot][block:, :] = value


def attend_backward(info, starts, logs, mixed, chunks, grads, everyone, parts):
    count = len(chunks)
    block = starts.shape[2]
    spread = everyone is not None
    blocks = everyone.shape[0] if spread else count
    rows = block + block // 2
    outs = [shaped((blocks, rows, 2 * HD), NARROW)] if spread else [shaped((rows, 2 * HD), NARROW)] * count
    tall = (block, HD)
    flat = (HD, block)
    return local_call(
        functools.partial(backward_kernel, groups=count, spread=spread, parts=parts),
        "backward",
        [info],
        [starts, logs, mixed, *chunks, *grads] + ([everyone] if spread else []),
        [],
        outs,
        [
            pltpu.VMEM((blocks,) + tall, NARROW),
            pltpu.VMEM((blocks,) + flat, NARROW),
            pltpu.VMEM((blocks,) + tall, NARROW),
            pltpu.VMEM((count,) + tall, NARROW),
            pltpu.VMEM((count,) + flat, NARROW),
            pltpu.VMEM((count,) + tall, NARROW),
            pltpu.VMEM((count,) + flat, NARROW),
            pltpu.VMEM((blocks,) + tall, WIDE),
            pltpu.VMEM((blocks,) + tall, WIDE),
            pltpu.VMEM((count,) + flat, WIDE),
        ],
        60,
    )


def join_kernel(place, *refs):
    count = len(refs) - 3
    chunks, out, sums, held = refs[:count], refs[count], refs[count + 1], refs[count + 2]
    me = place[0]
    total = 0.0
    squares = 0.0
    for slot in range(count):
        held[me ^ slot] = chunks[slot][...]
        wide = chunks[slot][...].astype(WIDE)
        total = total + jnp.sum(wide, axis=0, keepdims=True)
        squares = squares + jnp.sum(wide * wide, axis=0, keepdims=True)
    sums[0:1, :] = total
    sums[1:2, :] = squares
    for pair in range(count // 2):
        both = jnp.concatenate([held[2 * pair], held[2 * pair + 1]], axis=0)
        out[:, pair * 2 * HD : (pair + 1) * 2 * HD] = both.T


def join_heads(place, chunks):
    count = len(chunks)
    block = chunks[0].shape[1]
    return local_call(
        join_kernel,
        "join",
        [place],
        chunks,
        [],
        [shaped((block, count * HD), NARROW), shaped((2, block), WIDE)],
        [pltpu.VMEM((count, HD, block), NARROW)],
        16,
    )


def unpack_kernel(place, straight, crossed, *refs):
    count = len(refs) - 3
    chunks, out, sums, held = refs[:count], refs[count], refs[count + 1], refs[count + 2]
    me = place[0]
    block = straight.shape[0]
    for slot in range(count):
        both = turn_packed(chunks[slot][:block, :].astype(WIDE), straight[...], -crossed[...])
        held[me ^ slot, :block, :] = both.astype(NARROW)
        held[me ^ slot, block:, :] = chunks[slot][block:, :]
    for pair in range(count // 2):
        parts = [split_chunk(held[2 * pair + side]) for side in range(2)]
        cols = slice(pair * 2 * HD, (pair + 1) * 2 * HD)
        for c in range(3):
            joined = jnp.concatenate([parts[0][c], parts[1][c]], axis=1)
            out[c, :, cols] = joined
            sums[c : c + 1, cols] = jnp.sum(joined.astype(WIDE), axis=0, keepdims=True)


def unpack_heads(place, straight, crossed, chunks):
    count = len(chunks)
    block = straight.shape[0]
    return local_call(
        unpack_kernel,
        "unpack",
        [place],
        [straight, crossed, *chunks],
        [],
        [shaped((3, block, count * HD), NARROW), shaped((3, count * HD), WIDE)],
        [pltpu.VMEM((count,) + chunks[0].shape, NARROW)],
        24,
    )


def mixed_out_kernel(mixed, gain, bias, *refs, width):
    sums, weight = refs[:-6], refs[-6]
    out, low, stats, kept, sems = refs[-5:]
    fetch_all(weight, kept, sems, 1)
    total = sums[0][...]
    for other in sums[1:]:
        total = total + other[...]
    center = total[0:1] / width
    spread = total[1:2] / width - center * center
    factor = lax.rsqrt(spread + EPSILON)
    stats[...] = jnp.concatenate([center, factor], axis=0)
    columns = jnp.concatenate([center, factor, total, total, total], axis=0).T
    unit = (mixed[...].astype(WIDE) - columns[:, 0:1]) * columns[:, 1:2]
    low[...] = (unit * gain[...] + bias[...]).astype(NARROW)
    for step in range(weight.shape[1] // SPAN):
        cols = slice(step * SPAN, (step + 1) * SPAN)
        fetch(weight, kept, sems, step, 1).wait()
        out[:, cols] = jnp.dot(low[...], kept[:, cols], preferred_element_type=WIDE).astype(NARROW)


def mixed_out_product(mixed, sums, gain, bias, weight):
    rows = mixed.shape[0]
    return local_call(
        functools.partial(mixed_out_kernel, width=weight.shape[1]),
        "mixed_out",
        [],
        [mixed, gain, bias, *sums],
        [weight],
        [shaped((rows, weight.shape[1]), NARROW), shaped(mixed.shape, NARROW), shaped((2, rows), WIDE)],
        [
            pltpu.VMEM(weight.shape, NARROW),
            pltpu.SemaphoreType.DMA((weight.shape[1] // SPAN,)),
        ],
        24,
    )


def fold_lanes(values):
    total = values[:, :128]
    for begin in range(128, values.shape[1], 128):
        total = total + values[:, begin : begin + 128]
    return total


def up_kernel(seat, *refs, parts, merge):
    rows_in = refs[:parts]
    bias, gain, grad = refs[parts : parts + 3]
    earlier = refs[parts + 3 : parts + 5] if merge else ()
    weight, active_out, slope_out, rows_out, stats, rows, sums, kept, sems = refs[-9:]
    fetch_all(weight, kept, sems, 1)
    part = rows_in[0].shape[0]
    own = [slice(i * part, (i + 1) * part) for i in range(parts)]
    for i in range(parts):
        rows[own[i], :] = rows_in[i][...]
    if merge:
        for i in range(parts):
            rows_out[rows_at(seat[i], part), :] = rows_in[i][...]
            rows_out[rows_at(seat[parts + i], part), :] = earlier[0][own[i], :]
    else:
        rows_out[...] = rows[...]
    sums[...] = jnp.zeros_like(sums)

    @pl.loop(0, weight.shape[1] // SPAN)
    def _(step):
        fetch(weight, kept, sems, step, 1).wait()
        cols = span_of(step)
        value = jnp.dot(rows[...], kept[:, cols], preferred_element_type=WIDE) + bias[:, cols]
        below = 0.5 + 0.5 * lax.erf(value * math.sqrt(0.5))
        active = value * below
        slope = below + value * (
            jnp.exp(-0.5 * value * value) * (1.0 / math.sqrt(2.0 * math.pi))
        )
        active_out[:, cols] = active.astype(NARROW)
        slope_out[:, cols] = slope.astype(NARROW)
        back = jnp.concatenate([grad[rows_at(seat[i], part), cols] for i in range(parts)], axis=0)
        scaled = back.astype(WIDE) * gain[:, cols]
        sums[0] += fold_lanes(active)
        sums[1] += fold_lanes(active * active)
        sums[2] += fold_lanes(scaled)
        sums[3] += fold_lanes(scaled * active)

    lines = jnp.concatenate([jnp.sum(sums[i].T, axis=0, keepdims=True) for i in range(4)], axis=0)
    if merge:
        for i in range(parts):
            stats[:, rows_at(seat[i], part)] = lines[:, own[i]]
            stats[:, rows_at(seat[parts + i], part)] = earlier[1][:, own[i]]
    else:
        stats[...] = lines


def up_product(seat, parts, weight, bias, gain, grad, earlier=()):
    count = len(parts)
    rows = count * parts[0].shape[0]
    depth, width = weight.shape
    both = rows * (2 if earlier else 1)
    return local_call(
        functools.partial(up_kernel, parts=count, merge=bool(earlier)),
        "up",
        [seat],
        [*parts, bias, gain, grad, *earlier],
        [weight],
        [
            shaped((rows, width), NARROW),
            shaped((rows, width), NARROW),
            shaped((both, depth), NARROW),
            shaped((4, both), WIDE),
        ],
        [
            pltpu.VMEM((rows, depth), NARROW),
            pltpu.VMEM((4, rows, 128), WIDE),
            pltpu.VMEM(weight.shape, NARROW),
            pltpu.SemaphoreType.DMA((width // SPAN,)),
        ],
        48,
    )


def ffn_back_kernel(seat, *refs, count, parts, width):
    sums = refs[:count]
    halves = refs[count : count + 2], refs[count + 2 : count + 4]
    grad, gain, shift, weight = refs[count + 4 : count + 8]
    hidden_out, grad_out, product, lines, columns, total, kept, sems = refs[count + 8 :]
    fetch_all(weight, kept, sems, 1)
    part = grad.shape[0] // parts
    whole = sums[0][...]
    for other in sums[1:]:
        whole = whole + other[...]
    whole = whole / width
    center, square, lean, cross = (whole[i : i + 1] for i in range(4))
    factor = lax.rsqrt(square - center * center + EPSILON)
    cross = (cross - center * lean) * factor
    columns[...] = jnp.concatenate([center, factor, lean, cross, whole], axis=0).T
    total[...] = jnp.zeros_like(total)

    @pl.loop(0, weight.shape[1] // SPAN)
    def _(step):
        cols = span_of(step)
        line = [0.0, 0.0, 0.0]
        grads = []
        for i in range(parts):
            active, slope = halves[i // (parts // 2)]
            own = i % (parts // 2)
            own = slice(own * part, (own + 1) * part)
            rows = rows_at(seat[i], part)
            center, factor, lean, cross = (columns[rows, k : k + 1] for k in range(4))
            unit = (active[own, cols].astype(WIDE) - center) * factor
            hidden_out[rows, cols] = (unit * gain[:, cols] + shift[:, cols]).astype(NARROW)
            back = grad[rows, cols].astype(WIDE)
            grad_active = (back * gain[:, cols] - lean - unit * cross) * factor
            grad_up = (grad_active * slope[own, cols].astype(WIDE)).astype(NARROW)
            grad_out[rows, cols] = grad_up
            grads.append(grad_up)
            line[0] = line[0] + jnp.sum(grad_up.astype(WIDE), axis=0, keepdims=True)
            line[1] = line[1] + jnp.sum(back * unit, axis=0, keepdims=True)
            line[2] = line[2] + jnp.sum(back, axis=0, keepdims=True)
        lines[:, cols] = jnp.concatenate(line, axis=0)
        fetch(weight, kept, sems, step, 1).wait()
        total[...] += lax.dot_general(
            jnp.concatenate(grads, axis=0),
            kept[:, cols],
            (((1,), (1,)), ((), ())),
            preferred_element_type=WIDE,
        )

    for i in range(parts):
        product[rows_at(seat[i], part), :] = total[i * part : (i + 1) * part, :].astype(NARROW)


def ffn_back_product(seat, sums, near, far, grad, gain, shift, weight, width):
    rows, local = grad.shape
    depth = weight.shape[0]
    both = shaped((rows, local), NARROW)
    return local_call(
        functools.partial(
            ffn_back_kernel, count=len(sums), parts=seat.shape[0], width=width
        ),
        "ffn_back",
        [seat],
        [*sums, *near, *far, grad, gain, shift],
        [weight],
        [both, both, shaped((rows, depth), NARROW), shaped((3, local), WIDE)],
        [
            pltpu.VMEM((rows, 8), WIDE),
            pltpu.VMEM((rows, depth), WIDE),
            pltpu.VMEM(weight.shape, NARROW),
            pltpu.SemaphoreType.DMA((local // SPAN,)),
        ],
        56,
    )


def mixed_back_kernel(seat, *refs, parts):
    mixed, stats, gain, weight, grad, rows, sums, lines, kept, sem = refs[parts:]
    copy = pltpu.make_async_copy(weight, kept, sem)
    copy.start()
    part = refs[0].shape[0]
    for i in range(parts):
        rows[rows_at(seat[i], part), :] = refs[i][...]
    columns = jnp.concatenate([stats[...]] * 4, axis=0).T
    unit = (mixed[...].astype(WIDE) - columns[:, 0:1]) * columns[:, 1:2]
    copy.wait()
    back = lax.dot_general(
        rows[...], kept[...], (((1,), (1,)), ((), ())), preferred_element_type=WIDE
    )
    grad[...] = back
    lines[0:1, :] = jnp.sum(back * unit, axis=0, keepdims=True)
    lines[1:2, :] = jnp.sum(back, axis=0, keepdims=True)
    scaled = back * gain[...]
    sums[0:1, :] = jnp.sum(fold_lanes(scaled).T, axis=0, keepdims=True)
    sums[1:2, :] = jnp.sum(fold_lanes(scaled * unit).T, axis=0, keepdims=True)


def mixed_back_product(seat, parts, mixed, stats, gain, weight):
    rows, local = mixed.shape
    return local_call(
        functools.partial(mixed_back_kernel, parts=len(parts)),
        "mixed_back",
        [seat],
        [*parts, mixed, stats, gain],
        [weight],
        [
            shaped((rows, local), WIDE),
            shaped((rows, weight.shape[1]), NARROW),
            shaped((2, rows), WIDE),
            shaped((2, local), WIDE),
        ],
        [pltpu.VMEM(weight.shape, NARROW), pltpu.SemaphoreType.DMA],
        24,
    )


def cut_kernel(seat, grad, mixed, stats, gain, *refs, count, width):
    sums = refs[:count]
    outs, held = refs[count:-1], refs[-1]
    total = sums[0][...]
    for other in sums[1:]:
        total = total + other[...]
    total = total / width
    columns = jnp.concatenate([stats[...], total] * 2, axis=0).T
    factor = columns[:, 1:2]
    unit = (mixed[...].astype(WIDE) - columns[:, 0:1]) * factor
    result = (grad[...] * gain[...] - columns[:, 2:3] - unit * columns[:, 3:4]) * factor
    result = result.astype(NARROW)
    heads = len(outs)
    for pair in range(heads // 2):
        both = result[:, pair * 2 * HD : (pair + 1) * 2 * HD].T
        held[2 * pair] = both[:HD]
        held[2 * pair + 1] = both[HD:]
    for slot in range(heads):
        outs[slot][...] = held[seat[0] ^ slot]


def cut_heads(seat, grad, mixed, stats, gain, sums, heads, width):
    block = grad.shape[0]
    return local_call(
        functools.partial(cut_kernel, count=len(sums), width=width),
        "cut",
        [seat],
        [grad, mixed, stats, gain, *sums],
        [],
        [shaped((HD, block), NARROW)] * heads,
        [pltpu.VMEM((heads, HD, block), NARROW)],
        16,
    )


def attn_back_kernel(grads, rows, gain, bias, weight, product, lines, kept, sems):
    fetch_all(weight, kept, sems, 1)

    @pl.loop(0, product.shape[1] // SPAN)
    def _(step):
        cols = span_of(step)
        fetch(weight, kept, sems, step, 1).wait()
        total = 0.0
        for c in range(grads.shape[0]):
            total = total + lax.dot_general(
                grads[c], kept[c, cols, :], (((1,), (1,)), ((), ())), preferred_element_type=WIDE
            )
        product[:, cols] = total.astype(NARROW)
        unit = (rows[:, cols].astype(WIDE) - bias[:, cols]) / gain[:, cols]
        lines[0:1, cols] = jnp.sum(total * unit, axis=0, keepdims=True)
        lines[1:2, cols] = jnp.sum(total, axis=0, keepdims=True)


def attn_back_product(grads, rows, gain, bias, weight):
    count, depth = rows.shape
    return local_call(
        attn_back_kernel,
        "attn_back",
        [],
        [grads, rows, gain, bias],
        [weight],
        [shaped((count, depth), NARROW), shaped((2, depth), WIDE)],
        [
            pltpu.VMEM(weight.shape, NARROW),
            pltpu.SemaphoreType.DMA((depth // SPAN,)),
        ],
        32,
    )


def shards(
    inputs,
    segment_ids,
    cotangent,
    qkv_weight,
    qkv_bias,
    out_weight,
    out_bias,
    up_weight,
    up_bias,
    down_weight,
    down_bias,
    input_gain,
    input_bias,
    mixed_gain,
    mixed_bias,
    middle_gain,
    middle_bias,
    hidden_gain,
    hidden_bias,
    qkv_average,
    out_average,
    up_average,
    down_average,
    decay_rate,
):
    seq_count = lax.axis_size("seq")
    seq_rank = lax.axis_index("seq")
    local_rows = segment_ids.shape[0]
    model_width = inputs.shape[1]
    local_width = qkv_weight.shape[2]
    heads_here = local_width // HD
    team = heads_here
    teams = seq_count // team
    place = seq_rank % team
    home = seq_rank - place

    def trade(chunks):
        return [chunks[0]] + [hop(chunks[m], "seq", m, seq_count) for m in range(1, team)]

    row_index = seq_rank * local_rows + jnp.arange(local_rows, dtype=jnp.int32)
    documents = jnp.arange(COUNT, dtype=jnp.int32)
    member = segment_ids[:, None] == documents[None, :]
    first_all = jnp.min(jnp.where(member, row_index[:, None], LARGEST), axis=0)
    bit = 1
    while bit < seq_count:
        first_all = jnp.minimum(first_all, hop(first_all, "seq", bit, seq_count))
        bit *= 2

    def starts_of(rows):
        earlier = first_all[None, :] <= rows[:, None]
        return jnp.max(jnp.where(earlier, first_all[None, :], 0), axis=1)

    cosine, sine, growth = xpos_tables(row_index - starts_of(row_index), HD)
    shrink = 1.0 / growth
    straight = jnp.concatenate([cosine * growth] * 2 + [cosine * shrink] * 2, axis=1)
    crossed = jnp.concatenate(
        [-sine * growth, sine * growth, -sine * shrink, sine * shrink], axis=1
    )
    team_rows = home * local_rows + jnp.arange(team * local_rows, dtype=jnp.int32)
    team_starts = starts_of(team_rows).reshape(team, local_rows)
    spans = jnp.stack([jnp.min(team_starts, axis=1), jnp.max(team_starts, axis=1)], axis=1)
    info = jnp.concatenate(
        [jnp.stack([place, home]).astype(jnp.int32), spans.reshape(-1)]
    )
    team_starts = team_starts.reshape(team, 1, local_rows)
    seat = jnp.reshape(place, (1,)).astype(jnp.int32)

    tp_count = lax.axis_size("tp")
    tp_rank = lax.axis_index("tp")
    inner = tp_count // 2
    owners = part_owners()
    near_first = owners[:inner] + owners[inner:]
    far_first = owners[inner:] + owners[:inner]

    def line(vector):
        return vector.astype(WIDE).reshape(1, -1)

    def exchange(values):
        mask = 1
        while 2 * mask < tp_count:
            values = values + hop(values, "tp", mask, tp_count)
            mask *= 2
        return [values, hop(values, "tp", mask, tp_count)]

    inputs_wide = inputs.astype(WIDE)
    input_normed, input_back = jax.vjp(
        norm_rows, inputs_wide, input_gain.astype(WIDE), input_bias.astype(WIDE)
    )
    attn_parts = gather_parts(input_normed.astype(NARROW))
    rate = decay_rate[0]
    seq_part = model_width // seq_count
    offset = seq_rank * seq_part

    def average(old, weight, axis):
        piece = lax.dynamic_slice_in_dim(weight, offset, seq_part, axis).astype(WIDE)
        return rate * old + (1.0 - rate) * piece

    qkv_new = average(qkv_average, qkv_weight, 1)
    out_new = average(out_average, out_weight, 1)
    up_new = average(up_average, up_weight, 0)
    down_new = average(down_average, down_weight, 1)
    attn_parts[0] = after(attn_parts[0], straight, crossed)

    def pack(parts, chairs, earlier=()):
        chair = jnp.stack([place.astype(jnp.int32)] + chairs)
        return pack_heads(
            chair, parts, qkv_weight, qkv_bias.astype(WIDE), straight, crossed, team, earlier
        )

    packed = pack(attn_parts[:inner], near_first)
    attn_parts[inner] = after(attn_parts[inner], *packed)
    *packs, attn_in = pack(attn_parts[inner:], far_first, packed)
    grad_rows = gather_rows(after(cotangent, packs[0]))
    chunks = trade(packs)
    everyone = None
    if teams > 1:
        rings = [[j + team * t for t in range(teams)] for j in range(team)]
        natural = jnp.stack(chunks)[jnp.arange(team) ^ place]
        everyone = lax.all_gather(
            natural, "seq", axis=0, tiled=True, axis_index_groups=rings
        )
    *mixed_out, mixed_wide, logs = attend_forward(info, team_starts, chunks, everyone, tp_count)
    mixed_got = trade(mixed_out)

    mixed_got[0] = after(mixed_got[0], grad_rows)
    mixed, mixed_sums = join_heads(seat, mixed_got)
    out_product, mixed_low, mixed_stats = mixed_out_product(
        mixed, exchange(mixed_sums), line(mixed_gain), line(mixed_bias), out_weight
    )
    grad_hidden = jnp.einsum(
        "rd,fd->rf", grad_rows, down_weight, preferred_element_type=WIDE
    ).astype(NARROW)
    summed = after(scatter_rows(out_product), grad_hidden, qkv_new, out_new, up_new, down_new)
    middle = inputs_wide + summed + out_bias.astype(WIDE)
    normed, middle_back = jax.vjp(
        norm_rows, middle, middle_gain.astype(WIDE), middle_bias.astype(WIDE)
    )
    ffn_parts = gather_parts(normed.astype(NARROW))
    gain_line = line(hidden_gain)

    def up(parts, chairs, earlier=()):
        return up_product(
            jnp.stack(chairs), parts, up_weight, line(up_bias), gain_line, grad_hidden, earlier
        )

    *up_near, ffn_near, sums_near = up(ffn_parts[:inner], near_first)
    ffn_parts[inner] = after(ffn_parts[inner], sums_near)
    *up_far, ffn_in, sums = up(ffn_parts[inner:], far_first, (ffn_near, sums_near))
    hidden_low, grad_up, ffn_back, hidden_lines = ffn_back_product(
        jnp.stack(owners),
        exchange(sums),
        up_near,
        up_far,
        grad_hidden,
        gain_line,
        line(hidden_bias),
        up_weight,
        FF,
    )
    upbias_part, hiddengain_part, hiddenbias_part = hidden_lines
    down_product = jnp.dot(hidden_low, down_weight, preferred_element_type=WIDE).astype(NARROW)
    late_rows = after(grad_rows, down_product)
    down_sent = send_gradient(hidden_low, late_rows, seq_rank, seq_count, True)
    up_sent = send_gradient(after(grad_up, down_product)[None], ffn_in, seq_rank, seq_count, False)
    summed = after(scatter_rows(ffn_back), down_sent, up_sent)
    norm_grad, middlegain_part, middlebias_part = middle_back(summed)
    grad_middle = cotangent.astype(WIDE) + norm_grad
    grad_low = grad_middle.astype(NARROW)
    middle_parts = gather_parts(grad_low)
    down_got = after(hop(down_sent, "seq", 1, seq_count), grad_low)
    up_got = hop(up_sent, "seq", 1, seq_count)
    down_pieces = keep_gradient(hidden_low, grad_rows, down_got, seq_rank, seq_count, True, True)
    up_pieces = keep_gradient(grad_up[None], ffn_in, up_got, seq_rank, seq_count, False)
    arrived = []
    down_grad = finish_gradient(down_pieces, seq_count, arrived)
    middle_parts[-1] = after(middle_parts[-1], *up_pieces, *arrived)
    outbias_part = jnp.sum(grad_low, axis=0, dtype=WIDE)
    downbias_part = jnp.sum(cotangent, axis=0, dtype=WIDE)
    grad_mixed_norm, grad_mixed_rows, back_sums, mixed_lines = mixed_back_product(
        jnp.stack(owners),
        middle_parts,
        mixed,
        mixed_stats,
        line(mixed_gain),
        out_weight,
    )
    mixedgain_part, mixedbias_part = mixed_lines
    grad_cuts = cut_heads(
        seat,
        grad_mixed_norm,
        mixed,
        mixed_stats,
        line(mixed_gain),
        exchange(back_sums),
        team,
        model_width,
    )
    grad_cuts = list(grad_cuts)
    grad_cuts[0] = after(grad_cuts[0], down_grad)
    grad_chunks = trade(grad_cuts)
    up_pieces = list(up_pieces)
    for slot in range(1, len(up_pieces)):
        up_pieces[slot] = after(up_pieces[slot], *grad_chunks)
    up_grad = finish_gradient(up_pieces, seq_count)[0]
    layer_out = (
        middle
        + scatter_rows(after(down_product, grad_mixed_norm))
        + down_bias.astype(WIDE)
    ).astype(NARROW)
    out_sent = send_gradient(mixed_low, grad_mixed_rows, seq_rank, seq_count, True)
    out_got = hop(out_sent, "seq", 1, seq_count)
    out_pieces = keep_gradient(mixed_low, grad_mixed_rows, out_got, seq_rank, seq_count, True)
    grad_chunks[0] = after(grad_chunks[0], *out_pieces)
    pieces = attend_backward(
        info,
        team_starts,
        logs,
        mixed_wide,
        chunks,
        grad_chunks,
        everyone,
        tp_count,
    )
    pieces = list(pieces)
    pieces[0] = after(pieces[0], layer_out, up_grad)
    if teams > 1:
        natural = lax.psum_scatter(
            pieces[0], "seq", scatter_dimension=0, tiled=True, axis_index_groups=rings
        )
        pieces = [
            lax.dynamic_index_in_dim(natural, place ^ m, 0, keepdims=False) for m in range(team)
        ]
    parts_got = trade(pieces)
    out_pieces = list(out_pieces)
    for slot in range(1, len(out_pieces)):
        out_pieces[slot] = after(out_pieces[slot], *parts_got)
    out_grad = finish_gradient(out_pieces, seq_count)
    stacked, qkvbias_part = unpack_heads(seat, straight, crossed, parts_got)
    qkv_got = hop(send_gradient(stacked, attn_in, seq_rank, seq_count, False), "seq", 1, seq_count)
    attn_back, attn_lines = attn_back_product(
        stacked, attn_in, line(input_gain), line(input_bias), qkv_weight
    )
    inputgain_part, inputbias_part = attn_lines
    grad_attn_in = scatter_rows(attn_back)
    qkv_pieces = keep_gradient(stacked, attn_in, qkv_got, seq_rank, seq_count, False, True)
    arrived = []
    qkv_grad = finish_gradient(qkv_pieces, seq_count, arrived)

    def spread_norms(parts):
        both = jnp.stack(parts).reshape(len(parts), seq_count, tp_count, -1)
        mine = tp_scatter(both.transpose(2, 1, 0, 3))
        return mine.reshape(seq_count, -1)

    vectors = jnp.concatenate(
        [
            item.reshape(seq_count, -1)
            for item in (
                upbias_part,
                hiddengain_part,
                hiddenbias_part,
                mixedgain_part,
                mixedbias_part,
                qkvbias_part[0],
                qkvbias_part[1],
                qkvbias_part[2],
            )
        ]
        + [
            spread_norms(
                [
                    middlegain_part,
                    middlebias_part,
                    outbias_part,
                    downbias_part,
                    inputgain_part,
                    inputbias_part,
                ]
            )
        ],
        axis=1,
    )
    vector_sums = vector_scatter(after(vectors, *arrived), seq_rank, seq_count)
    grad_attn_in = after(grad_attn_in, vector_sums)
    grad_input_norm, _, _ = input_back(grad_attn_in)
    input_grad = (grad_middle + grad_input_norm).astype(NARROW)
    narrow_part = local_width // seq_count
    wide_part = up_bias.shape[0] // seq_count
    norm_part = model_width // (seq_count * lax.axis_size("tp"))

    def cuts(vector, widths):
        begin = 0
        pieces = []
        for width in widths:
            pieces.append(vector[begin : begin + width])
            begin += width
        return pieces

    (
        upbias_grad,
        hiddengain_grad,
        hiddenbias_grad,
        mixedgain_grad,
        mixedbias_grad,
        q_bias,
        k_bias,
        v_bias,
        middlegain_grad,
        middlebias_grad,
        outbias_grad,
        downbias_grad,
        inputgain_grad,
        inputbias_grad,
    ) = cuts(vector_sums, (wide_part,) * 3 + (narrow_part,) * 5 + (norm_part,) * 6)
    return (
        layer_out,
        input_grad,
        qkv_grad,
        jnp.stack([q_bias, k_bias, v_bias]),
        out_grad,
        outbias_grad,
        up_grad,
        upbias_grad,
        down_grad,
        downbias_grad,
        inputgain_grad,
        inputbias_grad,
        mixedgain_grad,
        mixedbias_grad,
        middlegain_grad,
        middlebias_grad,
        hiddengain_grad,
        hiddenbias_grad,
        qkv_new,
        out_new,
        up_new,
        down_new,
    )


def solution(mesh):
    in_specs = (
        P(("seq", "tp"), None),
        P("seq"),
        P(("seq", "tp"), None),
        P(None, None, "tp"),
        P(None, "tp"),
        P("tp", None),
        P(),
        P(None, "tp"),
        P("tp"),
        P("tp", None),
        P(),
        P(),
        P(),
        P("tp"),
        P("tp"),
        P(),
        P(),
        P("tp"),
        P("tp"),
        P(None, "seq", "tp"),
        P("tp", "seq"),
        P("seq", "tp"),
        P("tp", "seq"),
        P(),
    )
    out_specs = (
        P(("seq", "tp"), None),
        P(("seq", "tp"), None),
        P(None, "seq", "tp"),
        P(None, ("tp", "seq")),
        P("tp", "seq"),
        P(("seq", "tp")),
        P("seq", "tp"),
        P(("tp", "seq")),
        P("tp", "seq"),
        P(("seq", "tp")),
        P(("seq", "tp")),
        P(("seq", "tp")),
        P(("tp", "seq")),
        P(("tp", "seq")),
        P(("seq", "tp")),
        P(("seq", "tp")),
        P(("tp", "seq")),
        P(("tp", "seq")),
        P(None, "seq", "tp"),
        P("tp", "seq"),
        P("seq", "tp"),
        P("tp", "seq"),
    )
    return jax.shard_map(shards, mesh=mesh, in_specs=in_specs, out_specs=out_specs, check_vma=False)
```

time: 671 us -> 572 us (0.85)
  waiting for transfers between devices: 300 us -> 178 us
  Pallas kernels: 111 us -> 165 us
  matrix products: 61.8 us -> 19 us
  local copies, waits for them, and re-layouts: 38.7 us -> 56.2 us
    all_gather x4 -> x1, waiting for transfers between devices: 82.5 us -> 0.01 us  [gather_rows(): return lax.all_gather(values, 'tp', axis=0, tiled=True)]
    ppermute x72 -> x61, waiting for transfers between devices: 139 us -> 71.8 us  [hop(): return lax.ppermute(values, axis, [(i, i ^ mask) for i in range(count)])]
    ppermute x0 -> x9, waiting for transfers between devices: none -> 66.1 us  [gather_parts(): parts.append(lax.ppermute(parts[-1], 'tp', pairs))]
    pallas_call x14 -> x21, Pallas kernels: 111 us -> 165 us  [the longest x13 126 us: local_call(): pl.pallas_call(kernel, name=name, grid=(1,), out_shape=tuple(outs), in_sp...]
    dot_general x6 -> x1, matrix products: 52.3 us -> 9.87 us  [shards(): jnp.dot(hidden_low, down_weight, preferred_element_type=WIDE).astype(NARROW)]
    reduce_scatter x4, waiting for transfers between devices: 78.3 us -> 39.8 us  [scatter_rows(): lax.psum_scatter(values.astype(NARROW), 'tp', scatter_dimension=0, tiled=...]
    unnamed x152 -> x248, local copies, waits for them, and re-layouts: 21.8 us -> 45.4 us
    ppermute x72 -> x61, starting transfers between devices: 72.3 us -> 60.3 us  [hop(): return lax.ppermute(values, axis, [(i, i ^ mask) for i in range(count)])]
  transfers between devices with their start and end apart: 80 -> 75, of which waited for: 38 -> 39; matrix products, arithmetic and copies ran while one was open for 14% -> 14% of each run, Pallas kernels for 16% -> 21%
where the time goes in v2:
time: 572 us; the launch traced here: 564 us
  waiting for transfers between devices  178 us (31%)
  Pallas kernels  165 us (29%)
  starting transfers between devices  68.6 us (12%)
  other arithmetic  58.7 us (10%)
  local copies, waits for them, and re-layouts  56.2 us (10%)
  matrix products  19 us (3%)
  between operations  18.6 us (3%)
    pallas_call x13, Pallas kernels, local_call(): pl.pallas_call(kernel, name=name, grid=(1,), out_shape=tuple(outs), in_sp...  126 us
    ppermute x61, waiting for transfers between devices, hop(): return lax.ppermute(values, axis, [(i, i ^ mask) for i in range(count)])  71.8 us
    ppermute x9, waiting for transfers between devices, gather_parts(): parts.append(lax.ppermute(parts[-1], 'tp', pairs))  66.1 us
    ppermute x61, starting transfers between devices, hop(): return lax.ppermute(values, axis, [(i, i ^ mask) for i in range(count)])  60.3 us
    unnamed x248, local copies, waits for them, and re-layouts  45.4 us
    reduce_scatter x4, waiting for transfers between devices, scatter_rows(): lax.psum_scatter(values.astype(NARROW), 'tp', scatter_dimension=0, tiled=...  39.8 us
    pallas_call x8, Pallas kernels, gradient_blocks(): pl.pallas_call(kernel, name='sent' if got is None else 'kept', grid_spec=...  39.2 us
  transfers between devices with their start and end apart: 75, of which 39 were waited for; matrix products, arithmetic and copies ran while one was open for 14% of the time, Pallas kernels for 21%

profile of v2, /device:TPU:0, one launch (start us, length us, event | category | flops | bytes accessed | tf_op | source)
XLA Modules:
  0.0 564.1 jit_solution(8014631176744704364)
XLA Ops:
  15.0 12.9 %collective-permute-done.3.refs_1_ = bf16[128,2048]{1,0:T(8,128)(2,1)S(1)} collective-permute-done((bf16[128,2048]{1,0:T(8,128)(2,1)S(1)}, bf16[128,2048]{1,0:T(8,128)(2,1)S(1)}, u32[]{:S(2)}, u32[]{:S(2)}) %collective-permute-start.3) | collective-permute-done | bytes 524320 | tf_op jit(solution)/shard_map/ppermute | solution.py:61
  50.7 5.3 pack.2
  59.5 6.6 %pack.3 = (bf16[768,128]{1,0:T(8,128)(2,1)S(1)}, bf16[768,128]{1,0:T(8,128)(2,1)S(1)}, bf16[768,128]{1,0:T(8,128)(2,1)S(1)}, bf16[768,128]{1,0:T(8,128)(2,1)S(1)...) custom-call(s32[5]{0:T(128)S(1)} %stack.45.seat, ...), custom_call_target="tpu_custom_call" | custom-call | flops 1048576 | bytes 65536 | tf_op jit(solution)/shard_map/pack/pallas_call | solution.py:278
  75.3 10.9 %collective-permute-done.10.refs_5_ = bf16[768,128]{1,0:T(8,128)(2,1)S(1)} collective-permute-done((bf16[768,128]{1,0:T(8,128)(2,1)}, bf16[768,128]{1,0:T(8,128)(2,1)S(1)}, u32[]{:S(2)}, u32[]{:S(2)}) %collective-permute-start.10) | collective-permute-done | bytes 196640 | tf_op jit(solution)/shard_map/ppermute | solution.py:78
  87.9 5.4 collective-permute-done.8.refs_3_
  95.0 29.4 %forward.1 = (bf16[64,512]{1,0:T(8,128)(2,1)S(1)}, bf16[64,512]{1,0:T(8,128)(2,1)S(1)}, bf16[64,512]{1,0:T(8,128)(2,1)S(1)}, bf16[64,512]{1,0:T(8,128)(2,1)}, bf...) custom-call(s32[18]{0:T(128)S(1)} %pad_add_fusion.1.info, ...), custom_call_target="tpu_custom_call" | custom-call | flops 1048576 | bytes 65536 | tf_op jit(solution)/shard_map/forward/pallas_call | solution.py:278
  155.0 4.4 mixed_out.1
  176.4 9.1 %convolution_convert_fusion.1.refs_4_.refs_6_ = bf16[512,2048]{1,0:T(8,128)(2,1)} fusion(bf16[512,2048]{1,0:T(8,128)(2,1)S(1)} %copy-done.7, bf16[2048,2048]{1,0:T(8,128)(2,1)} %param.35), kind=kOutput, calls=%fused_computation.1 | convolution fusion | flops 4296015872 | bytes 12582912 | tf_op jit(solution)/shard_map/rd,fd->rf/dot_general | solution.py:1153
  185.5 19.9 %reduce-scatter.5.cloned.1.call-done = bf16[128,2048]{1,0:T(8,128)(2,1)} async-done(((bf16[512,2048]{1,0:T(8,128)(2,1)}), bf16[128,2048]{1,0:T(8,128)(2,1)}) %reduce-scatter.5.cloned.1.call-update) | async-done | bytes 524304 | tf_op jit(solution)/shard_map/reduce_scatter | solution.py:74
  208.3 14.4 %collective-permute-done.22.refs_1_ = bf16[128,2048]{1,0:T(8,128)(2,1)S(1)} collective-permute-done((bf16[128,2048]{1,0:T(8,128)(2,1)S(1)}, bf16[128,2048]{1,0:T(8,128)(2,1)S(1)}, u32[]{:S(2)}, u32[]{:S(2)}) %collective-permute-start.22) | collective-permute-done | bytes 524320 | tf_op jit(solution)/shard_map/ppermute | solution.py:61
  222.7 13.5 %collective-permute-done.23.refs_0_ = bf16[128,2048]{1,0:T(8,128)(2,1)S(1)} collective-permute-done((bf16[128,2048]{1,0:T(8,128)(2,1)S(1)}, bf16[128,2048]{1,0:T(8,128)(2,1)S(1)}, u32[]{:S(2)}, u32[]{:S(2)}) %collective-permute-start.23) | collective-permute-done | bytes 524320 | tf_op jit(solution)/shard_map/ppermute | solution.py:61
  241.9 7.9 %up.2 = (bf16[256,2048]{1,0:T(8,128)(2,1)S(1)}, bf16[256,2048]{1,0:T(8,128)(2,1)S(1)}, bf16[256,2048]{1,0:T(8,128)(2,1)S(1)}, f32[4,256]{1,0:T(4,128)S(1)}) custom-call(s32[4]{0:T(128)S(1)} %pad_add_fusion.2.seat, bf16[128,2048]{1,0:T(8,128)(2,1)S(1)} %add_convert_fusion.1.refs_0_, bf16[128,2048]{1,0:T(8,128)(2,1)S(1)} %collective-permute-done.22.refs_1_, ...), custom_call_target="tpu_custom_call" | custom-call | flops 1048576 | bytes 65536 | tf_op jit(solution)/shard_map/up/pallas_call | solution.py:278
  251.9 8.4 %up.3 = (bf16[256,2048]{1,0:T(8,128)(2,1)S(1)}, bf16[256,2048]{1,0:T(8,128)(2,1)S(1)}, bf16[512,2048]{1,0:T(8,128)(2,1)}, f32[4,512]{1,0:T(4,128)S(1)}) custom-call(s32[4]{0:T(128)S(1)} %pad_add_fusion.3.seat, bf16[128,2048]{1,0:T(8,128)(2,1)S(1)} %collective-permute-done.23.refs_0_, bf16[128,2048]{1,0:T(8,128)(2,1)S(1)} %collective-permute-done.24.refs_1_, ...), custom_call_target="tpu_custom_call" | custom-call | flops 1048576 | bytes 65536 | tf_op jit(solution)/shard_map/up/pallas_call | solution.py:278
  271.8 16.0 %ffn_back.1 = (bf16[512,2048]{1,0:T(8,128)(2,1)}, bf16[512,2048]{1,0:T(8,128)(2,1)}, bf16[512,2048]{1,0:T(8,128)(2,1)}, f32[3,2048]{1,0:T(4,128)}) custom-call(s32[4]{0:T(128)} %copy-done.72, f32[4,512]{1,0:T(4,128)} %copy-done.110, f32[4,512]{1,0:T(4,128)} %copy-done.114, bf16[256,2048]{1,0:T(8,128)(2,1)} %copy-done.26, bf16[256,2048]{1,0:T(8,128)(2,1)} %copy-done.27, ...), custom_call_target="tpu_custom_call" | custom-call | flops 1048576 | bytes 65536 | tf_op jit(solution)/shard_map/ffn_back/pallas_call | solution.py:278
  288.0 9.9 %convolution_convert_fusion = bf16[512,2048]{1,0:T(8,128)(2,1)} fusion(bf16[512,2048]{1,0:T(8,128)(2,1)} %get-tuple-element.158.left, bf16[2048,2048]{1,0:T(8,128)(2,1)} %param.35), kind=kOutput, calls=%fused_computation | convolution fusion | flops 4296015872 | bytes 12582912 | tf_op jit(solution)/shard_map/dot_general | solution.py:1184
  301.1 5.1 sent.4
  306.1 5.0 sent.5
  311.6 19.9 %reduce-scatter.7.cloned.1.call-done = bf16[128,2048]{1,0:T(8,128)(2,1)} async-done(((bf16[512,2048]{1,0:T(8,128)(2,1)}), bf16[128,2048]{1,0:T(8,128)(2,1)}) %reduce-scatter.7.cloned.1.call-update) | async-done | bytes 524304 | tf_op jit(solution)/shard_map/reduce_scatter | solution.py:74
  336.6 6.3 %kept.5 = (f32[2048,256]{1,0:T(8,128)S(1)}, bf16[2,1024,256]{2,1,0:T(8,128)(2,1)S(1)}, bf16[2,1024,256]{2,1,0:T(8,128)(2,1)S(1)}, bf16[1024,256]{1,0:T(8,128)(2,1)S(1)}, bf16[1024,256]{1,0:T(8,128)(2,1)S(1)}) custom-call(s32[2]{0:T(128)S(1)} %pad_add_fusion.5.seat, bf16[512,2048]{1,0:T(8,128)(2,1)S(1)} %copy-done.15, bf16[512,2048]{1,0:T(8,128)(2,1)S(1)} %copy-done.9, ...), custom_call_target="tpu_custom_call" | custom-call | flops 1048576 | bytes 65536 | tf_op jit(solution)/shard_map/kept/pallas_call | solution.py:223
  350.6 13.5 %collective-permute-done.28.refs_2_ = bf16[128,2048]{1,0:T(8,128)(2,1)S(1)} collective-permute-done((bf16[128,2048]{1,0:T(8,128)(2,1)S(1)}, bf16[128,2048]{1,0:T(8,128)(2,1)S(1)}, u32[]{:S(2)}, u32[]{:S(2)}) %collective-permute-start.28) | collective-permute-done | bytes 524320 | tf_op jit(solution)/shard_map/ppermute | solution.py:61
  364.4 7.4 %kept.4 = (f32[1,256,2048]{2,1,0:T(8,128)S(1)}, bf16[1,256,2048]{2,1,0:T(8,128)(2,1)}, bf16[1,256,2048]{2,1,0:T(8,128)(2,1)}, bf16[1,256,2048]{2,1,0:T(8,128)(2,1)}) custom-call(s32[2]{0:T(128)S(1)} %pad_add_fusion.5.seat, bf16[1,512,2048]{2,1,0:T(8,128)(2,1)S(1)} %bitcast.121, bf16[512,2048]{1,0:T(8,128)(2,1)S(1)} %copy-done.11, ...), custom_call_target="tpu_custom_call" | custom-call | flops 1048576 | bytes 65536 | tf_op jit(solution)/shard_map/kept/pallas_call | solution.py:223
  371.9 5.1 collective-permute-done.29.refs_3_
  417.7 35.3 %backward.1 = (bf16[768,128]{1,0:T(8,128)(2,1)}, bf16[768,128]{1,0:T(8,128)(2,1)}, bf16[768,128]{1,0:T(8,128)(2,1)}, bf16[768,128]{1,0:T(8,128)(2,1)}, bf16[768,...) custom-call(s32[18]{0:T(128)} %copy-done.74, ...), custom_call_target="tpu_custom_call" | custom-call | flops 1048576 | bytes 65536 | tf_op jit(solution)/shard_map/backward/pallas_call | solution.py:278
  458.7 3.8 add_bitcast_fusion
  471.2 4.6 collective-permute-done.55.refs_7_
  479.3 4.6 sent.7
  487.2 6.0 %attn_back.1 = (bf16[512,2048]{1,0:T(8,128)(2,1)S(1)}, f32[2,2048]{1,0:T(2,128)S(1)}) custom-call(bf16[3,512,512]{2,1,0:T(8,128)(2,1)S(1)} %get-tuple-element.210.grads.left, bf16[512,2048]{1,0:T(8,128)(2,1)S(1)} %copy-done.1, f32[1,2048]{1,0:T(1,128)S(1)} %bitcast.124, f32[1,2048]{1,0:T(1,128)S(1)} %bitcast.128, bf16[3,2048,512]{2,1,0:T(8,128)(2,1)S(1)} %copy-done), custom_call_target="tpu_custom_call" | custom-call | flops 1048576 | bytes 65536 | tf_op jit(solution)/shard_map/attn_back/pallas_call | solution.py:278
  496.1 6.4 %kept.7 = (f32[3,256,512]{2,1,0:T(8,128)S(1)}, bf16[2,3,128,512]{3,2,1,0:T(8,128)(2,1)}, bf16[2,3,128,512]{3,2,1,0:T(8,128)(2,1)}, bf16[3,128,512]{2,1,0:T(8,128)(2,1)S(1)}, bf16[3,128,512]{2,1,0:T(8,128)(2,1)S(1)}) custom-call(s32[2]{0:T(128)S(1)} %pad_add_fusion.5.seat, bf16[3,512,512]{2,1,0:T(8,128)(2,1)S(1)} %copy-done.3, ...), custom_call_target="tpu_custom_call" | custom-call | flops 1048576 | bytes 65536 | tf_op jit(solution)/shard_map/kept/pallas_call | solution.py:223
  517.4 6.9 %collective-permute-done.57 = bf16[2,3,128,512]{3,2,1,0:T(8,128)(2,1)S(1)} collective-permute-done((bf16[2,3,128,512]{3,2,1,0:T(8,128)(2,1)}, bf16[2,3,128,512]{3,2,1,0:T(8,128)(2,1)S(1)}, u32[]{:S(2)}, u32[]{:S(2)}) %collective-permute-start.57) | collective-permute-done | bytes 786464 | tf_op jit(solution)/shard_map/ppermute | solution.py:78
  526.4 3.5 collective-permute-done.67
  529.9 6.0 %collective-permute-done.68 = bf16[512,256]{1,0:T(8,128)(2,1)} collective-permute-done((bf16[512,256]{1,0:T(8,128)(2,1)}, bf16[512,256]{1,0:T(8,128)(2,1)}, u32[]{:S(2)}, u32[]{:S(2)}) %collective-permute-start.68) | collective-permute-done | bytes 262176 | tf_op jit(solution)/shard_map/ppermute | solution.py:78
  550.2 4.5 collective-permute-done.60
  (507 shorter events, 227.3 us)
Async XLA Ops:
  7.2 127.5 %all-gather.2.cloned.1.call-start = ((), (), s32[]{:S(2)}) async-start(), calls=%async_computation.4 | async-start | bytes 2621440 | tf_op jit(solution)/shard_map/all_gather | solution.py:49
  11.9 16.0 %collective-permute-start.3 = (bf16[128,2048]{1,0:T(8,128)(2,1)S(1)}, bf16[128,2048]{1,0:T(8,128)(2,1)S(1)}, u32[]{:S(2)}, u32[]{:S(2)}) collective-permute-start(bf16[128,2048]{1,0:T(8,128)(2,1)S(1)} %fusion.4.refs_0_), channel_id=1, source_target_pairs={{0,1},{1,3},{3,2},{2,0},{4,5},{5,7},{7,6},{6,4},{8,9},{9,11},{11,1... | collective-permute-start | bytes 1572872 | tf_op jit(solution)/shard_map/ppermute | solution.py:61
  27.9 17.7 %collective-permute-start.4 = (bf16[128,2048]{1,0:T(8,128)(2,1)S(1)}, bf16[128,2048]{1,0:T(8,128)(2,1)S(1)}, u32[]{:S(2)}, u32[]{:S(2)}) collective-permute-start(bf16[128,2048]{1,0:T(8,128)(2,1)S(1)} %collective-permute-done.3.refs_1_), channel_id=1, source_target_pairs={{0,1},{1,3},{3,2},{2,0},{4,5},{5,7},{7,6},{6,4},{8,9},{9,11},{11,1... | collective-permute-start | bytes 1572872 | tf_op jit(solution)/shard_map/ppermute | solution.py:61
  45.6 13.8 %collective-permute-start.5 = (bf16[128,2048]{1,0:T(8,128)(2,1)S(1)}, bf16[128,2048]{1,0:T(8,128)(2,1)S(1)}, u32[]{:S(2)}, u32[]{:S(2)}) collective-permute-start(bf16[128,2048]{1,0:T(8,128)(2,1)S(1)} %collective-permute-done.4.refs_0_), channel_id=1, source_target_pairs={{0,1},{1,3},{3,2},{2,0},{4,5},{5,7},{7,6},{6,4},{8,9},{9,11},{11,1... | collective-permute-start | bytes 1572872 | tf_op jit(solution)/shard_map/ppermute | solution.py:61
  70.2 135.3 %reduce-scatter.5.cloned.1.call-start = ((), (), s32[]{:S(2)}) async-start(), calls=%async_computation.5 | async-start | bytes 2621440 | tf_op jit(solution)/shard_map/reduce_scatter | solution.py:74
  70.4 15.8 %collective-permute-start.10 = (bf16[768,128]{1,0:T(8,128)(2,1)}, bf16[768,128]{1,0:T(8,128)(2,1)S(1)}, u32[]{:S(2)}, u32[]{:S(2)}) collective-permute-start(bf16[768,128]{1,0:T(8,128)(2,1)} %copy-done.85), channel_id=1, source_target_pairs={{0,20},{4,16},{8,28},{12,24},{16,4},{20,0},{24,12},{28,8},{1,21},{... | collective-permute-start | bytes 589832 | tf_op jit(solution)/shard_map/ppermute | solution.py:78
  70.5 16.2 %collective-permute-start.11 = (bf16[768,128]{1,0:T(8,128)(2,1)}, bf16[768,128]{1,0:T(8,128)(2,1)S(1)}, u32[]{:S(2)}, u32[]{:S(2)}) collective-permute-start(bf16[768,128]{1,0:T(8,128)(2,1)} %copy-done.84), channel_id=1, source_target_pairs={{0,24},{4,28},{8,16},{12,20},{16,8},{20,12},{24,0},{28,4},{1,25},{... | collective-permute-start | bytes 589832 | tf_op jit(solution)/shard_map/ppermute | solution.py:78
  72.4 14.9 %collective-permute-start.12 = (bf16[768,128]{1,0:T(8,128)(2,1)}, bf16[768,128]{1,0:T(8,128)(2,1)S(1)}, u32[]{:S(2)}, u32[]{:S(2)}) collective-permute-start(bf16[768,128]{1,0:T(8,128)(2,1)} %copy-done.83), channel_id=1, source_target_pairs={{0,28},{4,24},{8,20},{12,16},{16,12},{20,8},{24,4},{28,0},{1,29},{... | collective-permute-start | bytes 589832 | tf_op jit(solution)/shard_map/ppermute | solution.py:78
  74.8 13.2 %collective-permute-start.6 = (bf16[768,128]{1,0:T(8,128)(2,1)}, bf16[768,128]{1,0:T(8,128)(2,1)}, u32[]{:S(2)}, u32[]{:S(2)}) collective-permute-start(bf16[768,128]{1,0:T(8,128)(2,1)} %copy-done.82), channel_id=1, source_target_pairs={{0,4},{4,0},{8,12},{12,8},{16,20},{20,16},{24,28},{28,24},{1,5},{5... | collective-permute-start | bytes 589832 | tf_op jit(solution)/shard_map/ppermute | solution.py:78
  162.2 169.3 %reduce-scatter.7.cloned.1.call-start = ((), (), s32[]{:S(2)}) async-start(), calls=%async_computation.6 | async-start | bytes 2621440 | tf_op jit(solution)/shard_map/reduce_scatter | solution.py:74
  208.2 14.4 %collective-permute-start.22 = (bf16[128,2048]{1,0:T(8,128)(2,1)S(1)}, bf16[128,2048]{1,0:T(8,128)(2,1)S(1)}, u32[]{:S(2)}, u32[]{:S(2)}) collective-permute-start(bf16[128,2048]{1,0:T(8,128)(2,1)S(1)} %add_convert_fusion.1.refs_0_), channel_id=1, source_target_pairs={{0,1},{1,3},{3,2},{2,0},{4,5},{5,7},{7,6},{6,4},{8,9},{9,11},{11,1... | collective-permute-start | bytes 1572872 | tf_op jit(solution)/shard_map/ppermute | solution.py:61
  222.7 13.5 %collective-permute-start.23 = (bf16[128,2048]{1,0:T(8,128)(2,1)S(1)}, bf16[128,2048]{1,0:T(8,128)(2,1)S(1)}, u32[]{:S(2)}, u32[]{:S(2)}) collective-permute-start(bf16[128,2048]{1,0:T(8,128)(2,1)S(1)} %collective-permute-done.22.refs_1_), channel_id=1, source_target_pairs={{0,1},{1,3},{3,2},{2,0},{4,5},{5,7},{7,6},{6,4},{8,9},{9,11},{11,1... | collective-permute-start | bytes 1572872 | tf_op jit(solution)/shard_map/ppermute | solution.py:61
  236.2 15.7 %collective-permute-start.24 = (bf16[128,2048]{1,0:T(8,128)(2,1)S(1)}, bf16[128,2048]{1,0:T(8,128)(2,1)S(1)}, u32[]{:S(2)}, u32[]{:S(2)}) collective-permute-start(bf16[128,2048]{1,0:T(8,128)(2,1)S(1)} %collective-permute-done.23.refs_0_), channel_id=1, source_target_pairs={{0,1},{1,3},{3,2},{2,0},{4,5},{5,7},{7,6},{6,4},{8,9},{9,11},{11,1... | collective-permute-start | bytes 1572872 | tf_op jit(solution)/shard_map/ppermute | solution.py:61
  287.8 179.0 %reduce-scatter.9.cloned.1.call-start = ((), (), s32[]{:S(2)}) async-start(), calls=%async_computation.7 | async-start | bytes 2621440 | tf_op jit(solution)/shard_map/reduce_scatter | solution.py:74
  306.1 30.2 %collective-permute-start.31 = (bf16[4,2048,256]{2,1,0:T(8,128)(2,1)}, bf16[4,2048,256]{2,1,0:T(8,128)(2,1)}, u32[]{:S(2)}, u32[]{:S(2)}) collective-permute-start(bf16[4,2048,256]{2,1,0:T(8,128)(2,1)} %sent.4), channel_id=1, source_target_pairs={{0,4},{4,0},{8,12},{12,8},{16,20},{20,16},{24,28},{28,24},{1,5},{5... | collective-permute-start | bytes 12582920 | tf_op jit(solution)/shard_map/ppermute | solution.py:78
  311.1 53.2 %collective-permute-start.30 = (bf16[4,1,256,2048]{3,2,1,0:T(8,128)(2,1)}, bf16[4,1,256,2048]{3,2,1,0:T(8,128)(2,1)}, u32[]{:S(2)}, u32[]{:S(2)}) collective-permute-start(bf16[4,1,256,2048]{3,2,1,0:T(8,128)(2,1)} %sent.5), channel_id=1, source_target_pairs={{0,4},{4,0},{8,12},{12,8},{16,20},{20,16},{24,28},{28,24},{1,5},{5... | collective-permute-start | bytes 12582920 | tf_op jit(solution)/shard_map/ppermute | solution.py:78
  336.2 14.4 %collective-permute-start.27 = (bf16[128,2048]{1,0:T(8,128)(2,1)S(1)}, bf16[128,2048]{1,0:T(8,128)(2,1)S(1)}, u32[]{:S(2)}, u32[]{:S(2)}) collective-permute-start(bf16[128,2048]{1,0:T(8,128)(2,1)S(1)} %get-tuple-element.247.refs_0_), channel_id=1, source_target_pairs={{0,1},{1,3},{3,2},{2,0},{4,5},{5,7},{7,6},{6,4},{8,9},{9,11},{11,1... | collective-permute-start | bytes 1572872 | tf_op jit(solution)/shard_map/ppermute | solution.py:61
  344.3 27.5 %collective-permute-start.32 = (bf16[2,1024,256]{2,1,0:T(8,128)(2,1)S(1)}, bf16[2,1024,256]{2,1,0:T(8,128)(2,1)}, u32[]{:S(2)}, u32[]{:S(2)}) collective-permute-start(bf16[2,1024,256]{2,1,0:T(8,128)(2,1)S(1)} %get-tuple-element.170), channel_id=1, source_target_pairs={{0,8},{4,12},{8,0},{12,4},{16,24},{20,28},{24,16},{28,20},{1,9},{5... | collective-permute-start | bytes 3145736 | tf_op jit(solution)/shard_map/ppermute | solution.py:78
  345.9 26.0 %collective-permute-start.33 = (bf16[2,1024,256]{2,1,0:T(8,128)(2,1)S(1)}, bf16[2,1024,256]{2,1,0:T(8,128)(2,1)S(1)}, u32[]{:S(2)}, u32[]{:S(2)}) collective-permute-start(bf16[2,1024,256]{2,1,0:T(8,128)(2,1)S(1)} %get-tuple-element.171), channel_id=1, source_target_pairs={{0,16},{4,20},{8,24},{12,28},{16,0},{20,4},{24,8},{28,12},{1,17},{... | collective-permute-start | bytes 3145736 | tf_op jit(solution)/shard_map/ppermute | solution.py:78
  350.6 13.5 %collective-permute-start.28 = (bf16[128,2048]{1,0:T(8,128)(2,1)S(1)}, bf16[128,2048]{1,0:T(8,128)(2,1)S(1)}, u32[]{:S(2)}, u32[]{:S(2)}) collective-permute-start(bf16[128,2048]{1,0:T(8,128)(2,1)S(1)} %collective-permute-done.27.refs_1_), channel_id=1, source_target_pairs={{0,1},{1,3},{3,2},{2,0},{4,5},{5,7},{7,6},{6,4},{8,9},{9,11},{11,1... | collective-permute-start | bytes 1572872 | tf_op jit(solution)/shard_map/ppermute | solution.py:61
  382.0 163.5 %reduce-scatter.11.cloned.1.call-start = ((), (), s32[]{:S(2)}) async-start(), calls=%async_computation.8 | async-start | bytes 2621440 | tf_op jit(solution)/shard_map/reduce_scatter | solution.py:74
  386.1 13.6 %collective-permute-start.37 = (bf16[1024,256]{1,0:T(8,128)(2,1)S(1)}, bf16[1024,256]{1,0:T(8,128)(2,1)S(1)}, u32[]{:S(2)}, u32[]{:S(2)}) collective-permute-start(bf16[1024,256]{1,0:T(8,128)(2,1)S(1)} %fusion.12), channel_id=1, source_target_pairs={{0,8},{4,12},{8,0},{12,4},{16,24},{20,28},{24,16},{28,20},{1,9},{5... | collective-permute-start | bytes 1572872 | tf_op jit(solution)/shard_map/ppermute | solution.py:78
  389.9 23.4 %collective-permute-start.38 = (bf16[4,512,256]{2,1,0:T(8,128)(2,1)S(1)}, bf16[4,512,256]{2,1,0:T(8,128)(2,1)S(1)}, u32[]{:S(2)}, u32[]{:S(2)}) collective-permute-start(bf16[4,512,256]{2,1,0:T(8,128)(2,1)S(1)} %sent.6), channel_id=1, source_target_pairs={{0,4},{4,0},{8,12},{12,8},{16,20},{20,16},{24,28},{28,24},{1,5},{5... | collective-permute-start | bytes 3145736 | tf_op jit(solution)/shard_map/ppermute | solution.py:78
  409.1 45.5 %collective-permute-start.46 = (bf16[1,256,2048]{2,1,0:T(8,128)(2,1)}, bf16[1,256,2048]{2,1,0:T(8,128)(2,1)}, u32[]{:S(2)}, u32[]{:S(2)}) collective-permute-start(bf16[1,256,2048]{2,1,0:T(8,128)(2,1)} %get-tuple-element.199), channel_id=1, source_target_pairs={{0,8},{4,12},{8,0},{12,4},{16,24},{20,28},{24,16},{28,20},{1,9},{5... | collective-permute-start | bytes 3145736 | tf_op jit(solution)/shard_map/ppermute | solution.py:78
  410.7 47.2 %collective-permute-start.47 = (bf16[1,256,2048]{2,1,0:T(8,128)(2,1)}, bf16[1,256,2048]{2,1,0:T(8,128)(2,1)}, u32[]{:S(2)}, u32[]{:S(2)}) collective-permute-start(bf16[1,256,2048]{2,1,0:T(8,128)(2,1)} %get-tuple-element.200), channel_id=1, source_target_pairs={{0,16},{4,20},{8,24},{12,28},{16,0},{20,4},{24,8},{28,12},{1,17},{... | collective-permute-start | bytes 3145736 | tf_op jit(solution)/shard_map/ppermute | solution.py:78
  411.4 47.3 %collective-permute-start.48 = (bf16[1,256,2048]{2,1,0:T(8,128)(2,1)}, bf16[1,256,2048]{2,1,0:T(8,128)(2,1)}, u32[]{:S(2)}, u32[]{:S(2)}) collective-permute-start(bf16[1,256,2048]{2,1,0:T(8,128)(2,1)} %get-tuple-element.201), channel_id=1, source_target_pairs={{0,24},{4,28},{8,16},{12,20},{16,8},{20,12},{24,0},{28,4},{1,25},{... | collective-permute-start | bytes 3145736 | tf_op jit(solution)/shard_map/ppermute | solution.py:78
  454.6 14.6 %collective-permute-start.51 = (bf16[768,128]{1,0:T(8,128)(2,1)}, bf16[768,128]{1,0:T(8,128)(2,1)}, u32[]{:S(2)}, u32[]{:S(2)}) collective-permute-start(bf16[768,128]{1,0:T(8,128)(2,1)} %get-tuple-element.205), channel_id=1, source_target_pairs={{0,12},{4,8},{8,4},{12,0},{16,28},{20,24},{24,20},{28,16},{1,13},{... | collective-permute-start | bytes 589832 | tf_op jit(solution)/shard_map/ppermute | solution.py:78
  503.7 20.6 %collective-permute-start.57 = (bf16[2,3,128,512]{3,2,1,0:T(8,128)(2,1)}, bf16[2,3,128,512]{3,2,1,0:T(8,128)(2,1)S(1)}, u32[]{:S(2)}, u32[]{:S(2)}) collective-permute-start(bf16[2,3,128,512]{3,2,1,0:T(8,128)(2,1)} %get-tuple-element.215), channel_id=1, source_target_pairs={{0,8},{4,12},{8,0},{12,4},{16,24},{20,28},{24,16},{28,20},{1,9},{5... | collective-permute-start | bytes 2359304 | tf_op jit(solution)/shard_map/ppermute | solution.py:78
  504.9 20.7 %collective-permute-start.59 = (bf16[2,3,128,512]{3,2,1,0:T(8,128)(2,1)}, bf16[2,3,128,512]{3,2,1,0:T(8,128)(2,1)S(1)}, u32[]{:S(2)}, u32[]{:S(2)}) collective-permute-start(bf16[2,3,128,512]{3,2,1,0:T(8,128)(2,1)} %get-tuple-element.217), channel_id=1, source_target_pairs={{0,16},{4,20},{8,24},{12,28},{16,0},{20,4},{24,8},{28,12},{1,17},{... | collective-permute-start | bytes 2359304 | tf_op jit(solution)/shard_map/ppermute | solution.py:78
  513.0 17.0 %collective-permute-start.67 = (bf16[512,256]{1,0:T(8,128)(2,1)}, bf16[512,256]{1,0:T(8,128)(2,1)S(1)}, u32[]{:S(2)}, u32[]{:S(2)}) collective-permute-start(bf16[512,256]{1,0:T(8,128)(2,1)} %copy-done.78), channel_id=1, source_target_pairs={{0,8},{4,12},{8,0},{12,4},{16,24},{20,28},{24,16},{28,20},{1,9},{5... | collective-permute-start | bytes 786440 | tf_op jit(solution)/shard_map/ppermute | solution.py:78
  513.9 22.0 %collective-permute-start.68 = (bf16[512,256]{1,0:T(8,128)(2,1)}, bf16[512,256]{1,0:T(8,128)(2,1)}, u32[]{:S(2)}, u32[]{:S(2)}) collective-permute-start(bf16[512,256]{1,0:T(8,128)(2,1)} %copy-done.77), channel_id=1, source_target_pairs={{0,16},{4,20},{8,24},{12,28},{16,0},{20,4},{24,8},{28,12},{1,17},{... | collective-permute-start | bytes 786440 | tf_op jit(solution)/shard_map/ppermute | solution.py:78
  516.0 19.9 %collective-permute-start.69 = (bf16[512,256]{1,0:T(8,128)(2,1)S(1)}, bf16[512,256]{1,0:T(8,128)(2,1)}, u32[]{:S(2)}, u32[]{:S(2)}) collective-permute-start(bf16[512,256]{1,0:T(8,128)(2,1)S(1)} %copy-done.76), channel_id=1, source_target_pairs={{0,24},{4,28},{8,16},{12,20},{16,8},{20,12},{24,0},{28,4},{1,25},{... | collective-permute-start | bytes 786440 | tf_op jit(solution)/shard_map/ppermute | solution.py:78
  (167 other events, 1666.1 us)
Sparse Core Ops, SparseCore 0:
  70.3 45.7 all-gather.1
  162.3 43.0 reduce-scatter.4
  287.9 43.5 reduce-scatter.6
  382.1 43.8 reduce-scatter.8
  494.8 44.9 reduce-scatter.10

commit v3 on v2

--- a/solution.py
+++ b/solution.py
@@ -62,12 +62,15 @@
     return parts
 
 
-def part_owners():
+def part_owners(first):
     order = ring_order(lax.axis_size("tp"))
     count = len(order)
-    spot = jnp.array([order.index(rank) for rank in range(count)], jnp.int32)[lax.axis_index("tp")]
-    ranks = jnp.array(order, jnp.int32)
-    return [ranks[(spot + count - slot) % count] for slot in range(count)]
+    rows = [
+        [order[(order.index(rank) - first - slot) % count] for slot in range(count)]
+        for rank in range(count)
+    ]
+    table = jnp.array(rows, jnp.int32)
+    return lax.dynamic_index_in_dim(table, lax.axis_index("tp"), 0, keepdims=False)
 
 
 def scatter_rows(values):
@@ -247,23 +250,40 @@
     )
 
 
-def finish_gradient(pieces, count, arrived=None):
+def add_gradient(rest, *earlier):
+    if isinstance(rest, list):
+        total = after(rest[0], *earlier) if earlier else rest[0]
+        for got in rest[1:]:
+            total = total + got.astype(WIDE)
+        return total
+    total, first, first_own, second, second_own, axis = rest
+    if earlier:
+        total = after(total, *earlier)
+    first = first.astype(WIDE) + first_own.astype(WIDE)
+    second = second.astype(WIDE) + second_own.astype(WIDE)
+    return total + jnp.concatenate([first, second], axis=axis)
+
+
+def start_gradient(pieces, count):
+    if count != 8:
+        return pieces
+    total, across, along, keep_first, keep_second = pieces
+    return total, hop(across, "seq", 2, count), hop(along, "seq", 4, count), keep_first, keep_second
+
+
+def finish_gradient(pieces, count, sent=None):
     total = pieces[0]
     if count == 8 and pieces[1].ndim > total.ndim:
         _, across, along, keep_first, keep_second = pieces
         axis = total.ndim - 2
-        across = hop(across, "seq", 2, count)
-        along = hop(along, "seq", 4, count)
-        if arrived is not None:
-            arrived += [across, along]
         first = (keep_first.astype(WIDE) + across[1].astype(WIDE)).astype(NARROW)
         second = (keep_second.astype(WIDE) + along[1].astype(WIDE)).astype(NARROW)
-        first = hop(first, "seq", 4, count).astype(WIDE) + across[0].astype(WIDE)
-        second = hop(second, "seq", 2, count).astype(WIDE) + along[0].astype(WIDE)
-        return total + jnp.concatenate([first, second], axis=axis)
-    for slot in range(1, len(pieces)):
-        total = total + hop(pieces[slot], "seq", 2 * slot, count).astype(WIDE)
-    return total
+        if sent is not None:
+            sent += [first, second]
+        first = hop(first, "seq", 4, count)
+        second = hop(second, "seq", 2, count)
+        return total, first, across[0], second, along[0], axis
+    return [total] + [hop(pieces[slot], "seq", 2 * slot, count) for slot in range(1, len(pieces))]
 
 
 def scalar_spec():
@@ -290,6 +310,22 @@
     )(*scalars, *inputs, *heavy)
 
 
+def resident_call(kernel, name, scalars, remote, inputs, outs, remote_outs, scratch, mib):
+    return pl.pallas_call(
+        kernel,
+        name=name,
+        out_shape=tuple(outs) + tuple(remote_outs),
+        in_specs=[scalar_spec()] * len(scalars)
+        + [pl.BlockSpec(memory_space=pl.ANY)] * len(remote)
+        + [pl.BlockSpec(memory_space=pltpu.VMEM)] * len(inputs),
+        out_specs=(pl.BlockSpec(memory_space=pltpu.VMEM),) * len(outs)
+        + (pl.BlockSpec(memory_space=pl.ANY),) * len(remote_outs),
+        scratch_shapes=list(scratch),
+        compiler_params=params(mib),
+        cost_estimate=SMALL,
+    )(*scalars, *remote, *inputs)
+
+
 def shaped(shape, dtype):
     return jax.ShapeDtypeStruct(tuple(shape), dtype)
 
@@ -327,38 +363,73 @@
     return pl.ds(pl.multiple_of(owner * rows, rows), rows)
 
 
-def pack_kernel(seat, *refs, parts, heads, merge):
+def pack_kernel(place, owners, *refs, parts, heads, merge):
     rows_in = refs[:parts]
-    bias, straight, crossed = refs[parts : parts + 3]
-    at = parts + 3
+    at = parts
     if merge:
         earlier, earlier_rows = refs[at : at + 2]
         at += 2
-    weight = refs[at]
-    at += 1
+    sources = refs[at : at + 4]
+    at += 4
     if merge:
         outs, rows_out = refs[at : at + heads], refs[at + heads]
     else:
         out, rows_out = refs[at], refs[at + 1]
-    rows, held, kept, sems = refs[-4:]
-    fetch_all(weight, kept, sems, 2)
+    if merge:
+        held_before, rows_before, *rest = refs[-10:]
+    else:
+        rest = refs[-8:]
+    weight, bias, straight, crossed, rows, held, sems, more_sems = rest
+    count = weight.shape[0]
+    loads = [
+        pltpu.make_async_copy(sources[0].at[c], weight.at[c], more_sems.at[c]) for c in range(count)
+    ] + [
+        pltpu.make_async_copy(source, target, more_sems.at[count + k])
+        for k, (source, target) in enumerate(zip(sources[1:], (bias, straight, crossed)))
+    ]
     part = rows_in[0].shape[0]
     half = part // 2
     size = part + half
+    incoming = [
+        pltpu.make_async_copy(rows_in[i], rows.at[i * part : (i + 1) * part, :], sems.at[0, i])
+        for i in range(parts)
+    ]
+    outgoing = []
+
+    def send(source, target, *where):
+        copy = pltpu.make_async_copy(source, target, sems.at[where])
+        copy.start()
+        outgoing.append(copy)
+
+    for copy in incoming + loads:
+        copy.start()
+    for copy in incoming:
+        copy.wait()
+    if merge:
+        before = [
+            pltpu.make_async_copy(earlier, held_before, sems.at[0, 3 * parts]),
+            pltpu.make_async_copy(earlier_rows, rows_before, sems.at[0, 3 * parts + 1]),
+        ]
+        for copy in before:
+            copy.start()
     for i in range(parts):
-        rows[i * part : (i + 1) * part, :] = rows_in[i][...]
+        mine = rows_at(owners[i], part) if merge else slice(i * part, (i + 1) * part)
+        send(rows.at[i * part : (i + 1) * part, :], rows_out.at[mine, :], 0, 2 * parts + i)
+    for copy in loads[count:]:
+        copy.wait()
     straight, crossed = (
-        jnp.concatenate([table[rows_at(seat[1 + i], part), :] for i in range(parts)], axis=0)
+        jnp.concatenate([table[rows_at(owners[i], part), :] for i in range(parts)], axis=0)
         for table in (straight, crossed)
     )
+    projected = []
+    for c in range(count):
+        loads[c].wait()
+        projected.append(
+            jnp.dot(rows[...], weight[c], preferred_element_type=WIDE) + bias[c : c + 1, :]
+        )
     for step in range(weight.shape[2] // SPAN):
-        fetch(weight, kept, sems, step, 2).wait()
         cols = slice(step * SPAN, (step + 1) * SPAN)
-        query, key, value = (
-            jnp.dot(rows[...], kept[c, :, cols], preferred_element_type=WIDE)
-            + bias[c : c + 1, cols]
-            for c in range(3)
-        )
+        query, key, value = (item[:, cols] for item in projected)
         for side in range(SPAN // HD):
             lanes = slice(side * HD, (side + 1) * HD)
             head = step * (SPAN // HD) + side
@@ -371,22 +442,37 @@
                     [one[:half], one[half:]], axis=1
                 ).astype(NARROW)
     if merge:
+        for copy in before:
+            copy.wait()
         for i in range(parts):
-            mine = rows_at(seat[1 + i], size)
-            other = rows_at(seat[1 + parts + i], size)
+            other = owners[parts + i]
+            send(
+                rows_before.at[i * part : (i + 1) * part, :],
+                rows_out.at[rows_at(other, part), :],
+                0,
+                parts + i,
+            )
             for slot in range(heads):
-                outs[slot][mine, :] = held[i, seat[0] ^ slot]
-                outs[slot][other, :] = earlier[i, seat[0] ^ slot]
-            rows_out[rows_at(seat[1 + i], part), :] = rows[i * part : (i + 1) * part, :]
-            rows_out[rows_at(seat[1 + parts + i], part), :] = earlier_rows[
-                i * part : (i + 1) * part, :
-            ]
+                send(
+                    held_before.at[i, place[0] ^ slot],
+                    outs[slot].at[rows_at(other, size), :],
+                    1 + i,
+                    slot,
+                )
+                send(
+                    held.at[i, place[0] ^ slot],
+                    outs[slot].at[rows_at(owners[i], size), :],
+                    1 + parts + i,
+                    slot,
+                )
     else:
-        out[...] = held[...]
-        rows_out[...] = rows[...]
-
-
-def pack_heads(seat, parts, weight, bias, straight, crossed, heads, earlier=()):
+        for i in range(parts):
+            send(held.at[i], out.at[i], 1, i)
+    for copy in outgoing:
+        copy.wait()
+
+
+def pack_heads(place, owners, parts, weight, bias, straight, crossed, heads, earlier=()):
     count = len(parts)
     part, depth = parts[0].shape
     size = part + part // 2
@@ -395,20 +481,26 @@
         outs += [shaped((2 * count * part, depth), NARROW)]
     else:
         outs = [shaped((count, heads, size, 2 * HD), NARROW), shaped((count * part, depth), NARROW)]
-    return local_call(
+    return resident_call(
         functools.partial(pack_kernel, parts=count, heads=heads, merge=bool(earlier)),
         "pack",
-        [seat],
-        [*parts, bias, straight, crossed, *earlier],
-        [weight],
+        [place, owners],
+        [*parts, *earlier, weight, bias, straight, crossed],
+        [],
+        [],
         outs,
-        [
+        [pltpu.VMEM(item.shape, NARROW) for item in earlier]
+        + [
+            pltpu.VMEM(weight.shape, NARROW),
+            pltpu.VMEM(bias.shape, WIDE),
+            pltpu.VMEM(straight.shape, WIDE),
+            pltpu.VMEM(crossed.shape, WIDE),
             pltpu.VMEM((count * part, depth), NARROW),
             pltpu.VMEM((count, heads, size, 2 * HD), NARROW),
-            pltpu.VMEM(weight.shape, NARROW),
-            pltpu.SemaphoreType.DMA((weight.shape[2] // SPAN,)),
+            pltpu.SemaphoreType.DMA((1 + 2 * count, max(heads, 3 * count + 2))),
+            pltpu.SemaphoreType.DMA((weight.shape[0] + 3,)),
         ],
-        48,
+        54,
     )
 
 
@@ -518,7 +610,7 @@
             pltpu.VMEM((blocks, HD, block), NARROW),
             pltpu.VMEM((count, HD, block), NARROW),
         ],
-        48,
+        60,
     )
 
 
@@ -682,7 +774,7 @@
         [],
         [shaped((block, count * HD), NARROW), shaped((2, block), WIDE)],
         [pltpu.VMEM((count, HD, block), NARROW)],
-        16,
+        60,
     )
 
 
@@ -715,7 +807,7 @@
         [],
         [shaped((3, block, count * HD), NARROW), shaped((3, count * HD), WIDE)],
         [pltpu.VMEM((count,) + chunks[0].shape, NARROW)],
-        24,
+        60,
     )
 
 
@@ -763,29 +855,26 @@
     return total
 
 
-def up_kernel(seat, *refs, parts, merge):
+def up_kernel(owners, *refs, parts, merge):
     rows_in = refs[:parts]
-    bias, gain, grad = refs[parts : parts + 3]
-    earlier = refs[parts + 3 : parts + 5] if merge else ()
-    weight, active_out, slope_out, rows_out, stats, rows, sums, kept, sems = refs[-9:]
-    fetch_all(weight, kept, sems, 1)
+    bias, gain, grad, weight = refs[parts : parts + 4]
+    earlier = refs[parts + 4 : parts + 6] if merge else ()
+    active_out, slope_out, rows_out, stats, rows, sums, sems = refs[-7:]
     part = rows_in[0].shape[0]
     own = [slice(i * part, (i + 1) * part) for i in range(parts)]
-    for i in range(parts):
-        rows[own[i], :] = rows_in[i][...]
-    if merge:
-        for i in range(parts):
-            rows_out[rows_at(seat[i], part), :] = rows_in[i][...]
-            rows_out[rows_at(seat[parts + i], part), :] = earlier[0][own[i], :]
-    else:
-        rows_out[...] = rows[...]
+    copies = [
+        pltpu.make_async_copy(rows_in[i], rows.at[own[i], :], sems.at[i]) for i in range(parts)
+    ]
+    for copy in copies:
+        copy.start()
     sums[...] = jnp.zeros_like(sums)
+    for copy in copies:
+        copy.wait()
 
     @pl.loop(0, weight.shape[1] // SPAN)
     def _(step):
-        fetch(weight, kept, sems, step, 1).wait()
         cols = span_of(step)
-        value = jnp.dot(rows[...], kept[:, cols], preferred_element_type=WIDE) + bias[:, cols]
+        value = jnp.dot(rows[...], weight[:, cols], preferred_element_type=WIDE) + bias[:, cols]
         below = 0.5 + 0.5 * lax.erf(value * math.sqrt(0.5))
         active = value * below
         slope = below + value * (
@@ -793,7 +882,7 @@
         )
         active_out[:, cols] = active.astype(NARROW)
         slope_out[:, cols] = slope.astype(NARROW)
-        back = jnp.concatenate([grad[rows_at(seat[i], part), cols] for i in range(parts)], axis=0)
+        back = jnp.concatenate([grad[rows_at(owners[i], part), cols] for i in range(parts)], axis=0)
         scaled = back.astype(WIDE) * gain[:, cols]
         sums[0] += fold_lanes(active)
         sums[1] += fold_lanes(active * active)
@@ -803,55 +892,58 @@
     lines = jnp.concatenate([jnp.sum(sums[i].T, axis=0, keepdims=True) for i in range(4)], axis=0)
     if merge:
         for i in range(parts):
-            stats[:, rows_at(seat[i], part)] = lines[:, own[i]]
-            stats[:, rows_at(seat[parts + i], part)] = earlier[1][:, own[i]]
+            mine = rows_at(owners[i], part)
+            other = rows_at(owners[parts + i], part)
+            stats[:, mine] = lines[:, own[i]]
+            stats[:, other] = earlier[1][:, own[i]]
+            rows_out[mine, :] = rows[own[i], :]
+            rows_out[other, :] = earlier[0][own[i], :]
     else:
         stats[...] = lines
-
-
-def up_product(seat, parts, weight, bias, gain, grad, earlier=()):
+        rows_out[...] = rows[...]
+
+
+def up_product(owners, parts, weight, bias, gain, grad, earlier=()):
     count = len(parts)
     rows = count * parts[0].shape[0]
     depth, width = weight.shape
     both = rows * (2 if earlier else 1)
-    return local_call(
+    return resident_call(
         functools.partial(up_kernel, parts=count, merge=bool(earlier)),
         "up",
-        [seat],
-        [*parts, bias, gain, grad, *earlier],
-        [weight],
+        [owners],
+        parts,
+        [bias, gain, grad, weight, *earlier],
         [
             shaped((rows, width), NARROW),
             shaped((rows, width), NARROW),
             shaped((both, depth), NARROW),
             shaped((4, both), WIDE),
         ],
+        [],
         [
             pltpu.VMEM((rows, depth), NARROW),
             pltpu.VMEM((4, rows, 128), WIDE),
-            pltpu.VMEM(weight.shape, NARROW),
-            pltpu.SemaphoreType.DMA((width // SPAN,)),
+            pltpu.SemaphoreType.DMA((count,)),
         ],
-        48,
-    )
-
-
-def ffn_back_kernel(seat, *refs, count, parts, width):
-    sums = refs[:count]
-    halves = refs[count : count + 2], refs[count + 2 : count + 4]
-    grad, gain, shift, weight = refs[count + 4 : count + 8]
-    hidden_out, grad_out, product, lines, columns, total, kept, sems = refs[count + 8 :]
-    fetch_all(weight, kept, sems, 1)
+        20,
+    )
+
+
+def ffn_back_kernel(owners, got, mine, *refs, parts, width):
+    halves = refs[:2], refs[2:4]
+    grad, gain, shift, weight, hidden_out, grad_out, lines, product = refs[4:12]
+    columns, total, sums, low, sems = refs[12:]
     part = grad.shape[0] // parts
-    whole = sums[0][...]
-    for other in sums[1:]:
-        whole = whole + other[...]
-    whole = whole / width
+    copy = pltpu.make_async_copy(got, sums, sems.at[0])
+    copy.start()
+    total[...] = jnp.zeros_like(total)
+    copy.wait()
+    whole = (mine[...] + sums[...]) / width
     center, square, lean, cross = (whole[i : i + 1] for i in range(4))
     factor = lax.rsqrt(square - center * center + EPSILON)
     cross = (cross - center * lean) * factor
     columns[...] = jnp.concatenate([center, factor, lean, cross, whole], axis=0).T
-    total[...] = jnp.zeros_like(total)
 
     @pl.loop(0, weight.shape[1] // SPAN)
     def _(step):
@@ -862,7 +954,7 @@
             active, slope = halves[i // (parts // 2)]
             own = i % (parts // 2)
             own = slice(own * part, (own + 1) * part)
-            rows = rows_at(seat[i], part)
+            rows = rows_at(owners[i], part)
             center, factor, lean, cross = (columns[rows, k : k + 1] for k in range(4))
             unit = (active[own, cols].astype(WIDE) - center) * factor
             hidden_out[rows, cols] = (unit * gain[:, cols] + shift[:, cols]).astype(NARROW)
@@ -875,39 +967,51 @@
             line[1] = line[1] + jnp.sum(back * unit, axis=0, keepdims=True)
             line[2] = line[2] + jnp.sum(back, axis=0, keepdims=True)
         lines[:, cols] = jnp.concatenate(line, axis=0)
-        fetch(weight, kept, sems, step, 1).wait()
         total[...] += lax.dot_general(
             jnp.concatenate(grads, axis=0),
-            kept[:, cols],
+            weight[:, cols],
             (((1,), (1,)), ((), ())),
             preferred_element_type=WIDE,
         )
 
+    outgoing = []
     for i in range(parts):
-        product[rows_at(seat[i], part), :] = total[i * part : (i + 1) * part, :].astype(NARROW)
-
-
-def ffn_back_product(seat, sums, near, far, grad, gain, shift, weight, width):
+        low[i * part : (i + 1) * part, :] = total[i * part : (i + 1) * part, :].astype(NARROW)
+        copy = pltpu.make_async_copy(
+            low.at[i * part : (i + 1) * part, :],
+            product.at[rows_at(owners[i], part), :],
+            sems.at[1 + i],
+        )
+        copy.start()
+        outgoing.append(copy)
+    for copy in outgoing:
+        copy.wait()
+
+
+def ffn_back_product(owners, sums, near, far, grad, gain, shift, weight, width):
     rows, local = grad.shape
     depth = weight.shape[0]
     both = shaped((rows, local), NARROW)
-    return local_call(
-        functools.partial(
-            ffn_back_kernel, count=len(sums), parts=seat.shape[0], width=width
-        ),
+    parts = owners.shape[0]
+    mine, got = sums
+    hidden, grad_up, lines, product = resident_call(
+        functools.partial(ffn_back_kernel, parts=parts, width=width),
         "ffn_back",
-        [seat],
-        [*sums, *near, *far, grad, gain, shift],
-        [weight],
-        [both, both, shaped((rows, depth), NARROW), shaped((3, local), WIDE)],
+        [owners],
+        [got],
+        [mine, *near, *far, grad, gain, shift, weight],
+        [both, both, shaped((3, local), WIDE)],
+        [shaped((rows, depth), NARROW)],
         [
             pltpu.VMEM((rows, 8), WIDE),
             pltpu.VMEM((rows, depth), WIDE),
-            pltpu.VMEM(weight.shape, NARROW),
-            pltpu.SemaphoreType.DMA((local // SPAN,)),
+            pltpu.VMEM(mine.shape, WIDE),
+            pltpu.VMEM((rows, depth), NARROW),
+            pltpu.SemaphoreType.DMA((1 + parts,)),
         ],
-        56,
-    )
+        24,
+    )
+    return hidden, grad_up, product, lines
 
 
 def mixed_back_kernel(seat, *refs, parts):
@@ -981,7 +1085,7 @@
         [],
         [shaped((HD, block), NARROW)] * heads,
         [pltpu.VMEM((heads, HD, block), NARROW)],
-        16,
+        60,
     )
 
 
@@ -1016,7 +1120,7 @@
             pltpu.VMEM(weight.shape, NARROW),
             pltpu.SemaphoreType.DMA((depth // SPAN,)),
         ],
-        32,
+        60,
     )
 
 
@@ -1058,7 +1162,9 @@
     home = seq_rank - place
 
     def trade(chunks):
-        return [chunks[0]] + [hop(chunks[m], "seq", m, seq_count) for m in range(1, team)]
+        got = {m: hop(chunks[m], "seq", m, seq_count) for m in range(2, team)}
+        got[1] = hop(after(chunks[1], got[2]), "seq", 1, seq_count)
+        return [chunks[0]] + [got[m] for m in range(1, team)]
 
     row_index = seq_rank * local_rows + jnp.arange(local_rows, dtype=jnp.int32)
     documents = jnp.arange(COUNT, dtype=jnp.int32)
@@ -1091,9 +1197,8 @@
     tp_count = lax.axis_size("tp")
     tp_rank = lax.axis_index("tp")
     inner = tp_count // 2
-    owners = part_owners()
-    near_first = owners[:inner] + owners[inner:]
-    far_first = owners[inner:] + owners[:inner]
+    near_first = part_owners(0)
+    far_first = part_owners(inner)
 
     def line(vector):
         return vector.astype(WIDE).reshape(1, -1)
@@ -1125,9 +1230,8 @@
     attn_parts[0] = after(attn_parts[0], straight, crossed)
 
     def pack(parts, chairs, earlier=()):
-        chair = jnp.stack([place.astype(jnp.int32)] + chairs)
         return pack_heads(
-            chair, parts, qkv_weight, qkv_bias.astype(WIDE), straight, crossed, team, earlier
+            seat, chairs, parts, qkv_weight, qkv_bias.astype(WIDE), straight, crossed, team, earlier
         )
 
     packed = pack(attn_parts[:inner], near_first)
@@ -1163,14 +1267,14 @@
 
     def up(parts, chairs, earlier=()):
         return up_product(
-            jnp.stack(chairs), parts, up_weight, line(up_bias), gain_line, grad_hidden, earlier
+            chairs, parts, up_weight, line(up_bias), gain_line, grad_hidden, earlier
         )
 
     *up_near, ffn_near, sums_near = up(ffn_parts[:inner], near_first)
     ffn_parts[inner] = after(ffn_parts[inner], sums_near)
     *up_far, ffn_in, sums = up(ffn_parts[inner:], far_first, (ffn_near, sums_near))
     hidden_low, grad_up, ffn_back, hidden_lines = ffn_back_product(
-        jnp.stack(owners),
+        near_first,
         exchange(sums),
         up_near,
         up_far,
@@ -1193,14 +1297,15 @@
     down_got = after(hop(down_sent, "seq", 1, seq_count), grad_low)
     up_got = hop(up_sent, "seq", 1, seq_count)
     down_pieces = keep_gradient(hidden_low, grad_rows, down_got, seq_rank, seq_count, True, True)
-    up_pieces = keep_gradient(grad_up[None], ffn_in, up_got, seq_rank, seq_count, False)
-    arrived = []
-    down_grad = finish_gradient(down_pieces, seq_count, arrived)
-    middle_parts[-1] = after(middle_parts[-1], *up_pieces, *arrived)
+    up_pieces = keep_gradient(
+        grad_up[None], ffn_in, up_got, seq_rank, seq_count, False, True
+    )
+    down_pieces = start_gradient(down_pieces, seq_count)
+    middle_parts[-1] = after(middle_parts[-1], *up_pieces, *down_pieces)
     outbias_part = jnp.sum(grad_low, axis=0, dtype=WIDE)
     downbias_part = jnp.sum(cotangent, axis=0, dtype=WIDE)
     grad_mixed_norm, grad_mixed_rows, back_sums, mixed_lines = mixed_back_product(
-        jnp.stack(owners),
+        near_first,
         middle_parts,
         mixed,
         mixed_stats,
@@ -1218,22 +1323,20 @@
         team,
         model_width,
     )
-    grad_cuts = list(grad_cuts)
-    grad_cuts[0] = after(grad_cuts[0], down_grad)
+    down_pieces = list(down_pieces)
+    for slot in range(1, len(down_pieces)):
+        down_pieces[slot] = after(down_pieces[slot], grad_mixed_norm)
+    down_rest = finish_gradient(down_pieces, seq_count)
     grad_chunks = trade(grad_cuts)
     up_pieces = list(up_pieces)
     for slot in range(1, len(up_pieces)):
         up_pieces[slot] = after(up_pieces[slot], *grad_chunks)
-    up_grad = finish_gradient(up_pieces, seq_count)[0]
+    up_pieces = list(start_gradient(up_pieces, seq_count))
     layer_out = (
         middle
         + scatter_rows(after(down_product, grad_mixed_norm))
         + down_bias.astype(WIDE)
     ).astype(NARROW)
-    out_sent = send_gradient(mixed_low, grad_mixed_rows, seq_rank, seq_count, True)
-    out_got = hop(out_sent, "seq", 1, seq_count)
-    out_pieces = keep_gradient(mixed_low, grad_mixed_rows, out_got, seq_rank, seq_count, True)
-    grad_chunks[0] = after(grad_chunks[0], *out_pieces)
     pieces = attend_backward(
         info,
         team_starts,
@@ -1245,7 +1348,13 @@
         tp_count,
     )
     pieces = list(pieces)
-    pieces[0] = after(pieces[0], layer_out, up_grad)
+    down_grad = add_gradient(down_rest, pieces[0])
+    arrived = list(down_rest[1:4:2]) + up_pieces[1:3]
+    pieces = [after(piece, *arrived) for piece in pieces]
+    out_sent = send_gradient(mixed_low, after(grad_mixed_rows, pieces[0]), seq_rank, seq_count, True)
+    out_got = hop(out_sent, "seq", 1, seq_count)
+    out_pieces = keep_gradient(mixed_low, grad_mixed_rows, out_got, seq_rank, seq_count, True)
+    pieces[0] = after(pieces[0], layer_out)
     if teams > 1:
         natural = lax.psum_scatter(
             pieces[0], "seq", scatter_dimension=0, tiled=True, axis_index_groups=rings
@@ -1254,10 +1363,14 @@
             lax.dynamic_index_in_dim(natural, place ^ m, 0, keepdims=False) for m in range(team)
         ]
     parts_got = trade(pieces)
+    parts_got[0] = after(parts_got[0], down_grad, *out_pieces)
+    for slot in range(1, len(up_pieces)):
+        up_pieces[slot] = after(up_pieces[slot], *parts_got)
+    up_rest = finish_gradient(up_pieces, seq_count)
     out_pieces = list(out_pieces)
     for slot in range(1, len(out_pieces)):
         out_pieces[slot] = after(out_pieces[slot], *parts_got)
-    out_grad = finish_gradient(out_pieces, seq_count)
+    out_grad = add_gradient(finish_gradient(out_pieces, seq_count))
     stacked, qkvbias_part = unpack_heads(seat, straight, crossed, parts_got)
     qkv_got = hop(send_gradient(stacked, attn_in, seq_rank, seq_count, False), "seq", 1, seq_count)
     attn_back, attn_lines = attn_back_product(
@@ -1265,15 +1378,18 @@
     )
     inputgain_part, inputbias_part = attn_lines
     grad_attn_in = scatter_rows(attn_back)
+    qkv_got = after(qkv_got, out_grad, attn_back, *(up_rest[1:4:2] if isinstance(up_rest, tuple) else ()))
     qkv_pieces = keep_gradient(stacked, attn_in, qkv_got, seq_rank, seq_count, False, True)
-    arrived = []
-    qkv_grad = finish_gradient(qkv_pieces, seq_count, arrived)
+    qkv_pieces = start_gradient(qkv_pieces, seq_count)
+    qkv_sent = []
+    qkv_grad = add_gradient(finish_gradient(qkv_pieces, seq_count, qkv_sent))
 
     def spread_norms(parts):
         both = jnp.stack(parts).reshape(len(parts), seq_count, tp_count, -1)
         mine = tp_scatter(both.transpose(2, 1, 0, 3))
         return mine.reshape(seq_count, -1)
 
+    inputgain_part = after(inputgain_part, qkv_pieces[0])
     vectors = jnp.concatenate(
         [
             item.reshape(seq_count, -1)
@@ -1302,7 +1418,8 @@
         ],
         axis=1,
     )
-    vector_sums = vector_scatter(after(vectors, *arrived), seq_rank, seq_count)
+    vector_sums = vector_scatter(after(vectors, *qkv_sent), seq_rank, seq_count)
+    up_grad = add_gradient(up_rest, vector_sums)[0]
     grad_attn_in = after(grad_attn_in, vector_sums)
     grad_input_norm, _, _ = input_back(grad_attn_in)
     input_grad = (grad_middle + grad_input_norm).astype(NARROW)

time: 572 us -> 552 us (0.965)
  local copies, waits for them, and re-layouts: 56.2 us -> 30.4 us
  waiting for transfers between devices: 178 us -> 195 us
  other arithmetic: 58.7 us -> 52.2 us
    pallas_call x0 -> x5, Pallas kernels: none -> 37.9 us  [resident_call(): pl.pallas_call(kernel, name=name, out_shape=tuple(outs) + tuple(remote_ou...]
    pallas_call x13 -> x8, Pallas kernels: 126 us -> 91.4 us  [local_call(): pl.pallas_call(kernel, name=name, grid=(1,), out_shape=tuple(outs), in_sp...]
    unnamed x248 -> x237, local copies, waits for them, and re-layouts: 45.4 us -> 25.3 us
    ppermute x61 -> x62, waiting for transfers between devices: 71.8 us -> 81 us  [hop(): return lax.ppermute(values, axis, [(i, i ^ mask) for i in range(count)])]
    reduce_scatter x4, waiting for transfers between devices: 39.8 us -> 46.9 us  [scatter_rows(): lax.psum_scatter(values.astype(NARROW), 'tp', scatter_dimension=0, tiled=...]
    ppermute x61 -> x62, starting transfers between devices: 60.3 us -> 59.7 us  [hop(): return lax.ppermute(values, axis, [(i, i ^ mask) for i in range(count)])]
  transfers between devices with their start and end apart: 75 -> 76, of which waited for: 39 -> 40; matrix products, arithmetic and copies ran while one was open for 14% -> 12% of each run, Pallas kernels for 21% -> 23%
where the time goes in v3:
time: 552 us; the launch traced here: 546 us
  waiting for transfers between devices  195 us (35%)
  Pallas kernels  167 us (30%)
  starting transfers between devices  66.6 us (12%)
  other arithmetic  52.2 us (9%)
  local copies, waits for them, and re-layouts  30.4 us (6%)
  matrix products  18.2 us (3%)
  between operations  16.4 us (3%)
    pallas_call x8, Pallas kernels, local_call(): pl.pallas_call(kernel, name=name, grid=(1,), out_shape=tuple(outs), in_sp...  91.4 us
    ppermute x62, waiting for transfers between devices, hop(): return lax.ppermute(values, axis, [(i, i ^ mask) for i in range(count)])  81 us
    ppermute x9, waiting for transfers between devices, gather_parts(): parts.append(lax.ppermute(parts[-1], 'tp', pairs))  67.3 us
    ppermute x62, starting transfers between devices, hop(): return lax.ppermute(values, axis, [(i, i ^ mask) for i in range(count)])  59.7 us
    reduce_scatter x4, waiting for transfers between devices, scatter_rows(): lax.psum_scatter(values.astype(NARROW), 'tp', scatter_dimension=0, tiled=...  46.9 us
    pallas_call x5, Pallas kernels, resident_call(): pl.pallas_call(kernel, name=name, out_shape=tuple(outs) + tuple(remote_ou...  37.9 us
    pallas_call x8, Pallas kernels, gradient_blocks(): pl.pallas_call(kernel, name='sent' if got is None else 'kept', grid_spec=...  37.4 us
    unnamed x237, local copies, waits for them, and re-layouts  25.3 us
  transfers between devices with their start and end apart: 76, of which 40 were waited for; matrix products, arithmetic and copies ran while one was open for 12% of the time, Pallas kernels for 23%

profile of v3, /device:TPU:0, one launch (start us, length us, event | category | flops | bytes accessed | tf_op | source)
XLA Modules:
  0.0 545.7 jit_solution(4836602083025500566)
XLA Ops:
  15.9 12.0 %collective-permute-done.3.refs_1_ = bf16[128,2048]{1,0:T(8,128)(2,1)S(1)} collective-permute-done((bf16[128,2048]{1,0:T(8,128)(2,1)S(1)}, bf16[128,2048]{1,0:T(8,128)(2,1)S(1)}, u32[]{:S(2)}, u32[]{:S(2)}) %collective-permute-start.3) | collective-permute-done | bytes 524320 | tf_op jit(solution)/shard_map/ppermute | solution.py:61
  45.5 7.9 %pack.2 = (bf16[2,8,192,128]{3,2,1,0:T(8,128)(2,1)}, bf16[256,2048]{1,0:T(8,128)(2,1)}) custom-call(s32[1]{0:T(128)} %bitcast.place.seat, s32[4]{0:T(128)} %fusion.30.owners.seat, bf16[128,2048]{1,0:T(8,128)(2,1)} %copy-done.51, bf16[128,2048]{1,0:T(8,128)(2,1)} %copy-done.68, bf16[3,2048,512]{2,1,0:T(8,128)(2,1)} %weight.1, ...), custom_call_target="tpu_custom_call" | custom-call | flops 1048576 | bytes 65536 | tf_op jit(solution)/shard_map/pack/pallas_call | solution.py:314
  55.8 8.5 %pack.3 = (bf16[768,128]{1,0:T(8,128)(2,1)}, bf16[768,128]{1,0:T(8,128)(2,1)}, bf16[768,128]{1,0:T(8,128)(2,1)}, bf16[768,128]{1,0:T(8,128)(2,1)}, bf16[768,128]...) custom-call(s32[1]{0:T(128)} %bitcast.place.seat, ...), custom_call_target="tpu_custom_call" | custom-call | flops 1048576 | bytes 65536 | tf_op jit(solution)/shard_map/pack/pallas_call | solution.py:314
  71.8 9.8 %collective-permute-done.10.refs_5_ = bf16[768,128]{1,0:T(8,128)(2,1)S(1)} collective-permute-done((bf16[768,128]{1,0:T(8,128)(2,1)}, bf16[768,128]{1,0:T(8,128)(2,1)S(1)}, u32[]{:S(2)}, u32[]{:S(2)}) %collective-permute-start.10) | collective-permute-done | bytes 196640 | tf_op jit(solution)/shard_map/ppermute | solution.py:81
  86.1 30.2 %forward.1 = (bf16[64,512]{1,0:T(8,128)(2,1)}, bf16[64,512]{1,0:T(8,128)(2,1)}, bf16[64,512]{1,0:T(8,128)(2,1)}, bf16[64,512]{1,0:T(8,128)(2,1)}, bf16[64,512]{1...) custom-call(s32[18]{0:T(128)} %pad_add_fusion.1.info, ...), custom_call_target="tpu_custom_call" | custom-call | flops 1048576 | bytes 65536 | tf_op jit(solution)/shard_map/forward/pallas_call | solution.py:298
  122.8 3.8 collective-permute-done.17.refs_5_
  140.2 4.2 mixed_out.1
  156.6 8.2 %convolution_convert_fusion.1.refs_4_ = bf16[512,2048]{1,0:T(8,128)(2,1)S(1)} fusion(bf16[512,2048]{1,0:T(8,128)(2,1)S(1)} %copy-done.7, bf16[2048,2048]{1,0:T(8,128)(2,1)} %param.35), kind=kOutput, calls=%fused_computation.1 | convolution fusion | flops 4296015872 | bytes 12582912 | tf_op jit(solution)/shard_map/rd,fd->rf/dot_general | solution.py:1257
  164.9 25.2 %reduce-scatter.5.cloned.1.call-done = bf16[128,2048]{1,0:T(8,128)(2,1)} async-done(((bf16[512,2048]{1,0:T(8,128)(2,1)}), bf16[128,2048]{1,0:T(8,128)(2,1)}) %reduce-scatter.5.cloned.1.call-update) | async-done | bytes 524304 | tf_op jit(solution)/shard_map/reduce_scatter | solution.py:77
  191.8 14.4 %collective-permute-done.22.refs_1_ = bf16[128,2048]{1,0:T(8,128)(2,1)S(1)} collective-permute-done((bf16[128,2048]{1,0:T(8,128)(2,1)S(1)}, bf16[128,2048]{1,0:T(8,128)(2,1)S(1)}, u32[]{:S(2)}, u32[]{:S(2)}) %collective-permute-start.22) | collective-permute-done | bytes 524320 | tf_op jit(solution)/shard_map/ppermute | solution.py:61
  206.2 13.5 %collective-permute-done.23.refs_0_ = bf16[128,2048]{1,0:T(8,128)(2,1)S(1)} collective-permute-done((bf16[128,2048]{1,0:T(8,128)(2,1)S(1)}, bf16[128,2048]{1,0:T(8,128)(2,1)S(1)}, u32[]{:S(2)}, u32[]{:S(2)}) %collective-permute-start.23) | collective-permute-done | bytes 524320 | tf_op jit(solution)/shard_map/ppermute | solution.py:61
  223.3 5.6 %up.2 = (bf16[256,2048]{1,0:T(8,128)(2,1)S(1)}, bf16[256,2048]{1,0:T(8,128)(2,1)S(1)}, bf16[256,2048]{1,0:T(8,128)(2,1)S(1)}, f32[4,256]{1,0:T(4,128)S(1)}) custom-call(s32[4]{0:T(128)S(1)} %copy-done.38, bf16[128,2048]{1,0:T(8,128)(2,1)S(1)} %add_convert_fusion.1.refs_0_, bf16[128,2048]{1,0:T(8,128)(2,1)S(1)} %collective-permute-done.22.refs_1_, ...), custom_call_target="tpu_custom_call" | custom-call | flops 1048576 | bytes 65536 | tf_op jit(solution)/shard_map/up/pallas_call | solution.py:314
  232.5 5.7 %up.3 = (bf16[256,2048]{1,0:T(8,128)(2,1)S(1)}, bf16[256,2048]{1,0:T(8,128)(2,1)S(1)}, bf16[512,2048]{1,0:T(8,128)(2,1)S(1)}, f32[4,512]{1,0:T(4,128)S(1)}) custom-call(s32[4]{0:T(128)S(1)} %copy-done.39, bf16[128,2048]{1,0:T(8,128)(2,1)S(1)} %collective-permute-done.23.refs_0_, bf16[128,2048]{1,0:T(8,128)(2,1)S(1)} %collective-permute-done.24.refs_1_, ...), custom_call_target="tpu_custom_call" | custom-call | flops 1048576 | bytes 65536 | tf_op jit(solution)/shard_map/up/pallas_call | solution.py:314
  238.2 3.6 collective-permute-done.25
  246.4 10.2 %ffn_back.1 = (bf16[512,2048]{1,0:T(8,128)(2,1)S(1)}, bf16[512,2048]{1,0:T(8,128)(2,1)S(1)}, f32[3,2048]{1,0:T(4,128)S(1)}, bf16[512,2048]{1,0:T(8,128)(2,1)S(1)}) custom-call(s32[4]{0:T(128)S(1)} %copy-done.38, f32[4,512]{1,0:T(4,128)S(1)} %collective-permute-done.26.got, f32[4,512]{1,0:T(4,128)S(1)} %add.278.mine, ...), custom_call_target="tpu_custom_call" | custom-call | flops 1048576 | bytes 65536 | tf_op jit(solution)/shard_map/ffn_back/pallas_call | solution.py:314
  260.9 10.0 %convolution_convert_fusion = bf16[512,2048]{1,0:T(8,128)(2,1)} fusion(bf16[512,2048]{1,0:T(8,128)(2,1)} %copy-done.15, bf16[2048,2048]{1,0:T(8,128)(2,1)} %param.35), kind=kOutput, calls=%fused_computation | convolution fusion | flops 4296015872 | bytes 12582912 | tf_op jit(solution)/shard_map/dot_general | solution.py:1288
  272.4 5.1 sent.4
  277.5 5.0 sent.5
  283.0 21.7 %reduce-scatter.7.cloned.1.call-done = bf16[128,2048]{1,0:T(8,128)(2,1)} async-done(((bf16[512,2048]{1,0:T(8,128)(2,1)}), bf16[128,2048]{1,0:T(8,128)(2,1)}) %reduce-scatter.7.cloned.1.call-update) | async-done | bytes 524304 | tf_op jit(solution)/shard_map/reduce_scatter | solution.py:77
  309.8 6.3 %kept.5 = (f32[2048,256]{1,0:T(8,128)S(1)}, bf16[2,1024,256]{2,1,0:T(8,128)(2,1)S(1)}, bf16[2,1024,256]{2,1,0:T(8,128)(2,1)S(1)}, bf16[1024,256]{1,0:T(8,128)(2,1)S(1)}, bf16[1024,256]{1,0:T(8,128)(2,1)S(1)}) custom-call(s32[2]{0:T(128)S(1)} %pad_add_fusion.3.seat, bf16[512,2048]{1,0:T(8,128)(2,1)S(1)} %copy-done.17, bf16[512,2048]{1,0:T(8,128)(2,1)S(1)} %copy-done.8, ...), custom_call_target="tpu_custom_call" | custom-call | flops 1048576 | bytes 65536 | tf_op jit(solution)/shard_map/kept/pallas_call | solution.py:226
  324.0 13.2 %collective-permute-done.28.refs_2_ = bf16[128,2048]{1,0:T(8,128)(2,1)S(1)} collective-permute-done((bf16[128,2048]{1,0:T(8,128)(2,1)S(1)}, bf16[128,2048]{1,0:T(8,128)(2,1)S(1)}, u32[]{:S(2)}, u32[]{:S(2)}) %collective-permute-start.28) | collective-permute-done | bytes 524320 | tf_op jit(solution)/shard_map/ppermute | solution.py:61
  337.4 6.0 %kept.4 = (f32[1,256,2048]{2,1,0:T(8,128)S(1)}, bf16[2,1,128,2048]{3,2,1,0:T(8,128)(2,1)S(1)}, bf16[2,1,128,2048]{3,2,1,0:T(8,128)(2,1)S(1)}, bf16[1,128,2048]{2,1,0:T(8,128)(2,1)S(1)}, bf16[1,128,2048]{2,1,0:T(8,128)(2,1)S(1)}) custom-call(s32[2]{0:T(128)S(1)} %pad_add_fusion.3.seat, bf16[1,512,2048]{2,1,0:T(8,128)(2,1)S(1)} %bitcast.126, ...), custom_call_target="tpu_custom_call" | custom-call | flops 1048576 | bytes 65536 | tf_op jit(solution)/shard_map/kept/pallas_call | solution.py:226
  344.6 5.2 collective-permute-done.29.refs_3_
  384.7 35.4 %backward.1 = (bf16[768,128]{1,0:T(8,128)(2,1)}, bf16[768,128]{1,0:T(8,128)(2,1)}, bf16[768,128]{1,0:T(8,128)(2,1)}, bf16[768,128]{1,0:T(8,128)(2,1)}, bf16[768,...) custom-call(s32[18]{0:T(128)} %pad_add_fusion.1.info, ...), custom_call_target="tpu_custom_call" | custom-call | flops 1048576 | bytes 65536 | tf_op jit(solution)/shard_map/backward/pallas_call | solution.py:298
  430.2 6.6 %collective-permute-done.48.refs_2_ = bf16[768,128]{1,0:T(8,128)(2,1)S(1)} collective-permute-done((bf16[768,128]{1,0:T(8,128)(2,1)S(1)}, bf16[768,128]{1,0:T(8,128)(2,1)S(1)}, u32[]{:S(2)}, u32[]{:S(2)}) %collective-permute-start.48) | collective-permute-done | bytes 196640 | tf_op jit(solution)/shard_map/ppermute | solution.py:81
  446.1 4.1 unpack.1
  451.7 4.3 sent.7
  464.5 4.6 collective-permute-done.56
  471.0 9.6 %attn_back.1 = (bf16[512,2048]{1,0:T(8,128)(2,1)}, f32[2,2048]{1,0:T(2,128)}) custom-call(bf16[3,512,512]{2,1,0:T(8,128)(2,1)} %get-tuple-element.254.grads.left, bf16[512,2048]{1,0:T(8,128)(2,1)} %get-tuple-element.255.rows.right, f32[1,2048]{1,0:T(1,128)} %bitcast.139, f32[1,2048]{1,0:T(1,128)} %bitcast.141, bf16[3,2048,512]{2,1,0:T(8,128)(2,1)} %weight.1), custom_call_target="tpu_custom_call" | custom-call | flops 1048576 | bytes 65536 | tf_op jit(solution)/shard_map/attn_back/pallas_call | solution.py:298
  480.7 4.7 collective-permute-done.58
  487.4 6.2 %kept.7 = (f32[3,256,512]{2,1,0:T(8,128)S(1)}, bf16[2,3,128,512]{3,2,1,0:T(8,128)(2,1)S(1)}, bf16[2,3,128,512]{3,2,1,0:T(8,128)(2,1)}, bf16[3,128,512]{2,1,0:T(8,128)(2,1)S(1)}, bf16[3,128,512]{2,1,0:T(8,128)(2,1)S(1)}) custom-call(s32[2]{0:T(128)S(1)} %pad_add_fusion.3.seat, bf16[3,512,512]{2,1,0:T(8,128)(2,1)S(1)} %copy-done.4, ...), custom_call_target="tpu_custom_call" | custom-call | flops 1048576 | bytes 65536 | tf_op jit(solution)/shard_map/kept/pallas_call | solution.py:226
  508.0 6.6 %collective-permute-done.65 = bf16[2,3,128,512]{3,2,1,0:T(8,128)(2,1)S(1)} collective-permute-done((bf16[2,3,128,512]{3,2,1,0:T(8,128)(2,1)}, bf16[2,3,128,512]{3,2,1,0:T(8,128)(2,1)S(1)}, u32[]{:S(2)}, u32[]{:S(2)}) %collective-permute-start.65) | collective-permute-done | bytes 786464 | tf_op jit(solution)/shard_map/ppermute | solution.py:81
  (497 shorter events, 211.9 us)
Async XLA Ops:
  7.2 115.6 %all-gather.2.cloned.1.call-start = ((), (), s32[]{:S(2)}) async-start(), calls=%async_computation.4 | async-start | bytes 2621440 | tf_op jit(solution)/shard_map/all_gather | solution.py:49
  11.9 16.0 %collective-permute-start.3 = (bf16[128,2048]{1,0:T(8,128)(2,1)S(1)}, bf16[128,2048]{1,0:T(8,128)(2,1)S(1)}, u32[]{:S(2)}, u32[]{:S(2)}) collective-permute-start(bf16[128,2048]{1,0:T(8,128)(2,1)S(1)} %fusion.5.refs_0_), channel_id=1, source_target_pairs={{0,1},{1,3},{3,2},{2,0},{4,5},{5,7},{7,6},{6,4},{8,9},{9,11},{11,1... | collective-permute-start | bytes 1572872 | tf_op jit(solution)/shard_map/ppermute | solution.py:61
  15.8 16.7 %collective-permute-start = (s32[16]{0:T(128)S(1)}, s32[16]{0:T(128)S(1)}, u32[]{:S(2)}, u32[]{:S(2)}) collective-permute-start(s32[16]{0:T(128)S(1)} %select_reduce_fusion.2), channel_id=1, source_target_pairs={{0,4},{4,0},{8,12},{12,8},{16,20},{20,16},{24,28},{28,24},{1,5},{5... | collective-permute-start | bytes 200 | tf_op jit(solution)/shard_map/ppermute | solution.py:81
  64.3 125.7 %reduce-scatter.5.cloned.1.call-start = ((), (), s32[]{:S(2)}) async-start(), calls=%async_computation.5 | async-start | bytes 2621440 | tf_op jit(solution)/shard_map/reduce_scatter | solution.py:77
  65.9 15.8 %collective-permute-start.10 = (bf16[768,128]{1,0:T(8,128)(2,1)}, bf16[768,128]{1,0:T(8,128)(2,1)S(1)}, u32[]{:S(2)}, u32[]{:S(2)}) collective-permute-start(bf16[768,128]{1,0:T(8,128)(2,1)} %get-tuple-element.161), channel_id=1, source_target_pairs={{0,20},{4,16},{8,28},{12,24},{16,4},{20,0},{24,12},{28,8},{1,21},{... | collective-permute-start | bytes 589832 | tf_op jit(solution)/shard_map/ppermute | solution.py:81
  66.2 16.6 %collective-permute-start.11 = (bf16[768,128]{1,0:T(8,128)(2,1)}, bf16[768,128]{1,0:T(8,128)(2,1)S(1)}, u32[]{:S(2)}, u32[]{:S(2)}) collective-permute-start(bf16[768,128]{1,0:T(8,128)(2,1)} %get-tuple-element.162), channel_id=1, source_target_pairs={{0,24},{4,28},{8,16},{12,20},{16,8},{20,12},{24,0},{28,4},{1,25},{... | collective-permute-start | bytes 589832 | tf_op jit(solution)/shard_map/ppermute | solution.py:81
  67.8 15.0 %collective-permute-start.12 = (bf16[768,128]{1,0:T(8,128)(2,1)}, bf16[768,128]{1,0:T(8,128)(2,1)S(1)}, u32[]{:S(2)}, u32[]{:S(2)}) collective-permute-start(bf16[768,128]{1,0:T(8,128)(2,1)} %get-tuple-element.163), channel_id=1, source_target_pairs={{0,28},{4,24},{8,20},{12,16},{16,12},{20,8},{24,4},{28,0},{1,29},{... | collective-permute-start | bytes 589832 | tf_op jit(solution)/shard_map/ppermute | solution.py:81
  71.0 15.0 %collective-permute-start.9 = (bf16[768,128]{1,0:T(8,128)(2,1)}, bf16[768,128]{1,0:T(8,128)(2,1)}, u32[]{:S(2)}, u32[]{:S(2)}) collective-permute-start(bf16[768,128]{1,0:T(8,128)(2,1)} %get-tuple-element.160), channel_id=1, source_target_pairs={{0,16},{4,20},{8,24},{12,28},{16,0},{20,4},{24,8},{28,12},{1,17},{... | collective-permute-start | bytes 589832 | tf_op jit(solution)/shard_map/ppermute | solution.py:81
  145.7 159.0 %reduce-scatter.7.cloned.1.call-start = ((), (), s32[]{:S(2)}) async-start(), calls=%async_computation.6 | async-start | bytes 2621440 | tf_op jit(solution)/shard_map/reduce_scatter | solution.py:77
  191.8 14.4 %collective-permute-start.22 = (bf16[128,2048]{1,0:T(8,128)(2,1)S(1)}, bf16[128,2048]{1,0:T(8,128)(2,1)S(1)}, u32[]{:S(2)}, u32[]{:S(2)}) collective-permute-start(bf16[128,2048]{1,0:T(8,128)(2,1)S(1)} %add_convert_fusion.1.refs_0_), channel_id=1, source_target_pairs={{0,1},{1,3},{3,2},{2,0},{4,5},{5,7},{7,6},{6,4},{8,9},{9,11},{11,1... | collective-permute-start | bytes 1572872 | tf_op jit(solution)/shard_map/ppermute | solution.py:61
  260.7 182.4 %reduce-scatter.9.cloned.1.call-start = ((), (), s32[]{:S(2)}) async-start(), calls=%async_computation.7 | async-start | bytes 2621440 | tf_op jit(solution)/shard_map/reduce_scatter | solution.py:77
  277.5 32.3 %collective-permute-start.31 = (bf16[4,2048,256]{2,1,0:T(8,128)(2,1)}, bf16[4,2048,256]{2,1,0:T(8,128)(2,1)}, u32[]{:S(2)}, u32[]{:S(2)}) collective-permute-start(bf16[4,2048,256]{2,1,0:T(8,128)(2,1)} %sent.4), channel_id=1, source_target_pairs={{0,4},{4,0},{8,12},{12,8},{16,20},{20,16},{24,28},{28,24},{1,5},{5... | collective-permute-start | bytes 12582920 | tf_op jit(solution)/shard_map/ppermute | solution.py:81
  282.5 54.8 %collective-permute-start.30 = (bf16[4,1,256,2048]{3,2,1,0:T(8,128)(2,1)}, bf16[4,1,256,2048]{3,2,1,0:T(8,128)(2,1)}, u32[]{:S(2)}, u32[]{:S(2)}) collective-permute-start(bf16[4,1,256,2048]{3,2,1,0:T(8,128)(2,1)} %sent.5), channel_id=1, source_target_pairs={{0,4},{4,0},{8,12},{12,8},{16,20},{20,16},{24,28},{28,24},{1,5},{5... | collective-permute-start | bytes 12582920 | tf_op jit(solution)/shard_map/ppermute | solution.py:81
  309.4 14.3 %collective-permute-start.27 = (bf16[128,2048]{1,0:T(8,128)(2,1)S(1)}, bf16[128,2048]{1,0:T(8,128)(2,1)S(1)}, u32[]{:S(2)}, u32[]{:S(2)}) collective-permute-start(bf16[128,2048]{1,0:T(8,128)(2,1)S(1)} %get-tuple-element.305.refs_0_), channel_id=1, source_target_pairs={{0,1},{1,3},{3,2},{2,0},{4,5},{5,7},{7,6},{6,4},{8,9},{9,11},{11,1... | collective-permute-start | bytes 1572872 | tf_op jit(solution)/shard_map/ppermute | solution.py:61
  319.1 24.3 %collective-permute-start.32 = (bf16[2,1024,256]{2,1,0:T(8,128)(2,1)S(1)}, bf16[2,1024,256]{2,1,0:T(8,128)(2,1)S(1)}, u32[]{:S(2)}, u32[]{:S(2)}) collective-permute-start(bf16[2,1024,256]{2,1,0:T(8,128)(2,1)S(1)} %get-tuple-element.201), channel_id=1, source_target_pairs={{0,8},{4,12},{8,0},{12,4},{16,24},{20,28},{24,16},{28,20},{1,9},{5... | collective-permute-start | bytes 3145736 | tf_op jit(solution)/shard_map/ppermute | solution.py:81
  320.5 24.1 %collective-permute-start.33 = (bf16[2,1024,256]{2,1,0:T(8,128)(2,1)S(1)}, bf16[2,1024,256]{2,1,0:T(8,128)(2,1)S(1)}, u32[]{:S(2)}, u32[]{:S(2)}) collective-permute-start(bf16[2,1024,256]{2,1,0:T(8,128)(2,1)S(1)} %get-tuple-element.202), channel_id=1, source_target_pairs={{0,16},{4,20},{8,24},{12,28},{16,0},{20,4},{24,8},{28,12},{1,17},{... | collective-permute-start | bytes 3145736 | tf_op jit(solution)/shard_map/ppermute | solution.py:81
  353.6 176.7 %reduce-scatter.11.cloned.1.call-start = ((), (), s32[]{:S(2)}) async-start(), calls=%async_computation.8 | async-start | bytes 2621440 | tf_op jit(solution)/shard_map/reduce_scatter | solution.py:77
  376.5 43.6 %collective-permute-start.46 = (bf16[2,1,128,2048]{3,2,1,0:T(8,128)(2,1)}, bf16[2,1,128,2048]{3,2,1,0:T(8,128)(2,1)}, u32[]{:S(2)}, u32[]{:S(2)}) collective-permute-start(bf16[2,1,128,2048]{3,2,1,0:T(8,128)(2,1)} %copy-done.41), channel_id=1, source_target_pairs={{0,16},{4,20},{8,24},{12,28},{16,0},{20,4},{24,8},{28,12},{1,17},{... | collective-permute-start | bytes 3145736 | tf_op jit(solution)/shard_map/ppermute | solution.py:81
  378.0 42.1 %collective-permute-start.45 = (bf16[2,1,128,2048]{3,2,1,0:T(8,128)(2,1)}, bf16[2,1,128,2048]{3,2,1,0:T(8,128)(2,1)}, u32[]{:S(2)}, u32[]{:S(2)}) collective-permute-start(bf16[2,1,128,2048]{3,2,1,0:T(8,128)(2,1)} %copy-done.40), channel_id=1, source_target_pairs={{0,8},{4,12},{8,0},{12,4},{16,24},{20,28},{24,16},{28,20},{1,9},{5... | collective-permute-start | bytes 3145736 | tf_op jit(solution)/shard_map/ppermute | solution.py:81
  381.1 39.0 %collective-permute-start.44 = (bf16[1024,256]{1,0:T(8,128)(2,1)}, bf16[1024,256]{1,0:T(8,128)(2,1)}, u32[]{:S(2)}, u32[]{:S(2)}) collective-permute-start(bf16[1024,256]{1,0:T(8,128)(2,1)} %fusion.15), channel_id=1, source_target_pairs={{0,8},{4,12},{8,0},{12,4},{16,24},{20,28},{24,16},{28,20},{1,9},{5... | collective-permute-start | bytes 1572872 | tf_op jit(solution)/shard_map/ppermute | solution.py:81
  384.1 36.0 %collective-permute-start.43 = (bf16[1024,256]{1,0:T(8,128)(2,1)}, bf16[1024,256]{1,0:T(8,128)(2,1)S(1)}, u32[]{:S(2)}, u32[]{:S(2)}) collective-permute-start(bf16[1024,256]{1,0:T(8,128)(2,1)} %fusion.16), channel_id=1, source_target_pairs={{0,16},{4,20},{8,24},{12,28},{16,0},{20,4},{24,8},{28,12},{1,17},{... | collective-permute-start | bytes 1572872 | tf_op jit(solution)/shard_map/ppermute | solution.py:81
  422.4 14.9 %collective-permute-start.47 = (bf16[4,512,256]{2,1,0:T(8,128)(2,1)S(1)}, bf16[4,512,256]{2,1,0:T(8,128)(2,1)S(1)}, u32[]{:S(2)}, u32[]{:S(2)}) collective-permute-start(bf16[4,512,256]{2,1,0:T(8,128)(2,1)S(1)} %sent.6), channel_id=1, source_target_pairs={{0,4},{4,0},{8,12},{12,8},{16,20},{20,16},{24,28},{28,24},{1,5},{5... | collective-permute-start | bytes 3145736 | tf_op jit(solution)/shard_map/ppermute | solution.py:81
  423.9 18.0 %collective-permute-start.54 = (bf16[768,128]{1,0:T(8,128)(2,1)S(1)}, bf16[768,128]{1,0:T(8,128)(2,1)}, u32[]{:S(2)}, u32[]{:S(2)}) collective-permute-start(bf16[768,128]{1,0:T(8,128)(2,1)S(1)} %copy-done.112), channel_id=1, source_target_pairs={{0,28},{4,24},{8,20},{12,16},{16,12},{20,8},{24,4},{28,0},{1,29},{... | collective-permute-start | bytes 589832 | tf_op jit(solution)/shard_map/ppermute | solution.py:81
  428.4 17.0 %collective-permute-start.53 = (bf16[768,128]{1,0:T(8,128)(2,1)}, bf16[768,128]{1,0:T(8,128)(2,1)}, u32[]{:S(2)}, u32[]{:S(2)}) collective-permute-start(bf16[768,128]{1,0:T(8,128)(2,1)} %get-tuple-element.251), channel_id=1, source_target_pairs={{0,24},{4,28},{8,16},{12,20},{16,8},{20,12},{24,0},{28,4},{1,25},{... | collective-permute-start | bytes 589832 | tf_op jit(solution)/shard_map/ppermute | solution.py:81
  429.6 15.8 %collective-permute-start.52 = (bf16[768,128]{1,0:T(8,128)(2,1)}, bf16[768,128]{1,0:T(8,128)(2,1)}, u32[]{:S(2)}, u32[]{:S(2)}) collective-permute-start(bf16[768,128]{1,0:T(8,128)(2,1)} %get-tuple-element.249), channel_id=1, source_target_pairs={{0,20},{4,16},{8,28},{12,24},{16,4},{20,0},{24,12},{28,8},{1,21},{... | collective-permute-start | bytes 589832 | tf_op jit(solution)/shard_map/ppermute | solution.py:81
  456.0 31.4 %collective-permute-start.55 = (bf16[4,3,256,512]{3,2,1,0:T(8,128)(2,1)}, bf16[4,3,256,512]{3,2,1,0:T(8,128)(2,1)}, u32[]{:S(2)}, u32[]{:S(2)}) collective-permute-start(bf16[4,3,256,512]{3,2,1,0:T(8,128)(2,1)} %sent.7), channel_id=1, source_target_pairs={{0,4},{4,0},{8,12},{12,8},{16,20},{20,16},{24,28},{28,24},{1,5},{5... | collective-permute-start | bytes 9437192 | tf_op jit(solution)/shard_map/ppermute | solution.py:81
  458.5 28.9 %collective-permute-start.59 = (bf16[1,128,2048]{2,1,0:T(8,128)(2,1)}, bf16[1,128,2048]{2,1,0:T(8,128)(2,1)}, u32[]{:S(2)}, u32[]{:S(2)}) collective-permute-start(bf16[1,128,2048]{2,1,0:T(8,128)(2,1)} %fusion.14), channel_id=1, source_target_pairs={{0,16},{4,20},{8,24},{12,28},{16,0},{20,4},{24,8},{28,12},{1,17},{... | collective-permute-start | bytes 1572872 | tf_op jit(solution)/shard_map/ppermute | solution.py:81
  462.7 24.6 %collective-permute-start.60 = (bf16[1,128,2048]{2,1,0:T(8,128)(2,1)}, bf16[1,128,2048]{2,1,0:T(8,128)(2,1)}, u32[]{:S(2)}, u32[]{:S(2)}) collective-permute-start(bf16[1,128,2048]{2,1,0:T(8,128)(2,1)} %fusion.13), channel_id=1, source_target_pairs={{0,8},{4,12},{8,0},{12,4},{16,24},{20,28},{24,16},{28,20},{1,9},{5... | collective-permute-start | bytes 1572872 | tf_op jit(solution)/shard_map/ppermute | solution.py:81
  463.7 16.9 %collective-permute-start.57 = (bf16[512,256]{1,0:T(8,128)(2,1)S(1)}, bf16[512,256]{1,0:T(8,128)(2,1)}, u32[]{:S(2)}, u32[]{:S(2)}) collective-permute-start(bf16[512,256]{1,0:T(8,128)(2,1)S(1)} %copy-done.44), channel_id=1, source_target_pairs={{0,16},{4,20},{8,24},{12,28},{16,0},{20,4},{24,8},{28,12},{1,17},{... | collective-permute-start | bytes 786440 | tf_op jit(solution)/shard_map/ppermute | solution.py:81
  469.1 16.3 %collective-permute-start.58 = (bf16[512,256]{1,0:T(8,128)(2,1)S(1)}, bf16[512,256]{1,0:T(8,128)(2,1)}, u32[]{:S(2)}, u32[]{:S(2)}) collective-permute-start(bf16[512,256]{1,0:T(8,128)(2,1)S(1)} %get-tuple-element.263), channel_id=1, source_target_pairs={{0,24},{4,28},{8,16},{12,20},{16,8},{20,12},{24,0},{28,4},{1,25},{... | collective-permute-start | bytes 786440 | tf_op jit(solution)/shard_map/ppermute | solution.py:81
  495.7 18.9 %collective-permute-start.65 = (bf16[2,3,128,512]{3,2,1,0:T(8,128)(2,1)}, bf16[2,3,128,512]{3,2,1,0:T(8,128)(2,1)S(1)}, u32[]{:S(2)}, u32[]{:S(2)}) collective-permute-start(bf16[2,3,128,512]{3,2,1,0:T(8,128)(2,1)} %get-tuple-element.276), channel_id=1, source_target_pairs={{0,16},{4,20},{8,24},{12,28},{16,0},{20,4},{24,8},{28,12},{1,17},{... | collective-permute-start | bytes 2359304 | tf_op jit(solution)/shard_map/ppermute | solution.py:81
  497.0 18.6 %collective-permute-start.64 = (bf16[2,3,128,512]{3,2,1,0:T(8,128)(2,1)}, bf16[2,3,128,512]{3,2,1,0:T(8,128)(2,1)S(1)}, u32[]{:S(2)}, u32[]{:S(2)}) collective-permute-start(bf16[2,3,128,512]{3,2,1,0:T(8,128)(2,1)} %copy-done.42), channel_id=1, source_target_pairs={{0,8},{4,12},{8,0},{12,4},{16,24},{20,28},{24,16},{28,20},{1,9},{5... | collective-permute-start | bytes 2359304 | tf_op jit(solution)/shard_map/ppermute | solution.py:81
  (160 other events, 1950.4 us)
Sparse Core Ops, SparseCore 0:
  64.5 46.5 all-gather.1
  145.8 44.1 reduce-scatter.4
  260.9 43.8 reduce-scatter.6
  353.7 44.0 reduce-scatter.8
  480.8 45.0 reduce-scatter.10

commit v4 on v3

--- a/solution.py
+++ b/solution.py
@@ -563,19 +563,31 @@
 
         def step(kb, carry, masked):
             top, total, accum = carry
-            raw = jnp.dot(keys[kb], query, preferred_element_type=WIDE)
-            if masked:
-                raw = jnp.where(
-                    allowed_mask(kb * block, here * block, begins, raw.shape), raw, OUTSIDE
+            cuts = [slice(i * block // 4, (i + 1) * block // 4) for i in range(4)]
+            raws = [
+                jnp.dot(keys[kb], query[:, cut], preferred_element_type=WIDE) for cut in cuts
+            ]
+            results = []
+            for cut, raw in zip(cuts, raws):
+                if masked:
+                    mask = allowed_mask(
+                        kb * block, here * block + cut.start, begins[:, cut], raw.shape
+                    )
+                    raw = jnp.where(mask, raw, OUTSIDE)
+                fresh = jnp.maximum(
+                    top[:, cut], jnp.max(raw, axis=0, keepdims=True) * (SCALE * LOG2E)
                 )
-            fresh = jnp.maximum(top, jnp.max(raw, axis=0, keepdims=True) * (SCALE * LOG2E))
-            kept = jnp.exp2(raw * (SCALE * LOG2E) - fresh)
-            fade = jnp.exp2(top - fresh)
-            total = total * fade + jnp.sum(kept, axis=0, keepdims=True)
-            accum = accum * fade + jnp.dot(
-                values[kb], kept.astype(NARROW), preferred_element_type=WIDE
-            )
-            return fresh, total, accum
+                kept = jnp.exp2(raw * (SCALE * LOG2E) - fresh)
+                fade = jnp.exp2(top[:, cut] - fresh)
+                results.append(
+                    (
+                        fresh,
+                        total[:, cut] * fade + jnp.sum(kept, axis=0, keepdims=True),
+                        accum[:, cut] * fade
+                        + jnp.dot(values[kb], kept.astype(NARROW), preferred_element_type=WIDE),
+                    )
+                )
+            return tuple(jnp.concatenate(item, axis=1) for item in zip(*results))
 
         carry = (
             jnp.full((1, block), LOWEST, WIDE),

time: 552 us -> 551 us (level)
  transfers between devices with their start and end apart: 76 -> 76, of which waited for: 40 -> 39; matrix products, arithmetic and copies ran while one was open for 12% -> 12% of each run, Pallas kernels for 23% -> 23%
where the time goes in v4:
time: 551 us; the launch traced here: 544 us
  waiting for transfers between devices  196 us (36%)
  Pallas kernels  165 us (30%)
  starting transfers between devices  65.6 us (12%)
  other arithmetic  52.2 us (9%)
  local copies, waits for them, and re-layouts  30.4 us (6%)
  matrix products  18.2 us (3%)
  between operations  16.4 us (3%)
    pallas_call x8, Pallas kernels, local_call(): pl.pallas_call(kernel, name=name, grid=(1,), out_shape=tuple(outs), in_sp...  89.7 us
    ppermute x62, waiting for transfers between devices, hop(): return lax.ppermute(values, axis, [(i, i ^ mask) for i in range(count)])  81.6 us
    ppermute x9, waiting for transfers between devices, gather_parts(): parts.append(lax.ppermute(parts[-1], 'tp', pairs))  67.8 us
    ppermute x62, starting transfers between devices, hop(): return lax.ppermute(values, axis, [(i, i ^ mask) for i in range(count)])  59.2 us
    reduce_scatter x4, waiting for transfers between devices, scatter_rows(): lax.psum_scatter(values.astype(NARROW), 'tp', scatter_dimension=0, tiled=...  46.9 us
    pallas_call x5, Pallas kernels, resident_call(): pl.pallas_call(kernel, name=name, out_shape=tuple(outs) + tuple(remote_ou...  37.9 us
    pallas_call x8, Pallas kernels, gradient_blocks(): pl.pallas_call(kernel, name='sent' if got is None else 'kept', grid_spec=...  37.4 us
    unnamed x237, local copies, waits for them, and re-layouts  25.2 us
  transfers between devices with their start and end apart: 76, of which 39 were waited for; matrix products, arithmetic and copies ran while one was open for 12% of the time, Pallas kernels for 23%

profile of v4, /device:TPU:0, one launch (start us, length us, event | category | flops | bytes accessed | tf_op | source)
XLA Modules:
  0.0 544.1 jit_solution(5582527930962479650)
XLA Ops:
  15.9 12.0 %collective-permute-done.3.refs_1_ = bf16[128,2048]{1,0:T(8,128)(2,1)S(1)} collective-permute-done((bf16[128,2048]{1,0:T(8,128)(2,1)S(1)}, bf16[128,2048]{1,0:T(8,128)(2,1)S(1)}, u32[]{:S(2)}, u32[]{:S(2)}) %collective-permute-start.3) | collective-permute-done | bytes 524320 | tf_op jit(solution)/shard_map/ppermute | solution.py:61
  45.5 7.9 %pack.2 = (bf16[2,8,192,128]{3,2,1,0:T(8,128)(2,1)}, bf16[256,2048]{1,0:T(8,128)(2,1)}) custom-call(s32[1]{0:T(128)} %bitcast.place.seat, s32[4]{0:T(128)} %fusion.30.owners.seat, bf16[128,2048]{1,0:T(8,128)(2,1)} %copy-done.51, bf16[128,2048]{1,0:T(8,128)(2,1)} %copy-done.68, bf16[3,2048,512]{2,1,0:T(8,128)(2,1)} %weight.1, ...), custom_call_target="tpu_custom_call" | custom-call | flops 1048576 | bytes 65536 | tf_op jit(solution)/shard_map/pack/pallas_call | solution.py:314
  55.8 8.5 %pack.3 = (bf16[768,128]{1,0:T(8,128)(2,1)}, bf16[768,128]{1,0:T(8,128)(2,1)}, bf16[768,128]{1,0:T(8,128)(2,1)}, bf16[768,128]{1,0:T(8,128)(2,1)}, bf16[768,128]...) custom-call(s32[1]{0:T(128)} %bitcast.place.seat, ...), custom_call_target="tpu_custom_call" | custom-call | flops 1048576 | bytes 65536 | tf_op jit(solution)/shard_map/pack/pallas_call | solution.py:314
  71.8 9.8 %collective-permute-done.10.refs_5_ = bf16[768,128]{1,0:T(8,128)(2,1)S(1)} collective-permute-done((bf16[768,128]{1,0:T(8,128)(2,1)}, bf16[768,128]{1,0:T(8,128)(2,1)S(1)}, u32[]{:S(2)}, u32[]{:S(2)}) %collective-permute-start.10) | collective-permute-done | bytes 196640 | tf_op jit(solution)/shard_map/ppermute | solution.py:81
  86.1 28.5 %forward.1 = (bf16[64,512]{1,0:T(8,128)(2,1)}, bf16[64,512]{1,0:T(8,128)(2,1)}, bf16[64,512]{1,0:T(8,128)(2,1)}, bf16[64,512]{1,0:T(8,128)(2,1)}, bf16[64,512]{1...) custom-call(s32[18]{0:T(128)} %pad_add_fusion.1.info, ...), custom_call_target="tpu_custom_call" | custom-call | flops 1048576 | bytes 65536 | tf_op jit(solution)/shard_map/forward/pallas_call | solution.py:298
  121.2 3.8 collective-permute-done.17.refs_5_
  138.5 4.2 mixed_out.1
  154.9 8.2 %convolution_convert_fusion.1.refs_4_ = bf16[512,2048]{1,0:T(8,128)(2,1)S(1)} fusion(bf16[512,2048]{1,0:T(8,128)(2,1)S(1)} %copy-done.7, bf16[2048,2048]{1,0:T(8,128)(2,1)} %param.35), kind=kOutput, calls=%fused_computation.1 | convolution fusion | flops 4296015872 | bytes 12582912 | tf_op jit(solution)/shard_map/rd,fd->rf/dot_general | solution.py:1269
  163.2 25.2 %reduce-scatter.5.cloned.1.call-done = bf16[128,2048]{1,0:T(8,128)(2,1)} async-done(((bf16[512,2048]{1,0:T(8,128)(2,1)}), bf16[128,2048]{1,0:T(8,128)(2,1)}) %reduce-scatter.5.cloned.1.call-update) | async-done | bytes 524304 | tf_op jit(solution)/shard_map/reduce_scatter | solution.py:77
  190.2 14.4 %collective-permute-done.22.refs_1_ = bf16[128,2048]{1,0:T(8,128)(2,1)S(1)} collective-permute-done((bf16[128,2048]{1,0:T(8,128)(2,1)S(1)}, bf16[128,2048]{1,0:T(8,128)(2,1)S(1)}, u32[]{:S(2)}, u32[]{:S(2)}) %collective-permute-start.22) | collective-permute-done | bytes 524320 | tf_op jit(solution)/shard_map/ppermute | solution.py:61
  204.6 13.5 %collective-permute-done.23.refs_0_ = bf16[128,2048]{1,0:T(8,128)(2,1)S(1)} collective-permute-done((bf16[128,2048]{1,0:T(8,128)(2,1)S(1)}, bf16[128,2048]{1,0:T(8,128)(2,1)S(1)}, u32[]{:S(2)}, u32[]{:S(2)}) %collective-permute-start.23) | collective-permute-done | bytes 524320 | tf_op jit(solution)/shard_map/ppermute | solution.py:61
  221.7 5.6 %up.2 = (bf16[256,2048]{1,0:T(8,128)(2,1)S(1)}, bf16[256,2048]{1,0:T(8,128)(2,1)S(1)}, bf16[256,2048]{1,0:T(8,128)(2,1)S(1)}, f32[4,256]{1,0:T(4,128)S(1)}) custom-call(s32[4]{0:T(128)S(1)} %copy-done.38, bf16[128,2048]{1,0:T(8,128)(2,1)S(1)} %add_convert_fusion.1.refs_0_, bf16[128,2048]{1,0:T(8,128)(2,1)S(1)} %collective-permute-done.22.refs_1_, ...), custom_call_target="tpu_custom_call" | custom-call | flops 1048576 | bytes 65536 | tf_op jit(solution)/shard_map/up/pallas_call | solution.py:314
  230.8 5.7 %up.3 = (bf16[256,2048]{1,0:T(8,128)(2,1)S(1)}, bf16[256,2048]{1,0:T(8,128)(2,1)S(1)}, bf16[512,2048]{1,0:T(8,128)(2,1)S(1)}, f32[4,512]{1,0:T(4,128)S(1)}) custom-call(s32[4]{0:T(128)S(1)} %copy-done.39, bf16[128,2048]{1,0:T(8,128)(2,1)S(1)} %collective-permute-done.23.refs_0_, bf16[128,2048]{1,0:T(8,128)(2,1)S(1)} %collective-permute-done.24.refs_1_, ...), custom_call_target="tpu_custom_call" | custom-call | flops 1048576 | bytes 65536 | tf_op jit(solution)/shard_map/up/pallas_call | solution.py:314
  236.6 3.6 collective-permute-done.25
  244.8 10.2 %ffn_back.1 = (bf16[512,2048]{1,0:T(8,128)(2,1)S(1)}, bf16[512,2048]{1,0:T(8,128)(2,1)S(1)}, f32[3,2048]{1,0:T(4,128)S(1)}, bf16[512,2048]{1,0:T(8,128)(2,1)S(1)}) custom-call(s32[4]{0:T(128)S(1)} %copy-done.38, f32[4,512]{1,0:T(4,128)S(1)} %collective-permute-done.26.got, f32[4,512]{1,0:T(4,128)S(1)} %add.278.mine, ...), custom_call_target="tpu_custom_call" | custom-call | flops 1048576 | bytes 65536 | tf_op jit(solution)/shard_map/ffn_back/pallas_call | solution.py:314
  259.2 10.0 %convolution_convert_fusion = bf16[512,2048]{1,0:T(8,128)(2,1)} fusion(bf16[512,2048]{1,0:T(8,128)(2,1)} %copy-done.15, bf16[2048,2048]{1,0:T(8,128)(2,1)} %param.35), kind=kOutput, calls=%fused_computation | convolution fusion | flops 4296015872 | bytes 12582912 | tf_op jit(solution)/shard_map/dot_general | solution.py:1300
  270.7 5.1 sent.4
  275.8 5.0 sent.5
  281.3 21.7 %reduce-scatter.7.cloned.1.call-done = bf16[128,2048]{1,0:T(8,128)(2,1)} async-done(((bf16[512,2048]{1,0:T(8,128)(2,1)}), bf16[128,2048]{1,0:T(8,128)(2,1)}) %reduce-scatter.7.cloned.1.call-update) | async-done | bytes 524304 | tf_op jit(solution)/shard_map/reduce_scatter | solution.py:77
  307.8 6.3 %kept.5 = (f32[2048,256]{1,0:T(8,128)S(1)}, bf16[2,1024,256]{2,1,0:T(8,128)(2,1)S(1)}, bf16[2,1024,256]{2,1,0:T(8,128)(2,1)S(1)}, bf16[1024,256]{1,0:T(8,128)(2,1)S(1)}, bf16[1024,256]{1,0:T(8,128)(2,1)S(1)}) custom-call(s32[2]{0:T(128)S(1)} %pad_add_fusion.3.seat, bf16[512,2048]{1,0:T(8,128)(2,1)S(1)} %copy-done.17, bf16[512,2048]{1,0:T(8,128)(2,1)S(1)} %copy-done.8, ...), custom_call_target="tpu_custom_call" | custom-call | flops 1048576 | bytes 65536 | tf_op jit(solution)/shard_map/kept/pallas_call | solution.py:226
  322.2 13.4 %collective-permute-done.28.refs_2_ = bf16[128,2048]{1,0:T(8,128)(2,1)S(1)} collective-permute-done((bf16[128,2048]{1,0:T(8,128)(2,1)S(1)}, bf16[128,2048]{1,0:T(8,128)(2,1)S(1)}, u32[]{:S(2)}, u32[]{:S(2)}) %collective-permute-start.28) | collective-permute-done | bytes 524320 | tf_op jit(solution)/shard_map/ppermute | solution.py:61
  335.8 6.0 %kept.4 = (f32[1,256,2048]{2,1,0:T(8,128)S(1)}, bf16[2,1,128,2048]{3,2,1,0:T(8,128)(2,1)S(1)}, bf16[2,1,128,2048]{3,2,1,0:T(8,128)(2,1)S(1)}, bf16[1,128,2048]{2,1,0:T(8,128)(2,1)S(1)}, bf16[1,128,2048]{2,1,0:T(8,128)(2,1)S(1)}) custom-call(s32[2]{0:T(128)S(1)} %pad_add_fusion.3.seat, bf16[1,512,2048]{2,1,0:T(8,128)(2,1)S(1)} %bitcast.126, ...), custom_call_target="tpu_custom_call" | custom-call | flops 1048576 | bytes 65536 | tf_op jit(solution)/shard_map/kept/pallas_call | solution.py:226
  343.0 5.4 collective-permute-done.29.refs_3_
  383.0 35.4 %backward.1 = (bf16[768,128]{1,0:T(8,128)(2,1)}, bf16[768,128]{1,0:T(8,128)(2,1)}, bf16[768,128]{1,0:T(8,128)(2,1)}, bf16[768,128]{1,0:T(8,128)(2,1)}, bf16[768,...) custom-call(s32[18]{0:T(128)} %pad_add_fusion.1.info, ...), custom_call_target="tpu_custom_call" | custom-call | flops 1048576 | bytes 65536 | tf_op jit(solution)/shard_map/backward/pallas_call | solution.py:298
  428.4 6.2 %collective-permute-done.48.refs_2_ = bf16[768,128]{1,0:T(8,128)(2,1)S(1)} collective-permute-done((bf16[768,128]{1,0:T(8,128)(2,1)S(1)}, bf16[768,128]{1,0:T(8,128)(2,1)S(1)}, u32[]{:S(2)}, u32[]{:S(2)}) %collective-permute-start.48) | collective-permute-done | bytes 196640 | tf_op jit(solution)/shard_map/ppermute | solution.py:81
  444.6 4.1 unpack.1
  450.1 4.3 sent.7
  462.9 4.4 collective-permute-done.56
  469.2 9.6 %attn_back.1 = (bf16[512,2048]{1,0:T(8,128)(2,1)}, f32[2,2048]{1,0:T(2,128)}) custom-call(bf16[3,512,512]{2,1,0:T(8,128)(2,1)} %get-tuple-element.254.grads.left, bf16[512,2048]{1,0:T(8,128)(2,1)} %get-tuple-element.255.rows.right, f32[1,2048]{1,0:T(1,128)} %bitcast.139, f32[1,2048]{1,0:T(1,128)} %bitcast.141, bf16[3,2048,512]{2,1,0:T(8,128)(2,1)} %weight.1), custom_call_target="tpu_custom_call" | custom-call | flops 1048576 | bytes 65536 | tf_op jit(solution)/shard_map/attn_back/pallas_call | solution.py:298
  478.8 5.0 collective-permute-done.58
  485.8 6.2 %kept.7 = (f32[3,256,512]{2,1,0:T(8,128)S(1)}, bf16[2,3,128,512]{3,2,1,0:T(8,128)(2,1)S(1)}, bf16[2,3,128,512]{3,2,1,0:T(8,128)(2,1)}, bf16[3,128,512]{2,1,0:T(8,128)(2,1)S(1)}, bf16[3,128,512]{2,1,0:T(8,128)(2,1)S(1)}) custom-call(s32[2]{0:T(128)S(1)} %pad_add_fusion.3.seat, bf16[3,512,512]{2,1,0:T(8,128)(2,1)S(1)} %copy-done.4, ...), custom_call_target="tpu_custom_call" | custom-call | flops 1048576 | bytes 65536 | tf_op jit(solution)/shard_map/kept/pallas_call | solution.py:226
  506.3 6.7 %collective-permute-done.65 = bf16[2,3,128,512]{3,2,1,0:T(8,128)(2,1)S(1)} collective-permute-done((bf16[2,3,128,512]{3,2,1,0:T(8,128)(2,1)}, bf16[2,3,128,512]{3,2,1,0:T(8,128)(2,1)S(1)}, u32[]{:S(2)}, u32[]{:S(2)}) %collective-permute-start.65) | collective-permute-done | bytes 786464 | tf_op jit(solution)/shard_map/ppermute | solution.py:81
  (497 shorter events, 211.8 us)
Async XLA Ops:
  7.2 114.0 %all-gather.2.cloned.1.call-start = ((), (), s32[]{:S(2)}) async-start(), calls=%async_computation.4 | async-start | bytes 2621440 | tf_op jit(solution)/shard_map/all_gather | solution.py:49
  11.9 16.0 %collective-permute-start.3 = (bf16[128,2048]{1,0:T(8,128)(2,1)S(1)}, bf16[128,2048]{1,0:T(8,128)(2,1)S(1)}, u32[]{:S(2)}, u32[]{:S(2)}) collective-permute-start(bf16[128,2048]{1,0:T(8,128)(2,1)S(1)} %fusion.5.refs_0_), channel_id=1, source_target_pairs={{0,1},{1,3},{3,2},{2,0},{4,5},{5,7},{7,6},{6,4},{8,9},{9,11},{11,1... | collective-permute-start | bytes 1572872 | tf_op jit(solution)/shard_map/ppermute | solution.py:61
  15.8 16.7 %collective-permute-start = (s32[16]{0:T(128)S(1)}, s32[16]{0:T(128)S(1)}, u32[]{:S(2)}, u32[]{:S(2)}) collective-permute-start(s32[16]{0:T(128)S(1)} %select_reduce_fusion.2), channel_id=1, source_target_pairs={{0,4},{4,0},{8,12},{12,8},{16,20},{20,16},{24,28},{28,24},{1,5},{5... | collective-permute-start | bytes 200 | tf_op jit(solution)/shard_map/ppermute | solution.py:81
  64.3 124.0 %reduce-scatter.5.cloned.1.call-start = ((), (), s32[]{:S(2)}) async-start(), calls=%async_computation.5 | async-start | bytes 2621440 | tf_op jit(solution)/shard_map/reduce_scatter | solution.py:77
  65.9 15.8 %collective-permute-start.10 = (bf16[768,128]{1,0:T(8,128)(2,1)}, bf16[768,128]{1,0:T(8,128)(2,1)S(1)}, u32[]{:S(2)}, u32[]{:S(2)}) collective-permute-start(bf16[768,128]{1,0:T(8,128)(2,1)} %get-tuple-element.161), channel_id=1, source_target_pairs={{0,20},{4,16},{8,28},{12,24},{16,4},{20,0},{24,12},{28,8},{1,21},{... | collective-permute-start | bytes 589832 | tf_op jit(solution)/shard_map/ppermute | solution.py:81
  66.2 16.6 %collective-permute-start.11 = (bf16[768,128]{1,0:T(8,128)(2,1)}, bf16[768,128]{1,0:T(8,128)(2,1)S(1)}, u32[]{:S(2)}, u32[]{:S(2)}) collective-permute-start(bf16[768,128]{1,0:T(8,128)(2,1)} %get-tuple-element.162), channel_id=1, source_target_pairs={{0,24},{4,28},{8,16},{12,20},{16,8},{20,12},{24,0},{28,4},{1,25},{... | collective-permute-start | bytes 589832 | tf_op jit(solution)/shard_map/ppermute | solution.py:81
  67.8 15.0 %collective-permute-start.12 = (bf16[768,128]{1,0:T(8,128)(2,1)}, bf16[768,128]{1,0:T(8,128)(2,1)S(1)}, u32[]{:S(2)}, u32[]{:S(2)}) collective-permute-start(bf16[768,128]{1,0:T(8,128)(2,1)} %get-tuple-element.163), channel_id=1, source_target_pairs={{0,28},{4,24},{8,20},{12,16},{16,12},{20,8},{24,4},{28,0},{1,29},{... | collective-permute-start | bytes 589832 | tf_op jit(solution)/shard_map/ppermute | solution.py:81
  71.0 15.0 %collective-permute-start.9 = (bf16[768,128]{1,0:T(8,128)(2,1)}, bf16[768,128]{1,0:T(8,128)(2,1)}, u32[]{:S(2)}, u32[]{:S(2)}) collective-permute-start(bf16[768,128]{1,0:T(8,128)(2,1)} %get-tuple-element.160), channel_id=1, source_target_pairs={{0,16},{4,20},{8,24},{12,28},{16,0},{20,4},{24,8},{28,12},{1,17},{... | collective-permute-start | bytes 589832 | tf_op jit(solution)/shard_map/ppermute | solution.py:81
  144.0 159.0 %reduce-scatter.7.cloned.1.call-start = ((), (), s32[]{:S(2)}) async-start(), calls=%async_computation.6 | async-start | bytes 2621440 | tf_op jit(solution)/shard_map/reduce_scatter | solution.py:77
  190.1 14.4 %collective-permute-start.22 = (bf16[128,2048]{1,0:T(8,128)(2,1)S(1)}, bf16[128,2048]{1,0:T(8,128)(2,1)S(1)}, u32[]{:S(2)}, u32[]{:S(2)}) collective-permute-start(bf16[128,2048]{1,0:T(8,128)(2,1)S(1)} %add_convert_fusion.1.refs_0_), channel_id=1, source_target_pairs={{0,1},{1,3},{3,2},{2,0},{4,5},{5,7},{7,6},{6,4},{8,9},{9,11},{11,1... | collective-permute-start | bytes 1572872 | tf_op jit(solution)/shard_map/ppermute | solution.py:61
  259.0 182.5 %reduce-scatter.9.cloned.1.call-start = ((), (), s32[]{:S(2)}) async-start(), calls=%async_computation.7 | async-start | bytes 2621440 | tf_op jit(solution)/shard_map/reduce_scatter | solution.py:77
  275.8 31.9 %collective-permute-start.31 = (bf16[4,2048,256]{2,1,0:T(8,128)(2,1)}, bf16[4,2048,256]{2,1,0:T(8,128)(2,1)}, u32[]{:S(2)}, u32[]{:S(2)}) collective-permute-start(bf16[4,2048,256]{2,1,0:T(8,128)(2,1)} %sent.4), channel_id=1, source_target_pairs={{0,4},{4,0},{8,12},{12,8},{16,20},{20,16},{24,28},{28,24},{1,5},{5... | collective-permute-start | bytes 12582920 | tf_op jit(solution)/shard_map/ppermute | solution.py:81
  280.8 55.0 %collective-permute-start.30 = (bf16[4,1,256,2048]{3,2,1,0:T(8,128)(2,1)}, bf16[4,1,256,2048]{3,2,1,0:T(8,128)(2,1)}, u32[]{:S(2)}, u32[]{:S(2)}) collective-permute-start(bf16[4,1,256,2048]{3,2,1,0:T(8,128)(2,1)} %sent.5), channel_id=1, source_target_pairs={{0,4},{4,0},{8,12},{12,8},{16,20},{20,16},{24,28},{28,24},{1,5},{5... | collective-permute-start | bytes 12582920 | tf_op jit(solution)/shard_map/ppermute | solution.py:81
  307.7 14.4 %collective-permute-start.27 = (bf16[128,2048]{1,0:T(8,128)(2,1)S(1)}, bf16[128,2048]{1,0:T(8,128)(2,1)S(1)}, u32[]{:S(2)}, u32[]{:S(2)}) collective-permute-start(bf16[128,2048]{1,0:T(8,128)(2,1)S(1)} %get-tuple-element.305.refs_0_), channel_id=1, source_target_pairs={{0,1},{1,3},{3,2},{2,0},{4,5},{5,7},{7,6},{6,4},{8,9},{9,11},{11,1... | collective-permute-start | bytes 1572872 | tf_op jit(solution)/shard_map/ppermute | solution.py:61
  317.0 24.8 %collective-permute-start.32 = (bf16[2,1024,256]{2,1,0:T(8,128)(2,1)S(1)}, bf16[2,1024,256]{2,1,0:T(8,128)(2,1)S(1)}, u32[]{:S(2)}, u32[]{:S(2)}) collective-permute-start(bf16[2,1024,256]{2,1,0:T(8,128)(2,1)S(1)} %get-tuple-element.201), channel_id=1, source_target_pairs={{0,8},{4,12},{8,0},{12,4},{16,24},{20,28},{24,16},{28,20},{1,9},{5... | collective-permute-start | bytes 3145736 | tf_op jit(solution)/shard_map/ppermute | solution.py:81
  318.5 24.5 %collective-permute-start.33 = (bf16[2,1024,256]{2,1,0:T(8,128)(2,1)S(1)}, bf16[2,1024,256]{2,1,0:T(8,128)(2,1)S(1)}, u32[]{:S(2)}, u32[]{:S(2)}) collective-permute-start(bf16[2,1024,256]{2,1,0:T(8,128)(2,1)S(1)} %get-tuple-element.202), channel_id=1, source_target_pairs={{0,16},{4,20},{8,24},{12,28},{16,0},{20,4},{24,8},{28,12},{1,17},{... | collective-permute-start | bytes 3145736 | tf_op jit(solution)/shard_map/ppermute | solution.py:81
  352.2 176.4 %reduce-scatter.11.cloned.1.call-start = ((), (), s32[]{:S(2)}) async-start(), calls=%async_computation.8 | async-start | bytes 2621440 | tf_op jit(solution)/shard_map/reduce_scatter | solution.py:77
  374.7 43.6 %collective-permute-start.46 = (bf16[2,1,128,2048]{3,2,1,0:T(8,128)(2,1)}, bf16[2,1,128,2048]{3,2,1,0:T(8,128)(2,1)}, u32[]{:S(2)}, u32[]{:S(2)}) collective-permute-start(bf16[2,1,128,2048]{3,2,1,0:T(8,128)(2,1)} %copy-done.41), channel_id=1, source_target_pairs={{0,16},{4,20},{8,24},{12,28},{16,0},{20,4},{24,8},{28,12},{1,17},{... | collective-permute-start | bytes 3145736 | tf_op jit(solution)/shard_map/ppermute | solution.py:81
  375.9 42.5 %collective-permute-start.45 = (bf16[2,1,128,2048]{3,2,1,0:T(8,128)(2,1)}, bf16[2,1,128,2048]{3,2,1,0:T(8,128)(2,1)}, u32[]{:S(2)}, u32[]{:S(2)}) collective-permute-start(bf16[2,1,128,2048]{3,2,1,0:T(8,128)(2,1)} %copy-done.40), channel_id=1, source_target_pairs={{0,8},{4,12},{8,0},{12,4},{16,24},{20,28},{24,16},{28,20},{1,9},{5... | collective-permute-start | bytes 3145736 | tf_op jit(solution)/shard_map/ppermute | solution.py:81
  379.3 39.0 %collective-permute-start.44 = (bf16[1024,256]{1,0:T(8,128)(2,1)}, bf16[1024,256]{1,0:T(8,128)(2,1)}, u32[]{:S(2)}, u32[]{:S(2)}) collective-permute-start(bf16[1024,256]{1,0:T(8,128)(2,1)} %fusion.15), channel_id=1, source_target_pairs={{0,8},{4,12},{8,0},{12,4},{16,24},{20,28},{24,16},{28,20},{1,9},{5... | collective-permute-start | bytes 1572872 | tf_op jit(solution)/shard_map/ppermute | solution.py:81
  382.0 36.4 %collective-permute-start.43 = (bf16[1024,256]{1,0:T(8,128)(2,1)}, bf16[1024,256]{1,0:T(8,128)(2,1)S(1)}, u32[]{:S(2)}, u32[]{:S(2)}) collective-permute-start(bf16[1024,256]{1,0:T(8,128)(2,1)} %fusion.16), channel_id=1, source_target_pairs={{0,16},{4,20},{8,24},{12,28},{16,0},{20,4},{24,8},{28,12},{1,17},{... | collective-permute-start | bytes 1572872 | tf_op jit(solution)/shard_map/ppermute | solution.py:81
  420.6 14.9 %collective-permute-start.47 = (bf16[4,512,256]{2,1,0:T(8,128)(2,1)S(1)}, bf16[4,512,256]{2,1,0:T(8,128)(2,1)S(1)}, u32[]{:S(2)}, u32[]{:S(2)}) collective-permute-start(bf16[4,512,256]{2,1,0:T(8,128)(2,1)S(1)} %sent.6), channel_id=1, source_target_pairs={{0,4},{4,0},{8,12},{12,8},{16,20},{20,16},{24,28},{28,24},{1,5},{5... | collective-permute-start | bytes 3145736 | tf_op jit(solution)/shard_map/ppermute | solution.py:81
  422.2 18.0 %collective-permute-start.54 = (bf16[768,128]{1,0:T(8,128)(2,1)S(1)}, bf16[768,128]{1,0:T(8,128)(2,1)}, u32[]{:S(2)}, u32[]{:S(2)}) collective-permute-start(bf16[768,128]{1,0:T(8,128)(2,1)S(1)} %copy-done.112), channel_id=1, source_target_pairs={{0,28},{4,24},{8,20},{12,16},{16,12},{20,8},{24,4},{28,0},{1,29},{... | collective-permute-start | bytes 589832 | tf_op jit(solution)/shard_map/ppermute | solution.py:81
  426.3 17.6 %collective-permute-start.53 = (bf16[768,128]{1,0:T(8,128)(2,1)}, bf16[768,128]{1,0:T(8,128)(2,1)}, u32[]{:S(2)}, u32[]{:S(2)}) collective-permute-start(bf16[768,128]{1,0:T(8,128)(2,1)} %get-tuple-element.251), channel_id=1, source_target_pairs={{0,24},{4,28},{8,16},{12,20},{16,8},{20,12},{24,0},{28,4},{1,25},{... | collective-permute-start | bytes 589832 | tf_op jit(solution)/shard_map/ppermute | solution.py:81
  428.0 15.8 %collective-permute-start.52 = (bf16[768,128]{1,0:T(8,128)(2,1)}, bf16[768,128]{1,0:T(8,128)(2,1)}, u32[]{:S(2)}, u32[]{:S(2)}) collective-permute-start(bf16[768,128]{1,0:T(8,128)(2,1)} %get-tuple-element.249), channel_id=1, source_target_pairs={{0,20},{4,16},{8,28},{12,24},{16,4},{20,0},{24,12},{28,8},{1,21},{... | collective-permute-start | bytes 589832 | tf_op jit(solution)/shard_map/ppermute | solution.py:81
  454.4 31.4 %collective-permute-start.55 = (bf16[4,3,256,512]{3,2,1,0:T(8,128)(2,1)}, bf16[4,3,256,512]{3,2,1,0:T(8,128)(2,1)}, u32[]{:S(2)}, u32[]{:S(2)}) collective-permute-start(bf16[4,3,256,512]{3,2,1,0:T(8,128)(2,1)} %sent.7), channel_id=1, source_target_pairs={{0,4},{4,0},{8,12},{12,8},{16,20},{20,16},{24,28},{28,24},{1,5},{5... | collective-permute-start | bytes 9437192 | tf_op jit(solution)/shard_map/ppermute | solution.py:81
  456.9 28.9 %collective-permute-start.59 = (bf16[1,128,2048]{2,1,0:T(8,128)(2,1)}, bf16[1,128,2048]{2,1,0:T(8,128)(2,1)}, u32[]{:S(2)}, u32[]{:S(2)}) collective-permute-start(bf16[1,128,2048]{2,1,0:T(8,128)(2,1)} %fusion.14), channel_id=1, source_target_pairs={{0,16},{4,20},{8,24},{12,28},{16,0},{20,4},{24,8},{28,12},{1,17},{... | collective-permute-start | bytes 1572872 | tf_op jit(solution)/shard_map/ppermute | solution.py:81
  460.6 25.2 %collective-permute-start.60 = (bf16[1,128,2048]{2,1,0:T(8,128)(2,1)}, bf16[1,128,2048]{2,1,0:T(8,128)(2,1)}, u32[]{:S(2)}, u32[]{:S(2)}) collective-permute-start(bf16[1,128,2048]{2,1,0:T(8,128)(2,1)} %fusion.13), channel_id=1, source_target_pairs={{0,8},{4,12},{8,0},{12,4},{16,24},{20,28},{24,16},{28,20},{1,9},{5... | collective-permute-start | bytes 1572872 | tf_op jit(solution)/shard_map/ppermute | solution.py:81
  461.9 16.9 %collective-permute-start.57 = (bf16[512,256]{1,0:T(8,128)(2,1)S(1)}, bf16[512,256]{1,0:T(8,128)(2,1)}, u32[]{:S(2)}, u32[]{:S(2)}) collective-permute-start(bf16[512,256]{1,0:T(8,128)(2,1)S(1)} %copy-done.44), channel_id=1, source_target_pairs={{0,16},{4,20},{8,24},{12,28},{16,0},{20,4},{24,8},{28,12},{1,17},{... | collective-permute-start | bytes 786440 | tf_op jit(solution)/shard_map/ppermute | solution.py:81
  467.3 16.5 %collective-permute-start.58 = (bf16[512,256]{1,0:T(8,128)(2,1)S(1)}, bf16[512,256]{1,0:T(8,128)(2,1)}, u32[]{:S(2)}, u32[]{:S(2)}) collective-permute-start(bf16[512,256]{1,0:T(8,128)(2,1)S(1)} %get-tuple-element.263), channel_id=1, source_target_pairs={{0,24},{4,28},{8,16},{12,20},{16,8},{20,12},{24,0},{28,4},{1,25},{... | collective-permute-start | bytes 786440 | tf_op jit(solution)/shard_map/ppermute | solution.py:81
  494.1 18.8 %collective-permute-start.65 = (bf16[2,3,128,512]{3,2,1,0:T(8,128)(2,1)}, bf16[2,3,128,512]{3,2,1,0:T(8,128)(2,1)S(1)}, u32[]{:S(2)}, u32[]{:S(2)}) collective-permute-start(bf16[2,3,128,512]{3,2,1,0:T(8,128)(2,1)} %get-tuple-element.276), channel_id=1, source_target_pairs={{0,16},{4,20},{8,24},{12,28},{16,0},{20,4},{24,8},{28,12},{1,17},{... | collective-permute-start | bytes 2359304 | tf_op jit(solution)/shard_map/ppermute | solution.py:81
  495.2 18.6 %collective-permute-start.64 = (bf16[2,3,128,512]{3,2,1,0:T(8,128)(2,1)}, bf16[2,3,128,512]{3,2,1,0:T(8,128)(2,1)S(1)}, u32[]{:S(2)}, u32[]{:S(2)}) collective-permute-start(bf16[2,3,128,512]{3,2,1,0:T(8,128)(2,1)} %copy-done.42), channel_id=1, source_target_pairs={{0,8},{4,12},{8,0},{12,4},{16,24},{20,28},{24,16},{28,20},{1,9},{5... | collective-permute-start | bytes 2359304 | tf_op jit(solution)/shard_map/ppermute | solution.py:81
  (160 other events, 1943.6 us)
Sparse Core Ops, SparseCore 0:
  64.5 46.5 all-gather.1
  144.2 44.1 reduce-scatter.4
  259.2 43.8 reduce-scatter.6
  352.3 43.8 reduce-scatter.8
  478.9 45.2 reduce-scatter.10

commit v5 on v4

--- a/solution.py
+++ b/solution.py
@@ -1432,7 +1432,7 @@
     )
     vector_sums = vector_scatter(after(vectors, *qkv_sent), seq_rank, seq_count)
     up_grad = add_gradient(up_rest, vector_sums)[0]
-    grad_attn_in = after(grad_attn_in, vector_sums)
+
     grad_input_norm, _, _ = input_back(grad_attn_in)
     input_grad = (grad_middle + grad_input_norm).astype(NARROW)
     narrow_part = local_width // seq_count

time: 551 us -> 553 us (level)
    unnamed x237 -> x239, local copies, waits for them, and re-layouts: 25.2 us -> 25.1 us
  transfers between devices with their start and end apart: 76 -> 76, of which waited for: 39 -> 40; matrix products, arithmetic and copies ran while one was open for 12% -> 13% of each run, Pallas kernels for 23% -> 23%
where the time goes in v5:
time: 553 us; the launch traced here: 546 us
  waiting for transfers between devices  192 us (35%)
  Pallas kernels  165 us (30%)
  starting transfers between devices  67.6 us (12%)
  other arithmetic  57 us (10%)
  local copies, waits for them, and re-layouts  30.2 us (5%)
  matrix products  18.2 us (3%)
  between operations  16.5 us (3%)
    pallas_call x8, Pallas kernels, local_call(): pl.pallas_call(kernel, name=name, grid=(1,), out_shape=tuple(outs), in_sp...  89.6 us
    ppermute x62, waiting for transfers between devices, hop(): return lax.ppermute(values, axis, [(i, i ^ mask) for i in range(count)])  77.5 us
    ppermute x9, waiting for transfers between devices, gather_parts(): parts.append(lax.ppermute(parts[-1], 'tp', pairs))  67.8 us
    ppermute x62, starting transfers between devices, hop(): return lax.ppermute(values, axis, [(i, i ^ mask) for i in range(count)])  60.8 us
    reduce_scatter x4, waiting for transfers between devices, scatter_rows(): lax.psum_scatter(values.astype(NARROW), 'tp', scatter_dimension=0, tiled=...  46.8 us
    pallas_call x5, Pallas kernels, resident_call(): pl.pallas_call(kernel, name=name, out_shape=tuple(outs) + tuple(remote_ou...  37.9 us
    pallas_call x8, Pallas kernels, gradient_blocks(): pl.pallas_call(kernel, name='sent' if got is None else 'kept', grid_spec=...  37.4 us
    unnamed x239, local copies, waits for them, and re-layouts  25.1 us
  transfers between devices with their start and end apart: 76, of which 40 were waited for; matrix products, arithmetic and copies ran while one was open for 13% of the time, Pallas kernels for 23%

profile of v5, /device:TPU:0, one launch (start us, length us, event | category | flops | bytes accessed | tf_op | source)
XLA Modules:
  0.0 546.5 jit_solution(4564087918770772833)
XLA Ops:
  15.9 12.0 %collective-permute-done.3.refs_1_ = bf16[128,2048]{1,0:T(8,128)(2,1)S(1)} collective-permute-done((bf16[128,2048]{1,0:T(8,128)(2,1)S(1)}, bf16[128,2048]{1,0:T(8,128)(2,1)S(1)}, u32[]{:S(2)}, u32[]{:S(2)}) %collective-permute-start.3) | collective-permute-done | bytes 524320 | tf_op jit(solution)/shard_map/ppermute | solution.py:61
  45.6 7.9 %pack.2 = (bf16[2,8,192,128]{3,2,1,0:T(8,128)(2,1)}, bf16[256,2048]{1,0:T(8,128)(2,1)}) custom-call(s32[1]{0:T(128)} %bitcast.place.seat, s32[4]{0:T(128)} %fusion.32.owners.seat, bf16[128,2048]{1,0:T(8,128)(2,1)} %copy-done.51, bf16[128,2048]{1,0:T(8,128)(2,1)} %copy-done.68, bf16[3,2048,512]{2,1,0:T(8,128)(2,1)} %weight.1, ...), custom_call_target="tpu_custom_call" | custom-call | flops 1048576 | bytes 65536 | tf_op jit(solution)/shard_map/pack/pallas_call | solution.py:314
  55.9 8.5 %pack.3 = (bf16[768,128]{1,0:T(8,128)(2,1)}, bf16[768,128]{1,0:T(8,128)(2,1)}, bf16[768,128]{1,0:T(8,128)(2,1)}, bf16[768,128]{1,0:T(8,128)(2,1)}, bf16[768,128]...) custom-call(s32[1]{0:T(128)} %bitcast.place.seat, ...), custom_call_target="tpu_custom_call" | custom-call | flops 1048576 | bytes 65536 | tf_op jit(solution)/shard_map/pack/pallas_call | solution.py:314
  71.9 9.9 %collective-permute-done.10.refs_5_ = bf16[768,128]{1,0:T(8,128)(2,1)S(1)} collective-permute-done((bf16[768,128]{1,0:T(8,128)(2,1)}, bf16[768,128]{1,0:T(8,128)(2,1)S(1)}, u32[]{:S(2)}, u32[]{:S(2)}) %collective-permute-start.10) | collective-permute-done | bytes 196640 | tf_op jit(solution)/shard_map/ppermute | solution.py:81
  86.2 28.5 %forward.1 = (bf16[64,512]{1,0:T(8,128)(2,1)}, bf16[64,512]{1,0:T(8,128)(2,1)}, bf16[64,512]{1,0:T(8,128)(2,1)}, bf16[64,512]{1,0:T(8,128)(2,1)}, bf16[64,512]{1...) custom-call(s32[18]{0:T(128)} %pad_add_fusion.1.info, ...), custom_call_target="tpu_custom_call" | custom-call | flops 1048576 | bytes 65536 | tf_op jit(solution)/shard_map/forward/pallas_call | solution.py:298
  121.2 3.8 collective-permute-done.17.refs_5_
  138.6 4.2 mixed_out.1
  155.0 8.2 %convolution_convert_fusion.1.refs_4_ = bf16[512,2048]{1,0:T(8,128)(2,1)S(1)} fusion(bf16[512,2048]{1,0:T(8,128)(2,1)S(1)} %copy-done.7, bf16[2048,2048]{1,0:T(8,128)(2,1)} %param.35), kind=kOutput, calls=%fused_computation.1 | convolution fusion | flops 4296015872 | bytes 12582912 | tf_op jit(solution)/shard_map/rd,fd->rf/dot_general | solution.py:1269
  163.3 25.1 %reduce-scatter.5.cloned.1.call-done = bf16[128,2048]{1,0:T(8,128)(2,1)} async-done(((bf16[512,2048]{1,0:T(8,128)(2,1)}), bf16[128,2048]{1,0:T(8,128)(2,1)}) %reduce-scatter.5.cloned.1.call-update) | async-done | bytes 524304 | tf_op jit(solution)/shard_map/reduce_scatter | solution.py:77
  190.2 14.4 %collective-permute-done.22.refs_1_ = bf16[128,2048]{1,0:T(8,128)(2,1)S(1)} collective-permute-done((bf16[128,2048]{1,0:T(8,128)(2,1)S(1)}, bf16[128,2048]{1,0:T(8,128)(2,1)S(1)}, u32[]{:S(2)}, u32[]{:S(2)}) %collective-permute-start.22) | collective-permute-done | bytes 524320 | tf_op jit(solution)/shard_map/ppermute | solution.py:61
  204.6 13.5 %collective-permute-done.23.refs_0_ = bf16[128,2048]{1,0:T(8,128)(2,1)S(1)} collective-permute-done((bf16[128,2048]{1,0:T(8,128)(2,1)S(1)}, bf16[128,2048]{1,0:T(8,128)(2,1)S(1)}, u32[]{:S(2)}, u32[]{:S(2)}) %collective-permute-start.23) | collective-permute-done | bytes 524320 | tf_op jit(solution)/shard_map/ppermute | solution.py:61
  221.7 5.6 %up.2 = (bf16[256,2048]{1,0:T(8,128)(2,1)S(1)}, bf16[256,2048]{1,0:T(8,128)(2,1)S(1)}, bf16[256,2048]{1,0:T(8,128)(2,1)S(1)}, f32[4,256]{1,0:T(4,128)S(1)}) custom-call(s32[4]{0:T(128)S(1)} %copy-done.38, bf16[128,2048]{1,0:T(8,128)(2,1)S(1)} %add_convert_fusion.1.refs_0_, bf16[128,2048]{1,0:T(8,128)(2,1)S(1)} %collective-permute-done.22.refs_1_, ...), custom_call_target="tpu_custom_call" | custom-call | flops 1048576 | bytes 65536 | tf_op jit(solution)/shard_map/up/pallas_call | solution.py:314
  230.8 5.7 %up.3 = (bf16[256,2048]{1,0:T(8,128)(2,1)S(1)}, bf16[256,2048]{1,0:T(8,128)(2,1)S(1)}, bf16[512,2048]{1,0:T(8,128)(2,1)S(1)}, f32[4,512]{1,0:T(4,128)S(1)}) custom-call(s32[4]{0:T(128)S(1)} %copy-done.39, bf16[128,2048]{1,0:T(8,128)(2,1)S(1)} %collective-permute-done.23.refs_0_, bf16[128,2048]{1,0:T(8,128)(2,1)S(1)} %collective-permute-done.24.refs_1_, ...), custom_call_target="tpu_custom_call" | custom-call | flops 1048576 | bytes 65536 | tf_op jit(solution)/shard_map/up/pallas_call | solution.py:314
  236.6 3.6 collective-permute-done.25
  244.8 10.2 %ffn_back.1 = (bf16[512,2048]{1,0:T(8,128)(2,1)S(1)}, bf16[512,2048]{1,0:T(8,128)(2,1)S(1)}, f32[3,2048]{1,0:T(4,128)S(1)}, bf16[512,2048]{1,0:T(8,128)(2,1)S(1)}) custom-call(s32[4]{0:T(128)S(1)} %copy-done.38, f32[4,512]{1,0:T(4,128)S(1)} %collective-permute-done.26.got, f32[4,512]{1,0:T(4,128)S(1)} %add.278.mine, ...), custom_call_target="tpu_custom_call" | custom-call | flops 1048576 | bytes 65536 | tf_op jit(solution)/shard_map/ffn_back/pallas_call | solution.py:314
  259.2 10.0 %convolution_convert_fusion = bf16[512,2048]{1,0:T(8,128)(2,1)} fusion(bf16[512,2048]{1,0:T(8,128)(2,1)} %copy-done.15, bf16[2048,2048]{1,0:T(8,128)(2,1)} %param.35), kind=kOutput, calls=%fused_computation | convolution fusion | flops 4296015872 | bytes 12582912 | tf_op jit(solution)/shard_map/dot_general | solution.py:1300
  270.8 5.1 sent.4
  275.9 5.0 sent.5
  281.4 21.7 %reduce-scatter.7.cloned.1.call-done = bf16[128,2048]{1,0:T(8,128)(2,1)} async-done(((bf16[512,2048]{1,0:T(8,128)(2,1)}), bf16[128,2048]{1,0:T(8,128)(2,1)}) %reduce-scatter.7.cloned.1.call-update) | async-done | bytes 524304 | tf_op jit(solution)/shard_map/reduce_scatter | solution.py:77
  308.1 6.3 %kept.5 = (f32[2048,256]{1,0:T(8,128)S(1)}, bf16[2,1024,256]{2,1,0:T(8,128)(2,1)S(1)}, bf16[2,1024,256]{2,1,0:T(8,128)(2,1)S(1)}, bf16[1024,256]{1,0:T(8,128)(2,1)S(1)}, bf16[1024,256]{1,0:T(8,128)(2,1)S(1)}) custom-call(s32[2]{0:T(128)S(1)} %pad_add_fusion.3.seat, bf16[512,2048]{1,0:T(8,128)(2,1)S(1)} %copy-done.17, bf16[512,2048]{1,0:T(8,128)(2,1)S(1)} %copy-done.8, ...), custom_call_target="tpu_custom_call" | custom-call | flops 1048576 | bytes 65536 | tf_op jit(solution)/shard_map/kept/pallas_call | solution.py:226
  322.3 13.2 %collective-permute-done.28.refs_2_ = bf16[128,2048]{1,0:T(8,128)(2,1)S(1)} collective-permute-done((bf16[128,2048]{1,0:T(8,128)(2,1)S(1)}, bf16[128,2048]{1,0:T(8,128)(2,1)S(1)}, u32[]{:S(2)}, u32[]{:S(2)}) %collective-permute-start.28) | collective-permute-done | bytes 524320 | tf_op jit(solution)/shard_map/ppermute | solution.py:61
  335.7 6.0 %kept.4 = (f32[1,256,2048]{2,1,0:T(8,128)S(1)}, bf16[2,1,128,2048]{3,2,1,0:T(8,128)(2,1)S(1)}, bf16[2,1,128,2048]{3,2,1,0:T(8,128)(2,1)S(1)}, bf16[1,128,2048]{2,1,0:T(8,128)(2,1)S(1)}, bf16[1,128,2048]{2,1,0:T(8,128)(2,1)S(1)}) custom-call(s32[2]{0:T(128)S(1)} %pad_add_fusion.3.seat, bf16[1,512,2048]{2,1,0:T(8,128)(2,1)S(1)} %bitcast.126, ...), custom_call_target="tpu_custom_call" | custom-call | flops 1048576 | bytes 65536 | tf_op jit(solution)/shard_map/kept/pallas_call | solution.py:226
  342.9 5.3 collective-permute-done.29.refs_3_
  383.8 35.3 %backward.1 = (bf16[768,128]{1,0:T(8,128)(2,1)}, bf16[768,128]{1,0:T(8,128)(2,1)}, bf16[768,128]{1,0:T(8,128)(2,1)}, bf16[768,128]{1,0:T(8,128)(2,1)}, bf16[768,...) custom-call(s32[18]{0:T(128)} %pad_add_fusion.1.info, ...), custom_call_target="tpu_custom_call" | custom-call | flops 1048576 | bytes 65536 | tf_op jit(solution)/shard_map/backward/pallas_call | solution.py:298
  429.3 6.1 %collective-permute-done.48.refs_2_ = bf16[768,128]{1,0:T(8,128)(2,1)S(1)} collective-permute-done((bf16[768,128]{1,0:T(8,128)(2,1)S(1)}, bf16[768,128]{1,0:T(8,128)(2,1)S(1)}, u32[]{:S(2)}, u32[]{:S(2)}) %collective-permute-start.48) | collective-permute-done | bytes 196640 | tf_op jit(solution)/shard_map/ppermute | solution.py:81
  445.1 4.1 unpack.1
  450.6 4.3 sent.7
  463.5 4.7 collective-permute-done.56
  469.9 9.6 %attn_back.1 = (bf16[512,2048]{1,0:T(8,128)(2,1)}, f32[2,2048]{1,0:T(2,128)}) custom-call(bf16[3,512,512]{2,1,0:T(8,128)(2,1)} %get-tuple-element.252.grads.left, bf16[512,2048]{1,0:T(8,128)(2,1)} %get-tuple-element.253.rows.right, f32[1,2048]{1,0:T(1,128)} %bitcast.139, f32[1,2048]{1,0:T(1,128)} %bitcast.141, bf16[3,2048,512]{2,1,0:T(8,128)(2,1)} %weight.1), custom_call_target="tpu_custom_call" | custom-call | flops 1048576 | bytes 65536 | tf_op jit(solution)/shard_map/attn_back/pallas_call | solution.py:298
  479.6 4.8 collective-permute-done.58
  486.4 6.3 %kept.7 = (f32[3,256,512]{2,1,0:T(8,128)S(1)}, bf16[2,3,128,512]{3,2,1,0:T(8,128)(2,1)}, bf16[2,3,128,512]{3,2,1,0:T(8,128)(2,1)S(1)}, bf16[3,128,512]{2,1,0:T(8,128)(2,1)S(1)}, bf16[3,128,512]{2,1,0:T(8,128)(2,1)S(1)}) custom-call(s32[2]{0:T(128)S(1)} %pad_add_fusion.3.seat, bf16[3,512,512]{2,1,0:T(8,128)(2,1)S(1)} %copy-done.4, ...), custom_call_target="tpu_custom_call" | custom-call | flops 1048576 | bytes 65536 | tf_op jit(solution)/shard_map/kept/pallas_call | solution.py:226
  506.7 6.8 %collective-permute-done.61 = bf16[2,3,128,512]{3,2,1,0:T(8,128)(2,1)S(1)} collective-permute-done((bf16[2,3,128,512]{3,2,1,0:T(8,128)(2,1)}, bf16[2,3,128,512]{3,2,1,0:T(8,128)(2,1)S(1)}, u32[]{:S(2)}, u32[]{:S(2)}) %collective-permute-start.61) | collective-permute-done | bytes 786464 | tf_op jit(solution)/shard_map/ppermute | solution.py:81
  (498 shorter events, 214.4 us)
Async XLA Ops:
  7.2 114.0 %all-gather.2.cloned.1.call-start = ((), (), s32[]{:S(2)}) async-start(), calls=%async_computation.4 | async-start | bytes 2621440 | tf_op jit(solution)/shard_map/all_gather | solution.py:49
  12.0 16.0 %collective-permute-start.3 = (bf16[128,2048]{1,0:T(8,128)(2,1)S(1)}, bf16[128,2048]{1,0:T(8,128)(2,1)S(1)}, u32[]{:S(2)}, u32[]{:S(2)}) collective-permute-start(bf16[128,2048]{1,0:T(8,128)(2,1)S(1)} %fusion.5.refs_0_), channel_id=1, source_target_pairs={{0,1},{1,3},{3,2},{2,0},{4,5},{5,7},{7,6},{6,4},{8,9},{9,11},{11,1... | collective-permute-start | bytes 1572872 | tf_op jit(solution)/shard_map/ppermute | solution.py:61
  15.8 16.7 %collective-permute-start = (s32[16]{0:T(128)S(1)}, s32[16]{0:T(128)S(1)}, u32[]{:S(2)}, u32[]{:S(2)}) collective-permute-start(s32[16]{0:T(128)S(1)} %select_reduce_fusion.2), channel_id=1, source_target_pairs={{0,4},{4,0},{8,12},{12,8},{16,20},{20,16},{24,28},{28,24},{1,5},{5... | collective-permute-start | bytes 200 | tf_op jit(solution)/shard_map/ppermute | solution.py:81
  64.4 124.0 %reduce-scatter.5.cloned.1.call-start = ((), (), s32[]{:S(2)}) async-start(), calls=%async_computation.5 | async-start | bytes 2621440 | tf_op jit(solution)/shard_map/reduce_scatter | solution.py:77
  66.0 15.8 %collective-permute-start.10 = (bf16[768,128]{1,0:T(8,128)(2,1)}, bf16[768,128]{1,0:T(8,128)(2,1)S(1)}, u32[]{:S(2)}, u32[]{:S(2)}) collective-permute-start(bf16[768,128]{1,0:T(8,128)(2,1)} %get-tuple-element.159), channel_id=1, source_target_pairs={{0,20},{4,16},{8,28},{12,24},{16,4},{20,0},{24,12},{28,8},{1,21},{... | collective-permute-start | bytes 589832 | tf_op jit(solution)/shard_map/ppermute | solution.py:81
  66.3 16.6 %collective-permute-start.11 = (bf16[768,128]{1,0:T(8,128)(2,1)}, bf16[768,128]{1,0:T(8,128)(2,1)S(1)}, u32[]{:S(2)}, u32[]{:S(2)}) collective-permute-start(bf16[768,128]{1,0:T(8,128)(2,1)} %get-tuple-element.160), channel_id=1, source_target_pairs={{0,24},{4,28},{8,16},{12,20},{16,8},{20,12},{24,0},{28,4},{1,25},{... | collective-permute-start | bytes 589832 | tf_op jit(solution)/shard_map/ppermute | solution.py:81
  67.9 15.0 %collective-permute-start.12 = (bf16[768,128]{1,0:T(8,128)(2,1)}, bf16[768,128]{1,0:T(8,128)(2,1)S(1)}, u32[]{:S(2)}, u32[]{:S(2)}) collective-permute-start(bf16[768,128]{1,0:T(8,128)(2,1)} %get-tuple-element.161), channel_id=1, source_target_pairs={{0,28},{4,24},{8,20},{12,16},{16,12},{20,8},{24,4},{28,0},{1,29},{... | collective-permute-start | bytes 589832 | tf_op jit(solution)/shard_map/ppermute | solution.py:81
  71.1 15.1 %collective-permute-start.9 = (bf16[768,128]{1,0:T(8,128)(2,1)}, bf16[768,128]{1,0:T(8,128)(2,1)}, u32[]{:S(2)}, u32[]{:S(2)}) collective-permute-start(bf16[768,128]{1,0:T(8,128)(2,1)} %get-tuple-element.158), channel_id=1, source_target_pairs={{0,16},{4,20},{8,24},{12,28},{16,0},{20,4},{24,8},{28,12},{1,17},{... | collective-permute-start | bytes 589832 | tf_op jit(solution)/shard_map/ppermute | solution.py:81
  144.1 158.9 %reduce-scatter.7.cloned.1.call-start = ((), (), s32[]{:S(2)}) async-start(), calls=%async_computation.6 | async-start | bytes 2621440 | tf_op jit(solution)/shard_map/reduce_scatter | solution.py:77
  190.1 14.4 %collective-permute-start.22 = (bf16[128,2048]{1,0:T(8,128)(2,1)S(1)}, bf16[128,2048]{1,0:T(8,128)(2,1)S(1)}, u32[]{:S(2)}, u32[]{:S(2)}) collective-permute-start(bf16[128,2048]{1,0:T(8,128)(2,1)S(1)} %add_convert_fusion.1.refs_0_), channel_id=1, source_target_pairs={{0,1},{1,3},{3,2},{2,0},{4,5},{5,7},{7,6},{6,4},{8,9},{9,11},{11,1... | collective-permute-start | bytes 1572872 | tf_op jit(solution)/shard_map/ppermute | solution.py:61
  259.1 183.0 %reduce-scatter.9.cloned.1.call-start = ((), (), s32[]{:S(2)}) async-start(), calls=%async_computation.7 | async-start | bytes 2621440 | tf_op jit(solution)/shard_map/reduce_scatter | solution.py:77
  275.9 32.2 %collective-permute-start.31 = (bf16[4,2048,256]{2,1,0:T(8,128)(2,1)}, bf16[4,2048,256]{2,1,0:T(8,128)(2,1)}, u32[]{:S(2)}, u32[]{:S(2)}) collective-permute-start(bf16[4,2048,256]{2,1,0:T(8,128)(2,1)} %sent.4), channel_id=1, source_target_pairs={{0,4},{4,0},{8,12},{12,8},{16,20},{20,16},{24,28},{28,24},{1,5},{5... | collective-permute-start | bytes 12582920 | tf_op jit(solution)/shard_map/ppermute | solution.py:81
  280.8 54.8 %collective-permute-start.30 = (bf16[4,1,256,2048]{3,2,1,0:T(8,128)(2,1)}, bf16[4,1,256,2048]{3,2,1,0:T(8,128)(2,1)}, u32[]{:S(2)}, u32[]{:S(2)}) collective-permute-start(bf16[4,1,256,2048]{3,2,1,0:T(8,128)(2,1)} %sent.5), channel_id=1, source_target_pairs={{0,4},{4,0},{8,12},{12,8},{16,20},{20,16},{24,28},{28,24},{1,5},{5... | collective-permute-start | bytes 12582920 | tf_op jit(solution)/shard_map/ppermute | solution.py:81
  307.7 14.4 %collective-permute-start.27 = (bf16[128,2048]{1,0:T(8,128)(2,1)S(1)}, bf16[128,2048]{1,0:T(8,128)(2,1)S(1)}, u32[]{:S(2)}, u32[]{:S(2)}) collective-permute-start(bf16[128,2048]{1,0:T(8,128)(2,1)S(1)} %get-tuple-element.297.refs_0_), channel_id=1, source_target_pairs={{0,1},{1,3},{3,2},{2,0},{4,5},{5,7},{7,6},{6,4},{8,9},{9,11},{11,1... | collective-permute-start | bytes 1572872 | tf_op jit(solution)/shard_map/ppermute | solution.py:61
  317.4 24.4 %collective-permute-start.32 = (bf16[2,1024,256]{2,1,0:T(8,128)(2,1)S(1)}, bf16[2,1024,256]{2,1,0:T(8,128)(2,1)S(1)}, u32[]{:S(2)}, u32[]{:S(2)}) collective-permute-start(bf16[2,1024,256]{2,1,0:T(8,128)(2,1)S(1)} %get-tuple-element.199), channel_id=1, source_target_pairs={{0,8},{4,12},{8,0},{12,4},{16,24},{20,28},{24,16},{28,20},{1,9},{5... | collective-permute-start | bytes 3145736 | tf_op jit(solution)/shard_map/ppermute | solution.py:81
  318.8 24.1 %collective-permute-start.33 = (bf16[2,1024,256]{2,1,0:T(8,128)(2,1)S(1)}, bf16[2,1024,256]{2,1,0:T(8,128)(2,1)S(1)}, u32[]{:S(2)}, u32[]{:S(2)}) collective-permute-start(bf16[2,1024,256]{2,1,0:T(8,128)(2,1)S(1)} %get-tuple-element.200), channel_id=1, source_target_pairs={{0,16},{4,20},{8,24},{12,28},{16,0},{20,4},{24,8},{28,12},{1,17},{... | collective-permute-start | bytes 3145736 | tf_op jit(solution)/shard_map/ppermute | solution.py:81
  352.0 177.2 %reduce-scatter.11.cloned.1.call-start = ((), (), s32[]{:S(2)}) async-start(), calls=%async_computation.8 | async-start | bytes 2621440 | tf_op jit(solution)/shard_map/reduce_scatter | solution.py:77
  375.1 44.2 %collective-permute-start.46 = (bf16[2,1,128,2048]{3,2,1,0:T(8,128)(2,1)}, bf16[2,1,128,2048]{3,2,1,0:T(8,128)(2,1)}, u32[]{:S(2)}, u32[]{:S(2)}) collective-permute-start(bf16[2,1,128,2048]{3,2,1,0:T(8,128)(2,1)} %copy-done.41), channel_id=1, source_target_pairs={{0,16},{4,20},{8,24},{12,28},{16,0},{20,4},{24,8},{28,12},{1,17},{... | collective-permute-start | bytes 3145736 | tf_op jit(solution)/shard_map/ppermute | solution.py:81
  376.1 43.1 %collective-permute-start.45 = (bf16[2,1,128,2048]{3,2,1,0:T(8,128)(2,1)}, bf16[2,1,128,2048]{3,2,1,0:T(8,128)(2,1)}, u32[]{:S(2)}, u32[]{:S(2)}) collective-permute-start(bf16[2,1,128,2048]{3,2,1,0:T(8,128)(2,1)} %copy-done.40), channel_id=1, source_target_pairs={{0,8},{4,12},{8,0},{12,4},{16,24},{20,28},{24,16},{28,20},{1,9},{5... | collective-permute-start | bytes 3145736 | tf_op jit(solution)/shard_map/ppermute | solution.py:81
  379.7 39.5 %collective-permute-start.44 = (bf16[1024,256]{1,0:T(8,128)(2,1)}, bf16[1024,256]{1,0:T(8,128)(2,1)}, u32[]{:S(2)}, u32[]{:S(2)}) collective-permute-start(bf16[1024,256]{1,0:T(8,128)(2,1)} %fusion.15), channel_id=1, source_target_pairs={{0,8},{4,12},{8,0},{12,4},{16,24},{20,28},{24,16},{28,20},{1,9},{5... | collective-permute-start | bytes 1572872 | tf_op jit(solution)/shard_map/ppermute | solution.py:81
  382.2 37.0 %collective-permute-start.43 = (bf16[1024,256]{1,0:T(8,128)(2,1)}, bf16[1024,256]{1,0:T(8,128)(2,1)S(1)}, u32[]{:S(2)}, u32[]{:S(2)}) collective-permute-start(bf16[1024,256]{1,0:T(8,128)(2,1)} %fusion.16), channel_id=1, source_target_pairs={{0,16},{4,20},{8,24},{12,28},{16,0},{20,4},{24,8},{28,12},{1,17},{... | collective-permute-start | bytes 1572872 | tf_op jit(solution)/shard_map/ppermute | solution.py:81
  421.4 14.9 %collective-permute-start.47 = (bf16[4,512,256]{2,1,0:T(8,128)(2,1)S(1)}, bf16[4,512,256]{2,1,0:T(8,128)(2,1)S(1)}, u32[]{:S(2)}, u32[]{:S(2)}) collective-permute-start(bf16[4,512,256]{2,1,0:T(8,128)(2,1)S(1)} %sent.6), channel_id=1, source_target_pairs={{0,4},{4,0},{8,12},{12,8},{16,20},{20,16},{24,28},{28,24},{1,5},{5... | collective-permute-start | bytes 3145736 | tf_op jit(solution)/shard_map/ppermute | solution.py:81
  423.0 18.0 %collective-permute-start.54 = (bf16[768,128]{1,0:T(8,128)(2,1)S(1)}, bf16[768,128]{1,0:T(8,128)(2,1)}, u32[]{:S(2)}, u32[]{:S(2)}) collective-permute-start(bf16[768,128]{1,0:T(8,128)(2,1)S(1)} %copy-done.113), channel_id=1, source_target_pairs={{0,28},{4,24},{8,20},{12,16},{16,12},{20,8},{24,4},{28,0},{1,29},{... | collective-permute-start | bytes 589832 | tf_op jit(solution)/shard_map/ppermute | solution.py:81
  427.1 17.3 %collective-permute-start.53 = (bf16[768,128]{1,0:T(8,128)(2,1)}, bf16[768,128]{1,0:T(8,128)(2,1)}, u32[]{:S(2)}, u32[]{:S(2)}) collective-permute-start(bf16[768,128]{1,0:T(8,128)(2,1)} %get-tuple-element.249), channel_id=1, source_target_pairs={{0,24},{4,28},{8,16},{12,20},{16,8},{20,12},{24,0},{28,4},{1,25},{... | collective-permute-start | bytes 589832 | tf_op jit(solution)/shard_map/ppermute | solution.py:81
  428.7 15.7 %collective-permute-start.52 = (bf16[768,128]{1,0:T(8,128)(2,1)}, bf16[768,128]{1,0:T(8,128)(2,1)}, u32[]{:S(2)}, u32[]{:S(2)}) collective-permute-start(bf16[768,128]{1,0:T(8,128)(2,1)} %get-tuple-element.247), channel_id=1, source_target_pairs={{0,20},{4,16},{8,28},{12,24},{16,4},{20,0},{24,12},{28,8},{1,21},{... | collective-permute-start | bytes 589832 | tf_op jit(solution)/shard_map/ppermute | solution.py:81
  454.9 31.5 %collective-permute-start.55 = (bf16[4,3,256,512]{3,2,1,0:T(8,128)(2,1)}, bf16[4,3,256,512]{3,2,1,0:T(8,128)(2,1)}, u32[]{:S(2)}, u32[]{:S(2)}) collective-permute-start(bf16[4,3,256,512]{3,2,1,0:T(8,128)(2,1)} %sent.7), channel_id=1, source_target_pairs={{0,4},{4,0},{8,12},{12,8},{16,20},{20,16},{24,28},{28,24},{1,5},{5... | collective-permute-start | bytes 9437192 | tf_op jit(solution)/shard_map/ppermute | solution.py:81
  457.5 28.9 %collective-permute-start.59 = (bf16[1,128,2048]{2,1,0:T(8,128)(2,1)}, bf16[1,128,2048]{2,1,0:T(8,128)(2,1)}, u32[]{:S(2)}, u32[]{:S(2)}) collective-permute-start(bf16[1,128,2048]{2,1,0:T(8,128)(2,1)} %fusion.14), channel_id=1, source_target_pairs={{0,16},{4,20},{8,24},{12,28},{16,0},{20,4},{24,8},{28,12},{1,17},{... | collective-permute-start | bytes 1572872 | tf_op jit(solution)/shard_map/ppermute | solution.py:81
  461.5 24.9 %collective-permute-start.60 = (bf16[1,128,2048]{2,1,0:T(8,128)(2,1)}, bf16[1,128,2048]{2,1,0:T(8,128)(2,1)}, u32[]{:S(2)}, u32[]{:S(2)}) collective-permute-start(bf16[1,128,2048]{2,1,0:T(8,128)(2,1)} %fusion.13), channel_id=1, source_target_pairs={{0,8},{4,12},{8,0},{12,4},{16,24},{20,28},{24,16},{28,20},{1,9},{5... | collective-permute-start | bytes 1572872 | tf_op jit(solution)/shard_map/ppermute | solution.py:81
  462.8 16.8 %collective-permute-start.57 = (bf16[512,256]{1,0:T(8,128)(2,1)S(1)}, bf16[512,256]{1,0:T(8,128)(2,1)}, u32[]{:S(2)}, u32[]{:S(2)}) collective-permute-start(bf16[512,256]{1,0:T(8,128)(2,1)S(1)} %copy-done.44), channel_id=1, source_target_pairs={{0,16},{4,20},{8,24},{12,28},{16,0},{20,4},{24,8},{28,12},{1,17},{... | collective-permute-start | bytes 786440 | tf_op jit(solution)/shard_map/ppermute | solution.py:81
  468.2 16.2 %collective-permute-start.58 = (bf16[512,256]{1,0:T(8,128)(2,1)S(1)}, bf16[512,256]{1,0:T(8,128)(2,1)}, u32[]{:S(2)}, u32[]{:S(2)}) collective-permute-start(bf16[512,256]{1,0:T(8,128)(2,1)S(1)} %get-tuple-element.257), channel_id=1, source_target_pairs={{0,24},{4,28},{8,16},{12,20},{16,8},{20,12},{24,0},{28,4},{1,25},{... | collective-permute-start | bytes 786440 | tf_op jit(solution)/shard_map/ppermute | solution.py:81
  494.7 18.8 %collective-permute-start.61 = (bf16[2,3,128,512]{3,2,1,0:T(8,128)(2,1)}, bf16[2,3,128,512]{3,2,1,0:T(8,128)(2,1)S(1)}, u32[]{:S(2)}, u32[]{:S(2)}) collective-permute-start(bf16[2,3,128,512]{3,2,1,0:T(8,128)(2,1)} %get-tuple-element.267), channel_id=1, source_target_pairs={{0,8},{4,12},{8,0},{12,4},{16,24},{20,28},{24,16},{28,20},{1,9},{5... | collective-permute-start | bytes 2359304 | tf_op jit(solution)/shard_map/ppermute | solution.py:81
  495.7 18.7 %collective-permute-start.63 = (bf16[2,3,128,512]{3,2,1,0:T(8,128)(2,1)}, bf16[2,3,128,512]{3,2,1,0:T(8,128)(2,1)S(1)}, u32[]{:S(2)}, u32[]{:S(2)}) collective-permute-start(bf16[2,3,128,512]{3,2,1,0:T(8,128)(2,1)} %copy-done.42), channel_id=1, source_target_pairs={{0,16},{4,20},{8,24},{12,28},{16,0},{20,4},{24,8},{28,12},{1,17},{... | collective-permute-start | bytes 2359304 | tf_op jit(solution)/shard_map/ppermute | solution.py:81
  (161 other events, 1991.4 us)
Sparse Core Ops, SparseCore 0:
  64.5 46.5 all-gather.1
  144.2 44.0 reduce-scatter.4
  259.2 43.7 reduce-scatter.6
  352.1 43.9 reduce-scatter.8
  479.7 44.9 reduce-scatter.10
